TPU v7x, 32 devices: a whole 2x2x4 slice. The times are simulated.
32 devices in a mesh: dp: 4 (over y, core), tensor: 8 (over z, x).
Axes of the slice: x: 2, y: 2, z: 4, core: 2. Of those that a mesh axis runs over, the one named last changes fastest.
Arguments:
- inputs: bfloat16 [3, 4, 1024, 1024], P(None, 'dp', 'tensor'), may hold values from -6 to 6
- doc_starts: int32 [3, 4, 4], P(None, 'dp'), may hold values from 0 to 1023, as said below
- w_qkv: bfloat16 [3, 1024, 1024], P(None, 'dp', 'tensor'), may hold values from -0.1875 to 0.1875
- w_out: bfloat16 [1024, 1024], P('tensor', 'dp'), may hold values from -0.1875 to 0.1875
- w_up: bfloat16 [1024, 4096], P('dp', 'tensor'), may hold values from -0.1875 to 0.1875
- w_down: bfloat16 [4096, 1024], P('tensor', 'dp'), may hold values from -0.09375 to 0.09375
- norm_gains: bfloat16 [4, 1024], P(None, 'dp'), may hold values from 0.25 to 1.75
- norm_biases: bfloat16 [4, 1024], P(None, 'dp'), may hold values from -3 to 3
- cotangent: bfloat16 [3, 4, 1024, 1024], P(None, 'dp', 'tensor'), may hold values from -6 to 6
Outputs:
- outputs: bfloat16 [3, 4, 1024, 1024], P(None, 'dp', 'tensor')
- inputs_grad: float32 [3, 4, 1024, 1024], P(None, 'dp', 'tensor')
- qkv_grad: float32 [3, 1024, 1024], P(None, 'dp', 'tensor')
- out_grad: float32 [1024, 1024], P('tensor', 'dp')
- up_grad: float32 [1024, 4096], P('dp', 'tensor')
- down_grad: float32 [4096, 1024], P('tensor', 'dp')
- gains_grad: float32 [4, 1024], P(None, 'dp')
- biases_grad: float32 [4, 1024], P(None, 'dp')
Inputs may be any that keep to these rules, and one draw needn't show every extreme that they name: `doc_starts`: each row's 4 document starts rise strictly and the first is 0; one document of each row, which one is drawn, begins before token 128 and has its last token at 896 or later; every other document has fewer than 128 tokens; in every draw some row has a document that starts at token 1023.
All inputs are finite; a program needn't handle non-finite values.
Results may differ from a plain program's by a relative error of at most 0.014.
Values may be sent and summed in bfloat16 or wider, within the bound.
No kernel may reach another device: no remote copies, remote signals or barrier semaphores. Data moves between devices by JAX's collectives and lax.ppermute only.
A program may use at most 192 MiB of HBM per device.

v0:
```python
import math

import jax
import jax.numpy as jnp
from jax import lax
from jax.sharding import PartitionSpec as P

HD = 64


EPSILON = 1e-05


def layer_norm(values, gain, shift):
    average = jnp.mean(values, axis=-1, keepdims=True)
    centred = values - average
    variance = jnp.mean(centred * centred, axis=-1, keepdims=True)
    return centred * lax.rsqrt(variance + EPSILON) * gain + shift


def rotate(values, angles):
    half_dim = values.shape[-1] // 2
    lower_half = values[..., :half_dim]
    upper_half = values[..., half_dim:]
    cosines = jnp.cos(angles)
    sine_part = jnp.sin(angles)
    return jnp.concatenate(
        [
            lower_half * cosines - upper_half * sine_part,
            upper_half * cosines + lower_half * sine_part,
        ],
        axis=-1,
    )


def doc_layout(starts, length):
    token_index = jnp.arange(length, dtype=jnp.int32)
    inside = token_index[:, None] >= starts[None, :]
    segment = jnp.sum(inside.astype(jnp.int32), axis=1)
    begins = jnp.max(jnp.where(inside, starts[None, :], 0), axis=1)
    return (segment, token_index - begins)


def rotary_angles(position, head_dim):
    frequency = jnp.exp(
        jnp.arange(head_dim // 2, dtype=jnp.float32) * (-2.0 * math.log(10000.0) / head_dim)
    )
    return position.astype(jnp.float32)[..., None] * frequency


def smooth_gate(values):
    return jax.nn.gelu(values, approximate=True)


def block_mask(segment, offset, block_len, key_len):
    query_pos = jnp.arange(offset, offset + block_len, dtype=jnp.int32)
    key_pos = jnp.arange(key_len, dtype=jnp.int32)
    causal = key_pos[None, :] <= query_pos[:, None]
    same_doc = segment[:, offset : offset + block_len, None] == segment[:, None, :key_len]
    return (causal[None] & same_doc)[:, None]


def block_scores(q_block, key_rows, allowed, score_scale):
    scores = score_scale * jnp.einsum(
        "rhqe,rhke->rhqk", q_block, key_rows, preferred_element_type=jnp.float32
    )
    return jnp.where(allowed, scores, -1e30)


def pad_keys(term, seq_len):
    return jnp.pad(term, ((0, 0), (0, 0), (0, seq_len - term.shape[2]), (0, 0)))


def mlp_backward(normed_rows, activated, gate_pull, grad_rows, up_weight, down_weight):
    grad_act = jnp.einsum("rtd,fd->rtf", grad_rows, down_weight, preferred_element_type=jnp.float32)
    down_term = jnp.einsum("rtf,rtd->fd", activated, grad_rows, preferred_element_type=jnp.float32)
    grad_up = gate_pull(grad_act)[0].astype(jnp.bfloat16)
    up_term = jnp.einsum("rtd,rtf->df", normed_rows, grad_up, preferred_element_type=jnp.float32)
    grad_normed = jnp.einsum("rtf,df->rtd", grad_up, up_weight, preferred_element_type=jnp.float32)
    return (grad_normed, up_term, down_term)


def shards(inputs, doc_starts, w_qkv, w_out, w_up, w_down, norm_gains, norm_biases, cotangent):
    qkv_full, out_full, up_full, down_full, gains_low, shifts_low = (
        lax.all_gather(w_qkv, "dp", axis=1, tiled=True),
        lax.all_gather(w_out, "dp", axis=1, tiled=True),
        lax.all_gather(w_up, "dp", axis=0, tiled=True),
        lax.all_gather(w_down, "dp", axis=1, tiled=True),
        lax.all_gather(norm_gains, "dp", axis=1, tiled=True),
        lax.all_gather(norm_biases, "dp", axis=1, tiled=True),
    )
    gain_rows = gains_low.astype(jnp.float32)
    shift_rows = shifts_low.astype(jnp.float32)
    micro_count, row_count, shard_len, feature_count = inputs.shape
    local_heads = w_out.shape[0] // HD
    seq_len = shard_len * lax.axis_size("tensor")
    block_len = min(512, seq_len)
    score_scale = 1.0 / math.sqrt(HD)
    up_weight, down_weight = (up_full, down_full)
    qkv_grad = jnp.zeros(qkv_full.shape, jnp.float32)
    out_grad = jnp.zeros(out_full.shape, jnp.float32)
    up_grad = jnp.zeros(up_weight.shape, jnp.float32)
    down_grad = jnp.zeros(down_weight.shape, jnp.float32)
    gains_grad = jnp.zeros(gain_rows.shape, jnp.float32)
    biases_grad = jnp.zeros(shift_rows.shape, jnp.float32)
    output_list = []
    grad_list = []
    for micro_index in range(micro_count):
        segment, position = jax.vmap(lambda starts: doc_layout(starts, seq_len))(
            doc_starts[micro_index]
        )
        head_angles = rotary_angles(position, HD)[:, None]
        x_local = inputs[micro_index].astype(jnp.float32)
        normed1, pull_first = jax.vjp(layer_norm, x_local, gain_rows[0], shift_rows[0])
        full1 = lax.all_gather(normed1.astype(jnp.bfloat16), "tensor", axis=1, tiled=True)
        projected = jnp.einsum("rtd,cde->crte", full1, qkv_full, preferred_element_type=jnp.float32)
        projected = projected.reshape(3, row_count, seq_len, local_heads, HD).transpose(
            0, 1, 3, 2, 4
        )
        queries = rotate(projected[0], head_angles).astype(jnp.bfloat16)
        key_rows = rotate(projected[1], head_angles).astype(jnp.bfloat16)
        values = projected[2].astype(jnp.bfloat16)
        pieces = []
        lse_pieces = []
        for offset in range(0, seq_len, block_len):
            key_end = offset + block_len
            allowed = block_mask(segment, offset, block_len, key_end)
            scores = block_scores(
                queries[:, :, offset:key_end], key_rows[:, :, :key_end], allowed, score_scale
            )
            row_peak = jnp.max(scores, axis=-1, keepdims=True)
            log_total = row_peak + jnp.log(
                jnp.sum(jnp.exp(scores - row_peak), axis=-1, keepdims=True)
            )
            probs = jnp.exp(scores - log_total).astype(jnp.bfloat16)
            pieces.append(
                jnp.einsum(
                    "rhqk,rhke->rhqe",
                    probs,
                    values[:, :, :key_end],
                    preferred_element_type=jnp.float32,
                ).astype(jnp.bfloat16)
            )
            lse_pieces.append(log_total)
        attended = jnp.concatenate(pieces, axis=2)
        mixed = attended.transpose(0, 2, 1, 3).reshape(row_count, seq_len, local_heads * HD)
        head_sums = jnp.einsum("rtf,fd->rtd", mixed, out_full, preferred_element_type=jnp.float32)
        branch1 = lax.psum_scatter(head_sums, "tensor", scatter_dimension=1, tiled=True)
        post1, pull_second = jax.vjp(layer_norm, branch1, gain_rows[1], shift_rows[1])
        hidden = x_local + post1
        normed2, pull_third = jax.vjp(layer_norm, hidden, gain_rows[2], shift_rows[2])
        normed2_low = normed2.astype(jnp.bfloat16)
        full2 = lax.all_gather(normed2_low, "tensor", axis=1, tiled=True)
        up_act = jnp.einsum("rtd,df->rtf", full2, up_weight, preferred_element_type=jnp.float32)
        gated, gate_pull = jax.vjp(smooth_gate, up_act)
        activated = gated.astype(jnp.bfloat16)
        unit_sums = jnp.einsum(
            "rtf,fd->rtd", activated, down_weight, preferred_element_type=jnp.float32
        )
        branch2 = lax.psum_scatter(unit_sums, "tensor", scatter_dimension=1, tiled=True)
        post2, pull_fourth = jax.vjp(layer_norm, branch2, gain_rows[3], shift_rows[3])
        output_list.append((hidden + post2).astype(jnp.bfloat16))
        upstream = cotangent[micro_index].astype(jnp.float32)
        grad_branch2, gain_three, shift_three = pull_fourth(upstream)
        grad_branch2_low = grad_branch2.astype(jnp.bfloat16)
        grad_full2 = lax.all_gather(grad_branch2_low, "tensor", axis=1, tiled=True)
        grad_normed_rows, up_term, down_term = mlp_backward(
            full2, activated, gate_pull, grad_full2, up_weight, down_weight
        )
        up_grad = up_grad + up_term
        down_grad = down_grad + down_term
        grad_normed2 = lax.psum_scatter(grad_normed_rows, "tensor", scatter_dimension=1, tiled=True)
        hidden_extra, gain_two, shift_two = pull_third(grad_normed2)
        grad_hidden = upstream + hidden_extra
        grad_branch1, gain_one, shift_one = pull_second(grad_hidden)
        grad_full1 = lax.all_gather(grad_branch1.astype(jnp.bfloat16), "tensor", axis=1, tiled=True)
        out_grad = out_grad + jnp.einsum(
            "rtf,rtd->fd", mixed, grad_full1, preferred_element_type=jnp.float32
        )
        grad_mixed = jnp.einsum(
            "rtd,fd->rtf", grad_full1, out_full, preferred_element_type=jnp.float32
        ).astype(jnp.bfloat16)
        grad_attended = grad_mixed.reshape(row_count, seq_len, local_heads, HD).transpose(
            0, 2, 1, 3
        )
        grad_keys = jnp.zeros(key_rows.shape, jnp.float32)
        grad_values = jnp.zeros(values.shape, jnp.float32)
        query_grads = []
        for block_index, offset in enumerate(range(0, seq_len, block_len)):
            key_end = offset + block_len
            allowed = block_mask(segment, offset, block_len, key_end)
            q_block = queries[:, :, offset:key_end]
            key_part = key_rows[:, :, :key_end]
            value_part = values[:, :, :key_end]
            scores = block_scores(q_block, key_part, allowed, score_scale)
            soft = jnp.exp(scores - lse_pieces[block_index])
            probs = soft.astype(jnp.bfloat16)
            grad_out_block = grad_attended[:, :, offset:key_end]
            grad_probs = jnp.einsum(
                "rhqe,rhke->rhqk", grad_out_block, value_part, preferred_element_type=jnp.float32
            )
            row_dot = jnp.sum(soft * grad_probs, axis=-1, keepdims=True)
            grad_scores = (soft * (grad_probs - row_dot)).astype(jnp.bfloat16)
            query_grads.append(
                score_scale
                * jnp.einsum(
                    "rhqk,rhke->rhqe", grad_scores, key_part, preferred_element_type=jnp.float32
                )
            )
            grad_keys = grad_keys + pad_keys(
                score_scale
                * jnp.einsum(
                    "rhqk,rhqe->rhke", grad_scores, q_block, preferred_element_type=jnp.float32
                ),
                seq_len,
            )
            grad_values = grad_values + pad_keys(
                jnp.einsum(
                    "rhqk,rhqe->rhke", probs, grad_out_block, preferred_element_type=jnp.float32
                ),
                seq_len,
            )
        grad_queries = rotate(jnp.concatenate(query_grads, axis=2), -head_angles)
        grad_keys = rotate(grad_keys, -head_angles)
        grad_projected = jnp.stack([grad_queries, grad_keys, grad_values]).transpose(0, 1, 3, 2, 4)
        grad_projected = grad_projected.reshape(3, row_count, seq_len, local_heads * HD).astype(
            jnp.bfloat16
        )
        qkv_grad = qkv_grad + jnp.einsum(
            "rtd,crte->cde", full1, grad_projected, preferred_element_type=jnp.float32
        )
        head_grads = jnp.einsum(
            "crte,cde->rtd", grad_projected, qkv_full, preferred_element_type=jnp.float32
        )
        grad_normed1 = lax.psum_scatter(
            head_grads.astype(jnp.bfloat16), "tensor", scatter_dimension=1, tiled=True
        ).astype(jnp.float32)
        grad_inputs, gain_zero, shift_zero = pull_first(grad_normed1)
        grad_list.append(grad_hidden + grad_inputs)
        gains_grad = gains_grad + jnp.stack([gain_zero, gain_one, gain_two, gain_three])
        biases_grad = biases_grad + jnp.stack([shift_zero, shift_one, shift_two, shift_three])
    qkv_part, out_part, up_part, down_part, gains_part, biases_part = (
        lax.psum_scatter(
            qkv_grad.astype(jnp.bfloat16), "dp", scatter_dimension=1, tiled=True
        ).astype(jnp.float32),
        lax.psum_scatter(
            out_grad.astype(jnp.bfloat16), "dp", scatter_dimension=1, tiled=True
        ).astype(jnp.float32),
        lax.psum_scatter(
            up_grad.astype(jnp.bfloat16), "dp", scatter_dimension=0, tiled=True
        ).astype(jnp.float32),
        lax.psum_scatter(
            down_grad.astype(jnp.bfloat16), "dp", scatter_dimension=1, tiled=True
        ).astype(jnp.float32),
        lax.psum_scatter(
            gains_grad.astype(jnp.bfloat16), "dp", scatter_dimension=1, tiled=True
        ).astype(jnp.float32),
        lax.psum_scatter(
            biases_grad.astype(jnp.bfloat16), "dp", scatter_dimension=1, tiled=True
        ).astype(jnp.float32),
    )
    gains_part, biases_part = lax.psum((gains_part, biases_part), "tensor")
    return (
        jnp.stack(output_list),
        jnp.stack(grad_list),
        qkv_part,
        out_part,
        up_part,
        down_part,
        gains_part,
        biases_part,
    )


def solution(mesh):
    placed = (
        P(None, "dp", "tensor", None),
        P(None, "dp", None),
        P(None, "dp", "tensor"),
        P("tensor", "dp"),
        P("dp", "tensor"),
        P("tensor", "dp"),
        P(None, "dp"),
        P(None, "dp"),
        P(None, "dp", "tensor", None),
    )
    return jax.shard_map(
        shards,
        mesh=mesh,
        in_specs=placed,
        out_specs=(
            P(None, "dp", "tensor", None),
            P(None, "dp", "tensor", None),
            P(None, "dp", "tensor"),
            P("tensor", "dp"),
            P("dp", "tensor"),
            P("tensor", "dp"),
            P(None, "dp"),
            P(None, "dp"),
        ),
        check_vma=False,
    )
```

profile of v0, /device:TPU:0, one launch (start us, length us, event | category | flops | bytes accessed | tf_op | source)
XLA Modules:
  0.0 1805.9 jit_solution(1437305494737454471)
XLA Ops:
  50.1 26.7 %all-gather.15.cloned.1.call-done = bf16[1,1024,1024]{2,1,0:T(8,128)(2,1)} async-done(((bf16[1,128,1024]{2,1,0:T(8,128)(2,1)}), bf16[1,1024,1024]{2,1,0:T(8,128)(2,1)}) %all-gather.15.cloned.1.call-update) | async-done | bytes 2097168 | tf_op jit(solution)/shard_map/all_gather | solution.py:115
  91.2 36.0 %all-gather.23.cloned.1.call-done = bf16[1,1024,1024]{2,1,0:T(8,128)(2,1)} async-done(((bf16[1,128,1024]{2,1,0:T(8,128)(2,1)}), bf16[1,1024,1024]{2,1,0:T(8,128)(2,1)}) %all-gather.23.cloned.1.call-update) | async-done | bytes 2097168 | tf_op jit(solution)/shard_map/all_gather | solution.py:115
  143.1 34.1 %all-gather.27.cloned.1.call-done = bf16[1,1024,1024]{2,1,0:T(8,128)(2,1)} async-done(((bf16[1,128,1024]{2,1,0:T(8,128)(2,1)}), bf16[1,1024,1024]{2,1,0:T(8,128)(2,1)}) %all-gather.27.cloned.1.call-update) | async-done | bytes 2097168 | tf_op jit(solution)/shard_map/all_gather | solution.py:115
  192.2 74.9 %reduce-scatter.23.cloned.1.call-done = f32[1,128,1024]{2,1,0:T(8,128)} async-done(((f32[1,1024,1024]{2,1,0:T(8,128)}), f32[1,128,1024]{2,1,0:T(8,128)}) %reduce-scatter.23.cloned.1.call-update) | async-done | bytes 524304 | tf_op jit(solution)/shard_map/reduce_scatter | solution.py:148
  271.2 87.7 %reduce-scatter.27.cloned.1.call-done = f32[1,128,1024]{2,1,0:T(8,128)} async-done(((f32[1,1024,1024]{2,1,0:T(8,128)}), f32[1,128,1024]{2,1,0:T(8,128)}) %reduce-scatter.27.cloned.1.call-update) | async-done | bytes 524304 | tf_op jit(solution)/shard_map/reduce_scatter | solution.py:148
  362.9 87.2 %reduce-scatter.31.cloned.1.call-done = f32[1,128,1024]{2,1,0:T(8,128)} async-done(((f32[1,1024,1024]{2,1,0:T(8,128)}), f32[1,128,1024]{2,1,0:T(8,128)}) %reduce-scatter.31.cloned.1.call-update) | async-done | bytes 524304 | tf_op jit(solution)/shard_map/reduce_scatter | solution.py:148
  459.3 47.1 %all-gather.17.cloned.1.call-done = bf16[1,1024,1024]{2,1,0:T(8,128)(2,1)} async-done(((bf16[1,128,1024]{2,1,0:T(8,128)(2,1)}), bf16[1,1024,1024]{2,1,0:T(8,128)(2,1)}) %all-gather.17.cloned.1.call-update) | async-done | bytes 2097168 | tf_op jit(solution)/shard_map/all_gather | solution.py:153
  528.5 46.3 %all-gather.25.cloned.1.call-done = bf16[1,1024,1024]{2,1,0:T(8,128)(2,1)} async-done(((bf16[1,128,1024]{2,1,0:T(8,128)(2,1)}), bf16[1,1024,1024]{2,1,0:T(8,128)(2,1)}) %all-gather.25.cloned.1.call-update) | async-done | bytes 2097168 | tf_op jit(solution)/shard_map/all_gather | solution.py:153
  582.9 42.2 %all-gather.29.cloned.1.call-done = bf16[1,1024,1024]{2,1,0:T(8,128)(2,1)} async-done(((bf16[1,128,1024]{2,1,0:T(8,128)(2,1)}), bf16[1,1024,1024]{2,1,0:T(8,128)(2,1)}) %all-gather.29.cloned.1.call-update) | async-done | bytes 2097168 | tf_op jit(solution)/shard_map/all_gather | solution.py:153
  633.0 82.4 %reduce-scatter.25.cloned.1.call-done = f32[1,128,1024]{2,1,0:T(8,128)} async-done(((f32[1,1024,1024]{2,1,0:T(8,128)}), f32[1,128,1024]{2,1,0:T(8,128)}) %reduce-scatter.25.cloned.1.call-update) | async-done | bytes 524304 | tf_op jit(solution)/shard_map/reduce_scatter | solution.py:160
  717.1 89.4 %reduce-scatter.29.cloned.1.call-done = f32[1,128,1024]{2,1,0:T(8,128)} async-done(((f32[1,1024,1024]{2,1,0:T(8,128)}), f32[1,128,1024]{2,1,0:T(8,128)}) %reduce-scatter.29.cloned.1.call-update) | async-done | bytes 524304 | tf_op jit(solution)/shard_map/reduce_scatter | solution.py:160
  814.3 83.7 %reduce-scatter.33.cloned.1.call-done = f32[1,128,1024]{2,1,0:T(8,128)} async-done(((f32[1,1024,1024]{2,1,0:T(8,128)}), f32[1,128,1024]{2,1,0:T(8,128)}) %reduce-scatter.33.cloned.1.call-update) | async-done | bytes 524304 | tf_op jit(solution)/shard_map/reduce_scatter | solution.py:160
  913.9 44.0 %all-gather.31.cloned.1.call-done = bf16[1,1024,1024]{2,1,0:T(8,128)(2,1)} async-done(((bf16[1,128,1024]{2,1,0:T(8,128)(2,1)}), bf16[1,1024,1024]{2,1,0:T(8,128)(2,1)}) %all-gather.31.cloned.1.call-update) | async-done | bytes 2097168 | tf_op jit(solution)/shard_map/all_gather | solution.py:166
  967.4 61.6 %all-gather.35.cloned.1.call-done = bf16[1,1024,1024]{2,1,0:T(8,128)(2,1)} async-done(((bf16[1,128,1024]{2,1,0:T(8,128)(2,1)}), bf16[1,1024,1024]{2,1,0:T(8,128)(2,1)}) %all-gather.35.cloned.1.call-update) | async-done | bytes 2097168 | tf_op jit(solution)/shard_map/all_gather | solution.py:166
  1038.4 52.9 %all-gather.39.cloned.1.call-done = bf16[1,1024,1024]{2,1,0:T(8,128)(2,1)} async-done(((bf16[1,128,1024]{2,1,0:T(8,128)(2,1)}), bf16[1,1024,1024]{2,1,0:T(8,128)(2,1)}) %all-gather.39.cloned.1.call-update) | async-done | bytes 2097168 | tf_op jit(solution)/shard_map/all_gather | solution.py:166
  1100.7 78.6 %reduce-scatter.39.cloned.1.call-done = f32[1,128,1024]{2,1,0:T(8,128)} async-done(((f32[1,1024,1024]{2,1,0:T(8,128)}), f32[1,128,1024]{2,1,0:T(8,128)}) %reduce-scatter.39.cloned.1.call-update) | async-done | bytes 524304 | tf_op jit(solution)/shard_map/reduce_scatter | solution.py:172
  1179.3 91.1 %reduce-scatter.43.cloned.1.call-done = f32[1,128,1024]{2,1,0:T(8,128)} async-done(((f32[1,1024,1024]{2,1,0:T(8,128)}), f32[1,128,1024]{2,1,0:T(8,128)}) %reduce-scatter.43.cloned.1.call-update) | async-done | bytes 524304 | tf_op jit(solution)/shard_map/reduce_scatter | solution.py:172
  1300.2 28.9 %all-gather.37.cloned.1.call-done = bf16[1,1024,1024]{2,1,0:T(8,128)(2,1)} async-done(((bf16[1,128,1024]{2,1,0:T(8,128)(2,1)}), bf16[1,1024,1024]{2,1,0:T(8,128)(2,1)}) %all-gather.37.cloned.1.call-update) | async-done | bytes 2097168 | tf_op jit(solution)/shard_map/all_gather | solution.py:176
  1336.5 42.7 %all-gather.33.cloned.1.call-done = bf16[1,1024,1024]{2,1,0:T(8,128)(2,1)} async-done(((bf16[1,128,1024]{2,1,0:T(8,128)(2,1)}), bf16[1,1024,1024]{2,1,0:T(8,128)(2,1)}) %all-gather.33.cloned.1.call-update) | async-done | bytes 2097168 | tf_op jit(solution)/shard_map/all_gather | solution.py:176
  1386.5 42.8 %all-gather.41.cloned.1.call-done = bf16[1,1024,1024]{2,1,0:T(8,128)(2,1)} async-done(((bf16[1,128,1024]{2,1,0:T(8,128)(2,1)}), bf16[1,1024,1024]{2,1,0:T(8,128)(2,1)}) %all-gather.41.cloned.1.call-update) | async-done | bytes 2097168 | tf_op jit(solution)/shard_map/all_gather | solution.py:176
  1517.2 69.9 %reduce-scatter.45.cloned.1.call-done = bf16[1,128,1024]{2,1,0:T(8,128)(2,1)} async-done(((bf16[1,1024,1024]{2,1,0:T(8,128)(2,1)}), bf16[1,128,1024]{2,1,0:T(8,128)(2,1)}) %reduce-scatter.45.cloned.1.call-update) | async-done | bytes 262160 | tf_op jit(solution)/shard_map/reduce_scatter | solution.py:235
  1587.0 70.7 %reduce-scatter.37.cloned.1.call-done = bf16[1,128,1024]{2,1,0:T(8,128)(2,1)} async-done(((bf16[1,1024,1024]{2,1,0:T(8,128)(2,1)}), bf16[1,128,1024]{2,1,0:T(8,128)(2,1)}) %reduce-scatter.37.cloned.1.call-update) | async-done | bytes 262160 | tf_op jit(solution)/shard_map/reduce_scatter | solution.py:235
  1657.7 70.7 %reduce-scatter.41.cloned.1.call-done = bf16[1,128,1024]{2,1,0:T(8,128)(2,1)} async-done(((bf16[1,1024,1024]{2,1,0:T(8,128)(2,1)}), bf16[1,128,1024]{2,1,0:T(8,128)(2,1)}) %reduce-scatter.41.cloned.1.call-update) | async-done | bytes 262160 | tf_op jit(solution)/shard_map/reduce_scatter | solution.py:235
  1775.8 22.2 %all-reduce.6 = (f32[4,256]{1,0:T(4,128)}, f32[4,256]{1,0:T(4,128)}) all-reduce(bf16[4,256]{1,0:T(4,128)(2,1)S(1)} %copy.105, bf16[4,256]{1,0:T(4,128)(2,1)S(1)} %copy.107), channel_id=1, replica_groups=mesh['dp'=4,'tensor'=8] {'tensor'}, use_global_device_ids=true, to_apply=%region_101.102 | all-reduce | flops 2048 | bytes 12288 | tf_op jit(solution)/shard_map/psum | solution.py:262
  (817 shorter events, 372.4 us)
Async XLA Ops:
  26.6 150.6 %all-gather.27.cloned.1.call-start = ((), (), s32[]{:S(2)}) async-start(), calls=%async_computation.28 | async-start | bytes 2359296 | tf_op jit(solution)/shard_map/all_gather | solution.py:115
  27.3 239.8 %reduce-scatter.23.cloned.1.call-start = ((), (), s32[]{:S(2)}) async-start(), calls=%async_computation.19 | async-start | bytes 4718592 | tf_op jit(solution)/shard_map/reduce_scatter | solution.py:148
  90.0 268.9 %reduce-scatter.27.cloned.1.call-start = ((), (), s32[]{:S(2)}) async-start(), calls=%async_computation.25 | async-start | bytes 4718592 | tf_op jit(solution)/shard_map/reduce_scatter | solution.py:148
  141.5 308.5 %reduce-scatter.31.cloned.1.call-start = ((), (), s32[]{:S(2)}) async-start(), calls=%async_computation.29 | async-start | bytes 4718592 | tf_op jit(solution)/shard_map/reduce_scatter | solution.py:148
  191.6 267.7 %all-gather.19.cloned.1.call-start = ((), (), s32[]{:S(2)}) async-start(), calls=%async_computation.21 | async-start | bytes 1310720 | tf_op jit(solution)/shard_map/all_gather | solution.py:87
  192.1 314.2 %all-gather.17.cloned.1.call-start = ((), (), s32[]{:S(2)}) async-start(), calls=%async_computation.20 | async-start | bytes 2359296 | tf_op jit(solution)/shard_map/all_gather | solution.py:153
  458.5 166.6 %all-gather.29.cloned.1.call-start = ((), (), s32[]{:S(2)}) async-start(), calls=%async_computation.30 | async-start | bytes 2359296 | tf_op jit(solution)/shard_map/all_gather | solution.py:153
  459.2 256.3 %reduce-scatter.25.cloned.1.call-start = ((), (), s32[]{:S(2)}) async-start(), calls=%async_computation.23 | async-start | bytes 4718592 | tf_op jit(solution)/shard_map/reduce_scatter | solution.py:160
  528.3 278.2 %reduce-scatter.29.cloned.1.call-start = ((), (), s32[]{:S(2)}) async-start(), calls=%async_computation.27 | async-start | bytes 4718592 | tf_op jit(solution)/shard_map/reduce_scatter | solution.py:160
  582.8 315.2 %reduce-scatter.33.cloned.1.call-start = ((), (), s32[]{:S(2)}) async-start(), calls=%async_computation.31 | async-start | bytes 4718592 | tf_op jit(solution)/shard_map/reduce_scatter | solution.py:160
  633.0 324.9 %all-gather.31.cloned.1.call-start = ((), (), s32[]{:S(2)}) async-start(), calls=%async_computation.32 | async-start | bytes 2359296 | tf_op jit(solution)/shard_map/all_gather | solution.py:166
  908.7 120.3 %all-gather.35.cloned.1.call-start = ((), (), s32[]{:S(2)}) async-start(), calls=%async_computation.36 | async-start | bytes 2359296 | tf_op jit(solution)/shard_map/all_gather | solution.py:166
  911.3 180.0 %all-gather.39.cloned.1.call-start = ((), (), s32[]{:S(2)}) async-start(), calls=%async_computation.40 | async-start | bytes 2359296 | tf_op jit(solution)/shard_map/all_gather | solution.py:166
  913.8 186.9 %reduce-scatter.35.cloned.1.call-start = ((), (), s32[]{:S(2)}) async-start(), calls=%async_computation.33 | async-start | bytes 4718592 | tf_op jit(solution)/shard_map/reduce_scatter | solution.py:172
  967.1 212.2 %reduce-scatter.39.cloned.1.call-start = ((), (), s32[]{:S(2)}) async-start(), calls=%async_computation.37 | async-start | bytes 4718592 | tf_op jit(solution)/shard_map/reduce_scatter | solution.py:172
  1038.3 232.1 %reduce-scatter.43.cloned.1.call-start = ((), (), s32[]{:S(2)}) async-start(), calls=%async_computation.41 | async-start | bytes 4718592 | tf_op jit(solution)/shard_map/reduce_scatter | solution.py:172
  1100.6 228.5 %all-gather.37.cloned.1.call-start = ((), (), s32[]{:S(2)}) async-start(), calls=%async_computation.38 | async-start | bytes 2359296 | tf_op jit(solution)/shard_map/all_gather | solution.py:176
  1282.5 146.8 %all-gather.41.cloned.1.call-start = ((), (), s32[]{:S(2)}) async-start(), calls=%async_computation.42 | async-start | bytes 2359296 | tf_op jit(solution)/shard_map/all_gather | solution.py:176
  1283.4 212.5 %reduce-scatter.53.cloned.1.call-start = ((), (), s32[]{:S(2)}) async-start(), calls=%async_computation.47 | async-start | bytes 1310720 | tf_op jit(solution)/shard_map/reduce_scatter | solution.py:252
  1292.3 205.3 %reduce-scatter.51.cloned.1.call-start = ((), (), s32[]{:S(2)}) async-start(), calls=%async_computation.46 | async-start | bytes 1310720 | tf_op jit(solution)/shard_map/reduce_scatter | solution.py:249
  1299.9 199.6 %reduce-scatter.49.cloned.1.call-start = ((), (), s32[]{:S(2)}) async-start(), calls=%async_computation.45 | async-start | bytes 327680 | tf_op jit(solution)/shard_map/reduce_scatter | solution.py:246
  1484.8 172.9 %reduce-scatter.37.cloned.1.call-start = ((), (), s32[]{:S(2)}) async-start(), calls=%async_computation.35 | async-start | bytes 2359296 | tf_op jit(solution)/shard_map/reduce_scatter | solution.py:235
  1489.8 238.7 %reduce-scatter.41.cloned.1.call-start = ((), (), s32[]{:S(2)}) async-start(), calls=%async_computation.39 | async-start | bytes 2359296 | tf_op jit(solution)/shard_map/reduce_scatter | solution.py:235
  1493.6 258.9 %reduce-scatter.55.cloned.1.call-start = ((), (), s32[]{:S(2)}) async-start(), calls=%async_computation.48 | async-start | bytes 327680
  (263 other events, 7898.2 us)
Sparse Core Ops, SparseCore 0:
  25.9 50.7 all-gather.14
  79.4 47.7 all-gather.22
  129.4 47.7 all-gather.26
  180.7 86.4 reduce-scatter.22
  271.0 87.8 reduce-scatter.26
  362.4 87.6 reduce-scatter.30
  908.8 48.9 all-gather.30
  960.2 68.7 all-gather.34
  1031.1 60.1 all-gather.38
  1280.1 48.9 all-gather.36
  1331.4 47.7 all-gather.32
  1381.4 47.7 all-gather.40
Sparse Core Ops, SparseCore 1:
  193.6 15.1 all-gather.18
  457.2 49.1 all-gather.16
  507.9 15.1 all-gather.20
  525.4 49.3 all-gather.24
  577.2 47.8 all-gather.28
  629.1 86.3 reduce-scatter.24
  719.0 87.5 reduce-scatter.28
  810.5 87.5 reduce-scatter.32
  967.2 119.6 reduce-scatter.34
  1090.9 88.3 reduce-scatter.38
  1182.8 87.5 reduce-scatter.42
  1292.4 24.6 reduce-scatter.52
  1319.5 24.9 reduce-scatter.50
  1471.1 18.4 reduce-scatter.48
  1492.1 23.2 reduce-scatter.46
  1519.3 67.7 reduce-scatter.44
  1591.0 66.7 reduce-scatter.36
  1661.7 66.7 reduce-scatter.40
  1733.5 18.9 reduce-scatter.54
  1754.9 19.9 reduce-scatter.56
where the time goes:
time: 1820 us; the launch traced here: 1810 us
  waiting for transfers between devices  1460 us (80%)
  matrix products  148 us (8%)
  other arithmetic  84.9 us (5%)
  blocking collectives  48.7 us (3%)
  local copies, waits for them, and re-layouts  41.2 us (2%)
  between operations  19.6 us (1%)
    reduce_scatter x3, waiting for transfers between devices, shards(): lax.psum_scatter(unit_sums, 'tensor', scatter_dimension=1, tiled=True)  256 us
    reduce_scatter x3, waiting for transfers between devices, shards(): lax.psum_scatter(head_sums, 'tensor', scatter_dimension=1, tiled=True)  250 us
    reduce_scatter x3, waiting for transfers between devices, shards(): lax.psum_scatter(head_grads.astype(jnp.bfloat16), 'tensor', scatter_dimen...  211 us
    reduce_scatter x3, waiting for transfers between devices, shards(): lax.psum_scatter(grad_normed_rows, 'tensor', scatter_dimension=1, tiled=T...  170 us
    all_gather x3, waiting for transfers between devices, shards(): grad_full2 = lax.all_gather(grad_branch2_low, 'tensor', axis=1, tiled=True)  159 us
    all_gather x3, waiting for transfers between devices, shards(): full2 = lax.all_gather(normed2_low, 'tensor', axis=1, tiled=True)  136 us
    all_gather x3, waiting for transfers between devices, shards(): lax.all_gather(grad_branch1.astype(jnp.bfloat16), 'tensor', axis=1, tiled...  114 us
    all_gather x3, waiting for transfers between devices, shards(): lax.all_gather(normed1.astype(jnp.bfloat16), 'tensor', axis=1, tiled=True)  96.8 us
  transfers between devices with their start and end apart: 32, of which 27 were waited for; matrix products, arithmetic and copies ran while one was open for 12% of the time, Pallas kernels for 0%

commit v1 on v0

v1 whole, which is shorter than its diff:
```python
import math

import jax
import jax.numpy as jnp
from jax import lax
from jax.sharding import Mesh, PartitionSpec as P

HD = 64
EPSILON = 1e-05
F32 = jnp.float32
BF16 = jnp.bfloat16
CHIPS = ("y", "z", "x")
SEQ = ("z", "x")
SWAP = [(0, 1), (1, 0)]


def ln_forward(values, gain, shift):
    average = jnp.mean(values, axis=-1, keepdims=True)
    centred = values - average
    variance = jnp.mean(centred * centred, axis=-1, keepdims=True)
    scale = lax.rsqrt(variance + EPSILON)
    xhat = centred * scale
    return xhat * gain + shift, xhat, scale


def ln_backward(grad, xhat, scale, gain):
    e = grad * gain
    dv = scale * (
        e - jnp.mean(e, axis=-1, keepdims=True) - xhat * jnp.mean(e * xhat, axis=-1, keepdims=True)
    )
    return dv, jnp.sum(grad * xhat, axis=0), jnp.sum(grad, axis=0)


def rotate(values, cosines, sines):
    half_dim = values.shape[-1] // 2
    lower = values[..., :half_dim]
    upper = values[..., half_dim:]
    return jnp.concatenate(
        [lower * cosines - upper * sines, upper * cosines + lower * sines], axis=-1
    )


def doc_layout(starts, token_index):
    inside = token_index[:, None] >= starts[None, :]
    segment = jnp.sum(inside.astype(jnp.int32), axis=1)
    begins = jnp.max(jnp.where(inside, starts[None, :], 0), axis=1)
    return segment, token_index - begins


def angles_of(position):
    frequency = jnp.exp(
        jnp.arange(HD // 2, dtype=F32) * (-2.0 * math.log(10000.0) / HD)
    )
    angles = position.astype(F32)[..., None] * frequency
    return jnp.cos(angles), jnp.sin(angles)


def block_mask(segment, offset, block_len, key_len):
    query_pos = jnp.arange(offset, offset + block_len, dtype=jnp.int32)
    key_pos = jnp.arange(key_len, dtype=jnp.int32)
    causal = key_pos[None, :] <= query_pos[:, None]
    return causal & (segment[offset : offset + block_len, None] == segment[None, :key_len])


def attention_forward(q, k, v, segment):
    seq_len = q.shape[1]
    block_len = min(512, seq_len)
    pieces, lses = [], []
    for offset in range(0, seq_len, block_len):
        end = offset + block_len
        allowed = block_mask(segment, offset, block_len, end)[None]
        scores = 0.125 * jnp.einsum(
            "hqe,hke->hqk", q[:, offset:end], k[:, :end], preferred_element_type=F32
        )
        scores = jnp.where(allowed, scores, -1e30)
        peak = jnp.max(scores, axis=-1, keepdims=True)
        lse = peak + jnp.log(jnp.sum(jnp.exp(scores - peak), axis=-1, keepdims=True))
        probs = jnp.exp(scores - lse).astype(BF16)
        pieces.append(
            jnp.einsum("hqk,hke->hqe", probs, v[:, :end], preferred_element_type=F32).astype(BF16)
        )
        lses.append(lse)
    return jnp.concatenate(pieces, axis=1), lses


def attention_backward(q, k, v, do, lses, segment):
    seq_len = q.shape[1]
    block_len = min(512, seq_len)
    dq = []
    dk = jnp.zeros(k.shape, F32)
    dv = jnp.zeros(v.shape, F32)
    for index, offset in enumerate(range(0, seq_len, block_len)):
        end = offset + block_len
        allowed = block_mask(segment, offset, block_len, end)[None]
        qb, kb, vb, dob = q[:, offset:end], k[:, :end], v[:, :end], do[:, offset:end]
        scores = 0.125 * jnp.einsum("hqe,hke->hqk", qb, kb, preferred_element_type=F32)
        scores = jnp.where(allowed, scores, -1e30)
        soft = jnp.exp(scores - lses[index])
        probs = soft.astype(BF16)
        dp = jnp.einsum("hqe,hke->hqk", dob, vb, preferred_element_type=F32)
        dot = jnp.sum(soft * dp, axis=-1, keepdims=True)
        ds = (soft * (dp - dot)).astype(BF16)
        dq.append(0.125 * jnp.einsum("hqk,hke->hqe", ds, kb, preferred_element_type=F32))
        pad = ((0, 0), (0, seq_len - end), (0, 0))
        dk = dk + jnp.pad(
            0.125 * jnp.einsum("hqk,hqe->hke", ds, qb, preferred_element_type=F32), pad
        )
        dv = dv + jnp.pad(jnp.einsum("hqk,hqe->hke", probs, dob, preferred_element_type=F32), pad)
    return jnp.concatenate(dq, axis=1), dk, dv


def gather_both(shard):
    mine = lax.all_gather(shard, CHIPS, axis=0, tiled=False)
    return jnp.stack([mine, lax.ppermute(mine, "c", SWAP)])


def scatter_both(partial, sizes):
    ny, nz, nx = sizes
    shard_shape = partial.shape[2:]
    low = partial.astype(BF16)
    got = lax.ppermute(low[1], "c", SWAP)
    mine = (low[0].astype(F32) + got.astype(F32)).astype(BF16)
    mine = mine.reshape((ny, nz, nx) + shard_shape)
    mine = mine.transpose((0, 2, 1) + tuple(range(3, mine.ndim)))
    mine = mine.reshape((ny * nx, nz) + shard_shape)
    mine = lax.psum_scatter(mine, ("y", "x"), scatter_dimension=0, tiled=False)
    return lax.psum_scatter(mine, "z", scatter_dimension=0, tiled=False).astype(F32)


def shards(inputs, doc_starts, w_qkv, w_out, w_up, w_down, norm_gains, norm_biases, cotangent):
    ny, nz, nx = (lax.axis_size(name) for name in CHIPS)
    core = lax.axis_index("c")
    sizes = (ny, nz, nx)
    parts = nz * nx
    micro, _, shard_len, width = inputs.shape
    tokens = micro * shard_len
    seq_len = shard_len * parts
    dpart = width // (2 * ny)
    hcols = w_out.shape[0]
    heads = hcols // HD
    units = w_up.shape[1]

    def to_own(values):
        pieces = values.reshape(values.shape[:-1] + (ny, 2, dpart))
        pieces = jnp.where(core == 0, pieces, pieces[..., ::-1, :])
        return jnp.swapaxes(pieces, -3, -2).reshape(values.shape)

    def from_own(values):
        pieces = jnp.swapaxes(values.reshape(values.shape[:-1] + (2, ny, dpart)), -3, -2)
        return jnp.where(core == 0, pieces, pieces[..., ::-1, :]).reshape(values.shape)

    qkv_all = gather_both(w_qkv).reshape(2, ny, parts, 3, dpart, hcols)
    norms = jnp.stack([norm_gains, norm_biases])
    norms = gather_dp(norms, ny, dpart)
    norms = to_own(norms.astype(F32))
    gains, shifts = norms[0], norms[1]
    out_all = gather_both(w_out).reshape(2, ny, parts, hcols, dpart)
    up_all = gather_both(w_up).reshape(2, ny, parts, dpart, units)
    down_all = gather_both(w_down).reshape(2, ny, parts, units, dpart)

    qkv_full = qkv_all.transpose(0, 1, 4, 3, 2, 5).reshape(width, 3 * parts * hcols)
    out_full = out_all.transpose(2, 3, 0, 1, 4).reshape(parts * hcols, width)
    up_full = up_all.transpose(0, 1, 3, 2, 4).reshape(width, parts * units)
    down_full = down_all.transpose(2, 3, 0, 1, 4).reshape(parts * units, width)

    x = to_own(inputs.reshape(tokens, width)).astype(F32)
    cot = to_own(cotangent.reshape(tokens, width)).astype(F32)
    place = lax.axis_index(SEQ) * shard_len + jnp.arange(shard_len, dtype=jnp.int32)
    cos_own, sin_own, cos_row, sin_row, segments = [], [], [], [], []
    for index in range(micro):
        starts = doc_starts[index, 0]
        c, s = angles_of(doc_layout(starts, place)[1])
        cos_own.append(c)
        sin_own.append(s)
        segment, position = doc_layout(starts, jnp.arange(seq_len, dtype=jnp.int32))
        c, s = angles_of(position)
        cos_row.append(c)
        sin_row.append(s)
        segments.append(segment)
    cos_own = jnp.concatenate(cos_own)[:, None, None]
    sin_own = jnp.concatenate(sin_own)[:, None, None]

    normed1, xhat0, scale0 = ln_forward(x, gains[0], shifts[0])
    normed1 = normed1.astype(BF16)
    projected = jnp.dot(normed1, qkv_full, preferred_element_type=F32)
    projected = projected.reshape(tokens, 3, parts * heads, HD)
    rotated = rotate(projected[:, :2], cos_own, sin_own)
    projected = jnp.concatenate([rotated, projected[:, 2:]], axis=1).astype(BF16)
    projected = projected.reshape(micro, shard_len, 3, parts, hcols).transpose(0, 3, 2, 1, 4)

    def to_heads(values):
        kinds = values.shape[1]
        got = lax.all_to_all(values, SEQ, 0, 0, tiled=True)
        got = got.reshape(parts, kinds, shard_len, heads, HD).transpose(1, 3, 0, 2, 4)
        return got.reshape(kinds, heads, seq_len, HD)

    def to_tokens(values):
        kinds = values.shape[0]
        sent = values.reshape(kinds, heads, parts, shard_len, HD).transpose(2, 0, 3, 1, 4)
        sent = sent.reshape(parts, kinds, shard_len, hcols)
        return lax.all_to_all(sent, SEQ, 0, 0, tiled=True)

    qkvs, lses, attended = [], [], []
    for index in range(micro):
        q, k, v = to_heads(projected[index])
        out, lse = attention_forward(q, k, v, segments[index])
        qkvs.append((q, k, v))
        lses.append(lse)
        attended.append(to_tokens(out[None])[:, 0])
    attended = jnp.stack(attended).transpose(0, 2, 1, 3).reshape(tokens, parts * hcols)

    branch1 = jnp.dot(attended, out_full, preferred_element_type=F32)
    post1, xhat1, scale1 = ln_forward(branch1, gains[1], shifts[1])
    hidden = x + post1
    normed2, xhat2, scale2 = ln_forward(hidden, gains[2], shifts[2])
    normed2 = normed2.astype(BF16)
    up_act = jnp.dot(normed2, up_full, preferred_element_type=F32)
    gated, gate_pull = jax.vjp(lambda u: jax.nn.gelu(u, approximate=True), up_act)
    activated = gated.astype(BF16)
    branch2 = jnp.dot(activated, down_full, preferred_element_type=F32)
    post2, xhat3, scale3 = ln_forward(branch2, gains[3], shifts[3])
    outputs = (hidden + post2).astype(BF16)

    grad_branch2, gain3, shift3 = ln_backward(cot, xhat3, scale3, gains[3])
    grad_branch2 = grad_branch2.astype(BF16)
    down_part = jnp.einsum("tf,td->fd", activated, grad_branch2, preferred_element_type=F32)
    down_part = down_part.astype(BF16).reshape(parts, units, 2, ny, dpart)
    down_grad = scatter_both(
        down_part.transpose(2, 3, 0, 1, 4).reshape(2, ny * parts, units, dpart), sizes
    )
    grad_act = jnp.einsum("td,fd->tf", grad_branch2, down_full, preferred_element_type=F32)
    grad_up = gate_pull(grad_act)[0].astype(BF16)
    up_part = jnp.einsum("td,tf->df", normed2, grad_up, preferred_element_type=F32)
    up_part = up_part.astype(BF16).reshape(2, ny, dpart, parts, units)
    up_grad = scatter_both(
        up_part.transpose(0, 1, 3, 2, 4).reshape(2, ny * parts, dpart, units), sizes
    )
    grad_normed2 = jnp.einsum("tf,df->td", grad_up, up_full, preferred_element_type=F32)
    extra, gain2, shift2 = ln_backward(grad_normed2, xhat2, scale2, gains[2])
    grad_hidden = cot + extra
    grad_branch1, gain1, shift1 = ln_backward(grad_hidden, xhat1, scale1, gains[1])
    grad_branch1 = grad_branch1.astype(BF16)
    grad_attended = jnp.einsum(
        "td,fd->tf", grad_branch1, out_full, preferred_element_type=F32
    ).astype(BF16)
    grad_attended = grad_attended.reshape(micro, shard_len, parts, 1, hcols)
    grad_attended = grad_attended.transpose(0, 2, 3, 1, 4)
    out_part = jnp.einsum("tf,td->fd", attended, grad_branch1, preferred_element_type=F32)
    out_part = out_part.astype(BF16).reshape(parts, hcols, 2, ny, dpart)
    out_grad = scatter_both(
        out_part.transpose(2, 3, 0, 1, 4).reshape(2, ny * parts, hcols, dpart), sizes
    )

    grad_projected = []
    for index in range(micro):
        do = to_heads(grad_attended[index])[0]
        q, k, v = qkvs[index]
        dq, dk, dv = attention_backward(q, k, v, do, lses[index], segments[index])
        cos, sin = cos_row[index], -sin_row[index]
        back = jnp.stack([rotate(dq, cos, sin), rotate(dk, cos, sin), dv]).astype(BF16)
        grad_projected.append(to_tokens(back))
    grad_projected = jnp.stack(grad_projected).transpose(0, 3, 2, 1, 4)
    grad_projected = grad_projected.reshape(tokens, 3 * parts * hcols)
    qkv_part = jnp.einsum("td,te->de", normed1, grad_projected, preferred_element_type=F32)
    qkv_part = qkv_part.astype(BF16).reshape(2, ny, dpart, 3, parts, hcols)
    qkv_grad = scatter_both(
        qkv_part.transpose(0, 1, 4, 3, 2, 5).reshape(2, ny * parts, 3, dpart, hcols), sizes
    )
    grad_normed1 = jnp.einsum(
        "te,de->td", grad_projected, qkv_full, preferred_element_type=F32
    )
    extra, gain0, shift0 = ln_backward(grad_normed1, xhat0, scale0, gains[0])
    inputs_grad = grad_hidden + extra
    sums = jnp.stack([gain0, gain1, gain2, gain3, shift0, shift1, shift2, shift3])
    sums = lax.psum(from_own(sums), ("y", "c", "z", "x"))
    place = (lax.axis_index("y") * 2 + core) * dpart
    sums = lax.dynamic_slice_in_dim(sums, place, dpart, 1)
    return (
        from_own(outputs).reshape(inputs.shape),
        from_own(inputs_grad).reshape(inputs.shape),
        qkv_grad,
        out_grad,
        up_grad,
        down_grad,
        sums[:4],
        sums[4:],
    )


def gather_dp(norms, ny, dpart):
    full = lax.all_gather(norms, ("y", "c"), axis=2, tiled=True)
    return full


def solution(mesh):
    dp, tensor = mesh.shape["dp"], mesh.shape["tensor"]
    names = ("y", "c", "z", "x")
    fine = Mesh(mesh.devices.reshape(dp // 2, 2, 4, tensor // 4), names)
    rows, seq = ("y", "c"), ("z", "x")
    tokens = P(None, rows, seq, None)
    weights = (P(None, rows, seq), P(seq, rows), P(rows, seq), P(seq, rows))
    norm = P(None, rows)
    return jax.shard_map(
        shards,
        mesh=fine,
        in_specs=(tokens, P(None, rows, None)) + weights + (norm, norm, tokens),
        out_specs=(tokens, tokens) + weights + (norm, norm),
        check_vma=False,
    )
```

time: 1820 us -> 1020 us (0.56)
  waiting for transfers between devices: 1460 us -> 382 us
  local copies, waits for them, and re-layouts: 41.2 us -> 270 us
  starting transfers between devices: 3.19 us -> 62.1 us
    reduce_scatter x16 -> x4, waiting for transfers between devices: 901 us -> 52.7 us  [scatter_both(): lax.psum_scatter(mine, 'z', scatter_dimension=0, tiled=False).astype(F32)]
    all_gather x14 -> x4, waiting for transfers between devices: 518 us -> 187 us  [gather_both(): mine = lax.all_gather(shard, CHIPS, axis=0, tiled=False)]
    transpose x0 -> x13, local copies, waits for them, and re-layouts: none -> 66.6 us  [the longest x1 16.2 us: shards(): qkv_all.transpose(0, 1, 4, 3, 2, 5).reshape(width, 3 * parts * hcols)]
    reshape x0 -> x14, local copies, waits for them, and re-layouts: none -> 60.9 us  [the longest x2 22.7 us: shards(): down_part = down_part.astype(BF16).reshape(parts, units, 2, ny, dpart)]
    all_to_all x0 -> x12, starting transfers between devices: none -> 59.5 us  [the longest x6 30.2 us: to_tokens(): return lax.all_to_all(sent, SEQ, 0, 0, tiled=True)]
    all_to_all x0 -> x12, waiting for transfers between devices: none -> 53.5 us  [the longest x6 27.3 us: to_heads(): got = lax.all_to_all(values, SEQ, 0, 0, tiled=True)]
    transpose x0 -> x8, other arithmetic: none -> 33.1 us  [the longest x1 7.54 us: shards(): down_full = down_all.transpose(2, 3, 0, 1, 4).reshape(parts * units, width)]
    slice x5 -> x12, local copies, waits for them, and re-layouts: 1.81 us -> 32.1 us  [the longest x4 19.8 us: shards(): q, k, v = to_heads(projected[index])]
  transfers between devices with their start and end apart: 32 -> 32, of which waited for: 27 -> 16; matrix products, arithmetic and copies ran while one was open for 12% -> 36% of each run, Pallas kernels for 0% -> 0%
where the time goes in v1:
time: 1020 us; the launch traced here: 1010 us
  waiting for transfers between devices  382 us (37%)
  local copies, waits for them, and re-layouts  270 us (26%)
  matrix products  134 us (13%)
  other arithmetic  103 us (10%)
  starting transfers between devices  62.1 us (6%)
  blocking collectives  46.1 us (5%)
  between operations  16.7 us (2%)
    all_gather x4, waiting for transfers between devices, gather_both(): mine = lax.all_gather(shard, CHIPS, axis=0, tiled=False)  187 us
    unnamed x16, waiting for transfers between devices  69.6 us
    unnamed x290, local copies, waits for them, and re-layouts  64.4 us
    reduce_scatter x4, waiting for transfers between devices, scatter_both(): lax.psum_scatter(mine, 'z', scatter_dimension=0, tiled=False).astype(F32)  52.7 us
    psum x1, blocking collectives, shards(): sums = lax.psum(from_own(sums), ('y', 'c', 'z', 'x'))  40 us
    all_to_all x6, starting transfers between devices, to_tokens(): return lax.all_to_all(sent, SEQ, 0, 0, tiled=True)  30.2 us
    all_to_all x6, starting transfers between devices, to_heads(): got = lax.all_to_all(values, SEQ, 0, 0, tiled=True)  29.3 us
    all_to_all x6, waiting for transfers between devices, to_heads(): got = lax.all_to_all(values, SEQ, 0, 0, tiled=True)  27.3 us
  transfers between devices with their start and end apart: 32, of which 16 were waited for; matrix products, arithmetic and copies ran while one was open for 36% of the time, Pallas kernels for 0%

profile of v1, /device:TPU:0, one launch (start us, length us, event | category | flops | bytes accessed | tf_op | source)
XLA Modules:
  0.0 1014.0 jit_solution(15324913078408496408)
XLA Ops:
  27.6 54.0 %all-gather.9.cloned.1.call-done = bf16[48,256,128]{2,1,0:T(8,128)(2,1)} async-done(((bf16[3,256,128]{2,1,0:T(8,128)(2,1)}), bf16[48,256,128]{2,1,0:T(8,128)(2,1)}) %all-gather.9.cloned.1.call-update) | async-done | bytes 3145744 | tf_op jit(solution)/shard_map/all_gather | solution.py:113
  94.2 16.2 %copy.230 = bf16[2,2,256,3,8,128]{2,1,0,5,4,3:T(2,128)(2,1)} copy(bf16[2,2,256,3,8,128]{5,2,3,4,1,0:T(8,128)(2,1)} %maximum_bitcast_fusion.2) | data formatting | bytes 12582912 | tf_op jit(solution)/shard_map/transpose | solution.py:161
  110.3 11.0 %reshape.954 = bf16[1024,3072]{0,1:T(8,128)(2,1)} reshape(bf16[2,2,256,3,8,128]{2,1,0,5,4,3:T(2,128)(2,1)} %copy.230) | data formatting | bytes 12582912 | tf_op jit(solution)/shard_map/reshape | solution.py:161
  167.5 55.4 %all-gather.15.cloned.1.call-done = bf16[8192,256]{1,0:T(8,128)(2,1)} async-done(((bf16[512,256]{1,0:T(8,128)(2,1)}), bf16[8192,256]{1,0:T(8,128)(2,1)}) %all-gather.15.cloned.1.call-update) | async-done | bytes 4194320 | tf_op jit(solution)/shard_map/all_gather | solution.py:113
  222.8 77.2 %all-gather.13.cloned.1.call-done = bf16[4096,512]{1,0:T(8,128)(2,1)} async-done(((bf16[256,512]{1,0:T(8,128)(2,1)}), bf16[4096,512]{1,0:T(8,128)(2,1)}) %all-gather.13.cloned.1.call-update) | async-done | bytes 4194320 | tf_op jit(solution)/shard_map/all_gather | solution.py:113
  324.4 10.7 %all-to-all-done.2 = bf16[8,3,128,128]{3,2,1,0:T(8,128)(2,1)} async-done(((bf16[8,3,128,128]{3,2,1,0:T(8,128)(2,1)}), bf16[8,3,128,128]{3,2,1,0:T(8,128)(2,1)}, u32[]{:S(2)}, u32[]{:S(2)}) %all-to-all-start.2) | async-done | bytes 786464 | tf_op jit(solution)/shard_map/all_to_all | solution.py:193
  348.3 11.3 %all-to-all-done = bf16[8,3,128,128]{3,2,1,0:T(8,128)(2,1)} async-done(((bf16[8,3,128,128]{3,2,1,0:T(8,128)(2,1)}), bf16[8,3,128,128]{3,2,1,0:T(8,128)(2,1)}, u32[]{:S(2)}, u32[]{:S(2)}) %all-to-all-start) | async-done | bytes 786464 | tf_op jit(solution)/shard_map/all_to_all | solution.py:193
  434.1 14.8 %copy.258 = bf16[8,512,2,2,256]{1,0,4,3,2:T(8,128)(2,1)} copy(bf16[8,512,2,2,256]{4,1,0,3,2:T(8,128)(2,1)} %maximum_bitcast_fusion.1) | data formatting | bytes 16777216 | tf_op jit(solution)/shard_map/transpose | solution.py:164
  449.0 12.3 %copy.320 = bf16[128,8,8,512]{3,1,2,0:T(8,128)(2,1)} copy(bf16[128,8,8,512]{3,2,1,0:T(8,128)(2,1)} %bitcast.434) | data formatting | bytes 16777216
  468.8 11.5 %copy.257 = bf16[2,2,256,8,512]{4,3,2,1,0:T(8,128)(2,1)} copy(bf16[2,2,256,8,512]{4,2,3,1,0:T(8,128)(2,1)} %maximum_bitcast_fusion) | data formatting | bytes 16777216 | tf_op jit(solution)/shard_map/transpose | solution.py:163
  480.3 12.8 %copy.319 = bf16[128,8,8,512]{3,1,2,0:T(8,128)(2,1)} copy(bf16[128,8,8,512]{3,2,1,0:T(8,128)(2,1)} %bitcast.435) | data formatting | bytes 16777216
  493.0 9.2 fusion.125
  502.3 9.4 fusion.144
  651.5 10.8 %all-to-all-done.9 = bf16[8,3,128,128]{2,3,1,0:T(8,128)(2,1)} async-done(((bf16[8,3,128,128]{2,3,1,0:T(8,128)(2,1)}), bf16[8,3,128,128]{2,3,1,0:T(8,128)(2,1)}, u32[]{:S(2)}, u32[]{:S(2)}) %all-to-all-start.9) | async-done | bytes 786464 | tf_op jit(solution)/shard_map/all_to_all | solution.py:201
  724.2 9.3 convolution_convert_fusion.1
  733.5 12.3 %copy.335 = bf16[128,8,8,512]{3,2,1,0:T(8,128)(2,1)} copy(bf16[128,8,8,512]{3,1,2,0:T(8,128)(2,1)} %bitcast.451) | data formatting | bytes 16777216
  745.8 9.9 copy.365
  772.2 10.6 %convolution_convert_fusion = bf16[4096,1024]{1,0:T(8,128)(2,1)} fusion(bf16[384,1024]{1,0:T(8,128)(2,1)S(1)} %copy-done.73, f32[384,4096]{1,0:T(8,128)} %fusion.125), kind=kOutput, calls=%fused_computation.10 | convolution fusion | flops 3239575552 | bytes 15466496 | tf_op jit(solution)/shard_map/tf,td->fd/dot_general | solution.py:226
  782.8 14.5 %reshape.984 = bf16[8,512,2,2,256]{4,3,2,1,0:T(2,128)(2,1)} reshape(bf16[4096,1024]{1,0:T(8,128)(2,1)} %convolution_convert_fusion) | data formatting | bytes 16777216 | tf_op jit(solution)/shard_map/reshape | solution.py:227
  822.2 24.6 %reduce-scatter.29.cloned.1.call-done = bf16[1,4,256,512]{3,2,1,0:T(8,128)(2,1)} async-done(((bf16[4,4,256,512]{3,2,1,0:T(8,128)(2,1)}), bf16[1,4,256,512]{3,2,1,0:T(8,128)(2,1)}) %reduce-scatter.29.cloned.1.call-update) | async-done | bytes 1048592
  861.4 41.1 %reduce-scatter.31.cloned.1.call-done = bf16[1,4,512,256]{3,2,1,0:T(8,128)(2,1)} async-done(((bf16[4,4,512,256]{3,2,1,0:T(8,128)(2,1)}), bf16[1,4,512,256]{3,2,1,0:T(8,128)(2,1)}) %reduce-scatter.31.cloned.1.call-update) | async-done | bytes 1048592
  906.8 40.0 %psum.7 = f32[8,1024]{1,0:T(8,128)S(1)} all-reduce(f32[8,1024]{1,0:T(8,128)S(1)} %reshape.987), channel_id=1, replica_groups=mesh['y'=2,'c'=2,'z'=4,'x'=2] {'y','c','z','x'}, use_global_device_ids=true, to_apply=%region_59.60 | all-reduce | flops 8192 | bytes 65536 | tf_op jit(solution)/shard_map/psum | solution.py:275
  950.7 26.4 %reduce-scatter.21.cloned.1.call-done = bf16[1,256,512]{2,1,0:T(8,128)(2,1)} async-done(((bf16[4,256,512]{2,1,0:T(8,128)(2,1)}), bf16[1,256,512]{2,1,0:T(8,128)(2,1)}) %reduce-scatter.21.cloned.1.call-update) | async-done | bytes 262160 | tf_op jit(solution)/shard_map/reduce_scatter | solution.py:127
  978.9 26.3 %reduce-scatter.23.cloned.1.call-done = bf16[1,512,256]{2,1,0:T(8,128)(2,1)} async-done(((bf16[4,512,256]{2,1,0:T(8,128)(2,1)}), bf16[1,512,256]{2,1,0:T(8,128)(2,1)}) %reduce-scatter.23.cloned.1.call-update) | async-done | bytes 262160 | tf_op jit(solution)/shard_map/reduce_scatter | solution.py:127
  (600 shorter events, 465.9 us)
Async XLA Ops:
  7.2 74.5 %all-gather.9.cloned.1.call-start = ((), (), s32[]{:S(2)}) async-start(), calls=%async_computation.24 | async-start | bytes 3342336 | tf_op jit(solution)/shard_map/all_gather | solution.py:113
  7.9 159.1 %all-gather.11.cloned.1.call-start = ((), (), s32[]{:S(2)}) async-start(), calls=%async_computation.25 | async-start | bytes 1114112 | tf_op jit(solution)/shard_map/all_gather | solution.py:113
  8.7 214.2 %all-gather.15.cloned.1.call-start = ((), (), s32[]{:S(2)}) async-start(), calls=%async_computation.27 | async-start | bytes 4456448 | tf_op jit(solution)/shard_map/all_gather | solution.py:113
  9.4 290.6 %all-gather.13.cloned.1.call-start = ((), (), s32[]{:S(2)}) async-start(), calls=%async_computation.26 | async-start | bytes 4456448 | tf_op jit(solution)/shard_map/all_gather | solution.py:113
  153.2 156.2 %all-to-all-start.4 = ((bf16[8,3,128,128]{3,2,1,0:T(8,128)(2,1)}), bf16[8,3,128,128]{3,2,1,0:T(8,128)(2,1)}, u32[]{:S(2)}, u32[]{:S(2)}) async-start(bf16[8,3,128,128]{3,2,1,0:T(8,128)(2,1)} %bitcast.34), calls=%async_computation.4 | async-start | bytes 1572864 | tf_op jit(solution)/shard_map/all_to_all | solution.py:193
  167.0 240.8 %collective-permute-start.1 = (bf16[16,128,256]{2,1,0:T(8,128)(2,1)}, bf16[16,128,256]{2,1,0:T(8,128)(2,1)}, u32[]{:S(2)}, u32[]{:S(2)}) collective-permute-start(bf16[16,128,256]{2,1,0:T(8,128)(2,1)} %bitcast.501), channel_id=1, source_target_pairs={{0,8},{8,0},{1,9},{9,1},{2,10},{10,2},{3,11},{11,3},{4,12},{12,4},... | collective-permute-start | bytes 3145736 | tf_op jit(solution)/shard_map/ppermute | solution.py:114
  222.8 203.7 %collective-permute-start.3 = (bf16[16,512,256]{2,1,0:T(8,128)(2,1)}, bf16[16,512,256]{2,1,0:T(8,128)(2,1)}, u32[]{:S(2)}, u32[]{:S(2)}) collective-permute-start(bf16[16,512,256]{2,1,0:T(8,128)(2,1)} %bitcast.459), channel_id=1, source_target_pairs={{0,8},{8,0},{1,9},{9,1},{2,10},{10,2},{3,11},{11,3},{4,12},{12,4},... | collective-permute-start | bytes 12582920 | tf_op jit(solution)/shard_map/ppermute | solution.py:114
  300.0 161.2 %collective-permute-start.2 = (bf16[16,256,512]{2,1,0:T(8,128)(2,1)}, bf16[16,256,512]{2,1,0:T(8,128)(2,1)}, u32[]{:S(2)}, u32[]{:S(2)}) collective-permute-start(bf16[16,256,512]{2,1,0:T(8,128)(2,1)} %bitcast.457), channel_id=1, source_target_pairs={{0,8},{8,0},{1,9},{9,1},{2,10},{10,2},{3,11},{11,3},{4,12},{12,4},... | collective-permute-start | bytes 12582920 | tf_op jit(solution)/shard_map/ppermute | solution.py:114
  309.3 25.7 %all-to-all-start.2 = ((bf16[8,3,128,128]{3,2,1,0:T(8,128)(2,1)}), bf16[8,3,128,128]{3,2,1,0:T(8,128)(2,1)}, u32[]{:S(2)}, u32[]{:S(2)}) async-start(bf16[8,3,128,128]{3,2,1,0:T(8,128)(2,1)} %bitcast.26), calls=%async_computation.2 | async-start | bytes 1572864 | tf_op jit(solution)/shard_map/all_to_all | solution.py:193
  335.0 24.6 %all-to-all-start = ((bf16[8,3,128,128]{3,2,1,0:T(8,128)(2,1)}), bf16[8,3,128,128]{3,2,1,0:T(8,128)(2,1)}, u32[]{:S(2)}, u32[]{:S(2)}) async-start(bf16[8,3,128,128]{3,2,1,0:T(8,128)(2,1)} %bitcast.18), calls=%async_computation | async-start | bytes 1572864 | tf_op jit(solution)/shard_map/all_to_all | solution.py:193
  359.6 21.7 %all-to-all-start.5 = ((bf16[8,1,128,128]{2,3,1,0:T(8,128)(2,1)}), bf16[8,1,128,128]{2,3,1,0:T(8,128)(2,1)}, u32[]{:S(2)}, u32[]{:S(2)}) async-start(bf16[8,1,128,128]{2,3,1,0:T(8,128)(2,1)} %bitcast.40), calls=%async_computation.5 | async-start | bytes 524288 | tf_op jit(solution)/shard_map/all_to_all | solution.py:201
  395.6 19.5 %all-to-all-start.1 = ((bf16[8,1,128,128]{2,3,1,0:T(8,128)(2,1)}), bf16[8,1,128,128]{2,3,1,0:T(8,128)(2,1)}, u32[]{:S(2)}, u32[]{:S(2)}) async-start(bf16[8,1,128,128]{2,3,1,0:T(8,128)(2,1)} %bitcast.478), calls=%async_computation.1 | async-start | bytes 524288 | tf_op jit(solution)/shard_map/all_to_all | solution.py:201
  577.5 21.8 %all-to-all-start.6 = ((bf16[8,1,128,128]{2,3,1,0:T(8,128)(2,1)}), bf16[8,1,128,128]{2,3,1,0:T(8,128)(2,1)}, u32[]{:S(2)}, u32[]{:S(2)}) async-start(bf16[8,1,128,128]{2,3,1,0:T(8,128)(2,1)} %get-tuple-element.55), calls=%async_computation.6 | async-start | bytes 524288 | tf_op jit(solution)/shard_map/all_to_all | solution.py:193
  615.0 25.2 %all-to-all-start.11 = ((bf16[8,3,128,128]{2,3,1,0:T(8,128)(2,1)}), bf16[8,3,128,128]{2,3,1,0:T(8,128)(2,1)}, u32[]{:S(2)}, u32[]{:S(2)}) async-start(bf16[8,3,128,128]{2,3,1,0:T(8,128)(2,1)} %bitcast.464), calls=%async_computation.11 | async-start | bytes 1572864 | tf_op jit(solution)/shard_map/all_to_all | solution.py:201
  640.2 22.1 %all-to-all-start.9 = ((bf16[8,3,128,128]{2,3,1,0:T(8,128)(2,1)}), bf16[8,3,128,128]{2,3,1,0:T(8,128)(2,1)}, u32[]{:S(2)}, u32[]{:S(2)}) async-start(bf16[8,3,128,128]{2,3,1,0:T(8,128)(2,1)} %bitcast.465), calls=%async_computation.9 | async-start | bytes 1572864 | tf_op jit(solution)/shard_map/all_to_all | solution.py:201
  662.3 21.8 %all-to-all-start.7 = ((bf16[8,3,128,128]{2,3,1,0:T(8,128)(2,1)}), bf16[8,3,128,128]{2,3,1,0:T(8,128)(2,1)S(1)}, u32[]{:S(2)}, u32[]{:S(2)}) async-start(bf16[8,3,128,128]{2,3,1,0:T(8,128)(2,1)} %bitcast.63), calls=%async_computation.7 | async-start | bytes 1572864 | tf_op jit(solution)/shard_map/all_to_all | solution.py:201
  665.9 155.0 %reduce-scatter.27.cloned.1.call-start = ((), (), s32[]{:S(2)}) async-start(), calls=%async_computation.29 | async-start | bytes 1310720
  716.9 104.8 %reduce-scatter.25.cloned.1.call-start = ((), (), s32[]{:S(2)}) async-start(), calls=%async_computation.28 | async-start | bytes 3932160
  722.8 124.1 %reduce-scatter.29.cloned.1.call-start = ((), (), s32[]{:S(2)}) async-start(), calls=%async_computation.30 | async-start | bytes 5242880
  771.1 131.4 %reduce-scatter.31.cloned.1.call-start = ((), (), s32[]{:S(2)}) async-start(), calls=%async_computation.31 | async-start | bytes 5242880
  820.8 126.6 %reduce-scatter.19.cloned.1.call-start = ((), (), s32[]{:S(2)}) async-start(), calls=%async_computation.21 | async-start | bytes 327680 | tf_op jit(solution)/shard_map/reduce_scatter | solution.py:127
  821.6 127.4 %reduce-scatter.17.cloned.1.call-start = ((), (), s32[]{:S(2)}) async-start(), calls=%async_computation.20 | async-start | bytes 983040 | tf_op jit(solution)/shard_map/reduce_scatter | solution.py:127
  822.2 154.9 %reduce-scatter.21.cloned.1.call-start = ((), (), s32[]{:S(2)}) async-start(), calls=%async_computation.22 | async-start | bytes 1310720 | tf_op jit(solution)/shard_map/reduce_scatter | solution.py:127
  846.9 158.3 %reduce-scatter.23.cloned.1.call-start = ((), (), s32[]{:S(2)}) async-start(), calls=%async_computation.23 | async-start | bytes 1310720 | tf_op jit(solution)/shard_map/reduce_scatter | solution.py:127
  (137 other events, 1802.8 us)
Sparse Core Ops, SparseCore 0:
  10.8 70.8 all-gather.8
  84.4 53.8 all-gather.10
  141.1 81.6 all-gather.14
  225.5 74.4 all-gather.12
  717.0 26.7 reduce-scatter.26
  746.9 43.9 reduce-scatter.24
  794.1 52.6 reduce-scatter.28
  849.8 52.6 reduce-scatter.30
  904.9 19.6 reduce-scatter.18
  926.7 21.6 reduce-scatter.16
  950.6 26.4 reduce-scatter.20
  979.3 25.7 reduce-scatter.22

commit v2 on v1

--- a/solution.py
+++ b/solution.py
@@ -3,6 +3,8 @@
 import jax
 import jax.numpy as jnp
 from jax import lax
+from jax.experimental import pallas as pl
+from jax.experimental.pallas import tpu as pltpu
 from jax.sharding import Mesh, PartitionSpec as P
 
 HD = 64
@@ -292,6 +294,726 @@
     return full
 
 
+NT = (((1,), (1,)), ((), ()))
+GELU_A = 0.7978845608
+GELU_B = 0.044715
+
+
+def dot(a, b):
+    return jnp.dot(a, b, preferred_element_type=F32)
+
+
+def dot_nt(a, b):
+    return lax.dot_general(a, b, NT, preferred_element_type=F32)
+
+
+def params(semantics=1):
+    return pltpu.CompilerParams(
+        dimension_semantics=("arbitrary",) * semantics, vmem_limit_bytes=60 * 1024 * 1024
+    )
+
+
+def cost(flops, size, transcendentals=0):
+    return pl.CostEstimate(
+        flops=int(flops), bytes_accessed=int(size), transcendentals=int(transcendentals)
+    )
+
+
+def whole(shape):
+    return pl.BlockSpec(shape, lambda *_: (0,) * len(shape))
+
+
+def swap_halves(values):
+    lane = lax.broadcasted_iota(jnp.int32, values.shape, 1)
+    low = lax.rem(lane, HD) < HD // 2
+    return jnp.where(low, pltpu.roll(values, 96, 1), pltpu.roll(values, 32, 1))
+
+
+def row_stats(values):
+    average = jnp.mean(values, axis=-1, keepdims=True)
+    centred = values - average
+    variance = jnp.mean(centred * centred, axis=-1, keepdims=True)
+    scale = lax.rsqrt(variance + EPSILON)
+    return centred * scale, scale
+
+
+def row_pull(grad, xhat, scale, gain):
+    e = grad * gain
+    return scale * (
+        e - jnp.mean(e, axis=-1, keepdims=True) - xhat * jnp.mean(e * xhat, axis=-1, keepdims=True)
+    )
+
+
+def column_sum(values):
+    return jnp.sum(values, axis=0, keepdims=True)
+
+
+def store_columns(ref, values, pos, part):
+    for dc in range(2):
+        for dy in range(2):
+            place = (lax.bitwise_xor(pos[0], dy) * 2 + lax.bitwise_xor(pos[1], dc)) * part
+            place = pl.multiple_of(place, part)
+            col = (dc * 2 + dy) * part
+            ref[:, pl.ds(place, part)] = values[:, col : col + part].astype(ref.dtype)
+
+
+def proj_kernel(pos, x, gains, shifts, cos, sin, *refs):
+    weights = [refs[2 * q : 2 * q + 2] for q in range(4)]
+    outs, normed = refs[8:11], refs[11]
+    part = weights[0][0].shape[2]
+    count = outs[0].shape[3]
+
+    @pl.when(pl.program_id(0) == 0)
+    def _():
+        xhat, _ = row_stats(x[...].astype(F32))
+        normed[...] = (xhat * gains[0:1] + shifts[0:1]).astype(BF16)
+
+    total = None
+    for q in range(4):
+        block = jnp.concatenate([weights[q][dx][0, kind] for dx in range(2) for kind in range(3)], 1)
+        term = dot(normed[:, q * part : (q + 1) * part], block)
+        total = term if total is None else total + term
+    for dx in range(2):
+        place = lax.bitwise_xor(pos[3], dx)
+        for kind in range(3):
+            at = (dx * 3 + kind) * 128
+            u = total[:, at : at + 128]
+            if kind < 2:
+                u = u * cos[...] + swap_halves(u) * sin[...]
+            u = u.astype(BF16)
+            for m in range(3):
+                outs[m][0, place, kind] = u[m * count : (m + 1) * count]
+
+
+def ring_index(nz):
+    return lambda i, pos: (lax.rem(pos[2] + i, nz), 0, 0, 0, 0)
+
+
+def call_proj(pos, x, gains, shifts, cos, sin, pieces, shard_len):
+    tokens, width = x.shape
+    nz, _, part, cols = pieces[0][0].shape
+    piece = pl.BlockSpec((1, 3, part, cols), lambda i, pos: (i, 0, 0, 0))
+    out = pl.BlockSpec((1, 2, 3, shard_len, cols), ring_index(nz))
+    out_shape = jax.ShapeDtypeStruct((nz, 2, 3, shard_len, cols), BF16)
+    return pl.pallas_call(
+        proj_kernel,
+        grid_spec=pltpu.PrefetchScalarGridSpec(
+            num_scalar_prefetch=1,
+            grid=(nz,),
+            in_specs=[whole(a.shape) for a in (x, gains, shifts, cos, sin)] + [piece] * 8,
+            out_specs=[out] * 3 + [whole((tokens, width))],
+        ),
+        out_shape=[out_shape] * 3 + [jax.ShapeDtypeStruct((tokens, width), BF16)],
+        compiler_params=params(),
+        cost_estimate=cost(2 * tokens * width * 3 * nz * 2 * cols, 12e6),
+        name="project",
+    )(pos, x, gains, shifts, cos, sin, *[p for pair in pieces for p in pair])
+
+
+def head_mask(shape, head):
+    lane = lax.broadcasted_iota(jnp.int32, shape, 1)
+    return (lane < HD) if head == 0 else (lane >= HD)
+
+
+def attend_kernel(begins, got, out, lse_out):
+    shards_n, _, count, lanes = got.shape
+    seq_len = shards_n * count
+    block = min(256, seq_len)
+    q_all = (got[:, 0] * 0.125).reshape(seq_len, lanes)
+    k_all = got[:, 1].reshape(seq_len, lanes)
+    v_all = got[:, 2].reshape(seq_len, lanes)
+    per = block // count
+    for start in range(0, seq_len, block):
+        end = start + block
+        qb = q_all[start:end]
+        key = lax.broadcasted_iota(jnp.int32, (block, end), 1)
+        query = start + lax.broadcasted_iota(jnp.int32, (block, end), 0)
+        allowed = (key <= query) & (key >= begins[start:end, 0:1])
+        results = []
+        for head in range(2):
+            mask = head_mask(qb.shape, head)
+            scores = dot_nt(jnp.where(mask, qb, 0), k_all[:end])
+            scores = jnp.where(allowed, scores, -1e30)
+            peak = jnp.max(scores, axis=-1, keepdims=True)
+            e = jnp.exp(scores - peak)
+            total = jnp.sum(e, axis=-1, keepdims=True)
+            results.append(dot(e.astype(BF16), v_all[:end]) / total)
+            lse = jnp.broadcast_to(peak + jnp.log(total), (block, 128))
+            lse_out[head : head + 1, start:end] = jnp.transpose(lse)[0:1]
+        mixed = jnp.where(head_mask(results[0].shape, 0), results[0], results[1]).astype(BF16)
+        out[start // count : end // count] = mixed.reshape(per, count, lanes)
+
+
+def call_attend(begins, got):
+    parts, _, count, lanes = got.shape
+    seq_len = parts * count
+    return pl.pallas_call(
+        attend_kernel,
+        out_shape=[
+            jax.ShapeDtypeStruct((parts, count, lanes), BF16),
+            jax.ShapeDtypeStruct((8, seq_len), F32),
+        ],
+        compiler_params=params(0),
+        cost_estimate=cost(4 * 2 * seq_len * seq_len * lanes, 2e6, 2 * seq_len * seq_len),
+        name="attend",
+    )(begins, got)
+
+
+def attend_back_kernel(begins, cos, sin, got, grad, att, lse, out, dq_ref, dk_ref, dv_ref):
+    shards_n, _, count, lanes = got.shape
+    seq_len = shards_n * count
+    block = min(256, seq_len)
+    q_all = (got[:, 0] * 0.125).reshape(seq_len, lanes)
+    k_all = got[:, 1].reshape(seq_len, lanes)
+    v_all = got[:, 2].reshape(seq_len, lanes)
+    do_all = grad[...].reshape(seq_len, lanes)
+    prod = do_all.astype(F32) * att[...].reshape(seq_len, lanes).astype(F32)
+    prod = jnp.transpose(prod)
+    deltas = [
+        jnp.sum(prod[:HD], axis=0, keepdims=True),
+        jnp.sum(prod[HD:], axis=0, keepdims=True),
+    ]
+    for start in range(0, seq_len, block):
+        end = start + block
+        kb, vb = k_all[start:end], v_all[start:end]
+        qs, dos = q_all[start:], do_all[start:]
+        span = seq_len - start
+        key = start + lax.broadcasted_iota(jnp.int32, (block, span), 0)
+        query = start + lax.broadcasted_iota(jnp.int32, (block, span), 1)
+        allowed = (key <= query) & (key >= begins[0:1, start:])
+        dks, dvs, dqs = [], [], []
+        for head in range(2):
+            mask = head_mask(kb.shape, head)
+            scores = dot_nt(jnp.where(mask, kb, 0), qs)
+            soft = jnp.exp(jnp.where(allowed, scores, -1e30) - lse[head : head + 1, start:])
+            pull = dot_nt(jnp.where(mask, vb, 0), dos)
+            ds = (soft * (pull - deltas[head][:, start:])).astype(BF16)
+            dvs.append(dot(soft.astype(BF16), dos))
+            dks.append(dot(ds, qs))
+            dqs.append(
+                lax.dot_general(ds, kb, (((0,), (0,)), ((), ())), preferred_element_type=F32)
+            )
+        low = head_mask(kb.shape, 0)
+        dk_ref[start:end] = jnp.where(low, dks[0], dks[1])
+        dv_ref[start:end] = jnp.where(low, dvs[0], dvs[1])
+        dq = jnp.where(head_mask(dqs[0].shape, 0), dqs[0], dqs[1])
+        if start == 0:
+            dq_ref[...] = dq
+        else:
+            dq_ref[start:] += dq
+    for kind, ref in enumerate((dq_ref, dk_ref, dv_ref)):
+        u = ref[...]
+        if kind == 0:
+            u = u * 0.125
+        if kind < 2:
+            u = u * cos[...] - swap_halves(u) * sin[...]
+        out[:, kind] = u.astype(BF16).reshape(shards_n, count, lanes)
+
+
+def call_attend_back(begins, cos, sin, got, grad, att, lse):
+    parts, _, count, lanes = got.shape
+    seq_len = parts * count
+    return pl.pallas_call(
+        attend_back_kernel,
+        out_shape=jax.ShapeDtypeStruct((parts, 3, count, lanes), BF16),
+        scratch_shapes=[pltpu.VMEM((seq_len, lanes), F32)] * 3,
+        compiler_params=params(0),
+        cost_estimate=cost(10 * 2 * seq_len * seq_len * lanes, 4e6, 2 * seq_len * seq_len),
+        name="attend_back",
+    )(begins, cos, sin, got, grad, att, lse)
+
+
+def layer_kernel(pos, *refs):
+    att = refs[0:3]
+    x, cot, gains, shifts = refs[3:7]
+    ups = [refs[7 + 2 * q : 9 + 2 * q] for q in range(4)]
+    downs = [refs[15 + 2 * q : 17 + 2 * q] for q in range(4)]
+    mixes = [refs[23 + 2 * q : 25 + 2 * q] for q in range(4)]
+    outputs, att_all, normed, act, g_up, g_b2, g_b1, g_hidden = refs[31:39]
+    g_att = refs[39:42]
+    sums = refs[42]
+    slope, xhat1, scale1, xhat2, scale2, hidden, total = refs[43:50]
+    nz = mixes[0][0].shape[0]
+    count = att[0].shape[1]
+    part = downs[0][0].shape[2]
+    step = pl.program_id(0)
+
+    def mix_block(q, zk):
+        return jnp.concatenate([mixes[q][0][zk], mixes[q][1][zk]], 0)
+
+    @pl.when(step == 0)
+    def _():
+        for zk in range(nz):
+            for dx in range(2):
+                place = zk * 2 + lax.bitwise_xor(pos[3], dx)
+                for m in range(3):
+                    at = (zk * 2 + dx) * 128
+                    att_all[m * count : (m + 1) * count, at : at + 128] = att[m][place]
+        for q in range(4):
+            acc = None
+            for zk in range(nz):
+                term = dot(att_all[:, zk * 256 : (zk + 1) * 256], mix_block(q, zk))
+                acc = term if acc is None else acc + term
+            total[:, q * part : (q + 1) * part] = acc
+        xhat, scale = row_stats(total[...])
+        xhat1[...] = xhat
+        scale1[...] = jnp.broadcast_to(scale, scale1.shape)
+        value = x[...].astype(F32) + xhat * gains[1:2] + shifts[1:2]
+        hidden[...] = value
+        xhat, scale = row_stats(value)
+        xhat2[...] = xhat
+        scale2[...] = jnp.broadcast_to(scale, scale2.shape)
+        normed[...] = (xhat * gains[2:3] + shifts[2:3]).astype(BF16)
+
+    @pl.when(step < nz)
+    def _():
+        zk = step
+        for dx in range(2):
+            u = None
+            for q in range(4):
+                term = dot(normed[:, q * part : (q + 1) * part], ups[q][dx][0])
+                u = term if u is None else u + term
+            square = u * u
+            t = jnp.tanh(GELU_A * (u * (1.0 + GELU_B * square)))
+            half = 0.5 * (1.0 + t)
+            act[0, dx] = (u * half).astype(BF16)
+            slope[zk, dx] = half + (0.5 * GELU_A) * u * (1.0 - t * t) * (1.0 + 3.0 * GELU_B * square)
+        for q in range(4):
+            term = dot(act[0, 0], downs[q][0][0]) + dot(act[0, 1], downs[q][1][0])
+
+            @pl.when(step == 0)
+            def _():
+                total[:, q * part : (q + 1) * part] = term
+
+            @pl.when(step > 0)
+            def _():
+                total[:, q * part : (q + 1) * part] += term
+
+    @pl.when(step == nz)
+    def _():
+        xhat, scale = row_stats(total[...])
+        value = hidden[...] + xhat * gains[3:4] + shifts[3:4]
+        store_columns(outputs, value, pos, part)
+        grad = cot[...].astype(F32)
+        sums[2:3] = column_sum(grad * xhat)
+        sums[5:6] = column_sum(grad)
+        g_b2[...] = row_pull(grad, xhat, scale, gains[3:4]).astype(BF16)
+
+    @pl.when(step >= nz)
+    def _():
+        zk = 2 * nz - 1 - step
+        for dx in range(2):
+            g = None
+            for q in range(4):
+                term = dot_nt(g_b2[:, q * part : (q + 1) * part], downs[q][dx][0])
+                g = term if g is None else g + term
+            g_up[0, dx] = (g * slope[zk, dx]).astype(BF16)
+        for q in range(4):
+            term = dot_nt(g_up[0, 0], ups[q][0][0]) + dot_nt(g_up[0, 1], ups[q][1][0])
+
+            @pl.when(step == nz)
+            def _():
+                total[:, q * part : (q + 1) * part] = term
+
+            @pl.when(step > nz)
+            def _():
+                total[:, q * part : (q + 1) * part] += term
+
+    @pl.when(step == 2 * nz - 1)
+    def _():
+        grad = total[...]
+        xhat = xhat2[...]
+        sums[1:2] = column_sum(grad * xhat)
+        sums[4:5] = column_sum(grad)
+        grad = cot[...].astype(F32) + row_pull(grad, xhat, scale2[:, 0:1], gains[2:3])
+        g_hidden[...] = grad
+        xhat = xhat1[...]
+        sums[0:1] = column_sum(grad * xhat)
+        sums[3:4] = column_sum(grad)
+        g_b1[...] = row_pull(grad, xhat, scale1[:, 0:1], gains[1:2]).astype(BF16)
+        for zk in range(nz):
+            acc = None
+            for q in range(4):
+                term = dot_nt(g_b1[:, q * part : (q + 1) * part], mix_block(q, zk))
+                acc = term if acc is None else acc + term
+            acc = acc.astype(BF16)
+            for dx in range(2):
+                place = zk * 2 + lax.bitwise_xor(pos[3], dx)
+                for m in range(3):
+                    g_att[m][place] = acc[m * count : (m + 1) * count, dx * 128 : (dx + 1) * 128]
+
+
+def call_layer(pos, att, x, cot, gains, shifts, ups, mixes):
+    tokens, width = x.shape
+    nz, part, units = ups[0][0].shape
+    rows = mixes[0][0].shape[1] - units
+    parts, count, cols = att[0].shape
+    turn = 2 * nz - 1
+
+    def weight_index(i, pos):
+        return (jnp.minimum(i, turn - i), 0, 0)
+
+    up = pl.BlockSpec((1, part, units), weight_index)
+    down = pl.BlockSpec((1, units, part), weight_index)
+    mix = pl.BlockSpec((nz, rows, part), lambda i, pos: (0, units // rows, 0))
+    act = pl.BlockSpec((1, 2, tokens, units), lambda i, pos: (jnp.minimum(i, nz - 1), 0, 0, 0))
+    g_up = pl.BlockSpec((1, 2, tokens, units), lambda i, pos: (jnp.minimum(turn - i, nz - 1), 0, 0, 0))
+    flat = (tokens, width)
+    ffn = jax.ShapeDtypeStruct((nz, 2, tokens, units), BF16)
+    low = jax.ShapeDtypeStruct(flat, BF16)
+    ups_flat = [p for pair in ups for p in pair]
+    mixes_flat = [p for pair in mixes for p in pair]
+    return pl.pallas_call(
+        layer_kernel,
+        grid_spec=pltpu.PrefetchScalarGridSpec(
+            num_scalar_prefetch=1,
+            grid=(2 * nz,),
+            in_specs=[whole(a.shape) for a in (*att, x, cot, gains, shifts)]
+            + [up] * 8
+            + [down] * 8
+            + [mix] * 8,
+            out_specs=[whole(flat)] * 3
+            + [act, g_up]
+            + [whole(flat)] * 3
+            + [whole(att[0].shape)] * 3
+            + [whole((8, width))],
+            scratch_shapes=[
+                pltpu.VMEM((nz, 2, tokens, units), F32),
+                pltpu.VMEM(flat, F32),
+                pltpu.VMEM((tokens, 128), F32),
+                pltpu.VMEM(flat, F32),
+                pltpu.VMEM((tokens, 128), F32),
+                pltpu.VMEM(flat, F32),
+                pltpu.VMEM(flat, F32),
+            ],
+        ),
+        out_shape=[low, low, low, ffn, ffn, low, low, jax.ShapeDtypeStruct(flat, F32)]
+        + [jax.ShapeDtypeStruct(att[0].shape, BF16)] * 3
+        + [jax.ShapeDtypeStruct((8, width), F32)],
+        compiler_params=params(),
+        cost_estimate=cost(
+            2 * tokens * width * (4 * nz * 2 * units + 2 * width), 60e6, tokens * nz * 2 * units
+        ),
+        name="layer",
+    )(pos, *att, x, cot, gains, shifts, *ups_flat, *mixes_flat, *mixes_flat)
+
+
+def weight_grad_kernel(act, g_up, normed, g_b2, att_all, g_b1, *refs):
+    ups = [refs[2 * q : 2 * q + 2] for q in range(4)]
+    mixes = [refs[8 + 2 * q : 10 + 2 * q] for q in range(4)]
+    flipped = refs[16]
+    part, units = ups[0][0].shape[1:]
+
+    @pl.when(pl.program_id(0) == 0)
+    def _():
+        flipped[...] = jnp.transpose(normed[...])
+
+    for dx in range(2):
+        side = jnp.transpose(act[0, dx])
+        for q in range(4):
+            cols = slice(q * part, (q + 1) * part)
+            mixes[q][dx][0, :units] = dot(side, g_b2[:, cols]).astype(BF16)
+            ups[q][dx][0] = dot(flipped[cols], g_up[0, dx]).astype(BF16)
+    side = jnp.transpose(att_all[...])
+    for q in range(4):
+        both = dot(side, g_b1[:, q * part : (q + 1) * part]).astype(BF16)
+        for dx in range(2):
+            mixes[q][dx][0, units:] = both[dx * 128 : (dx + 1) * 128]
+
+
+def call_weight_grad(act, g_up, normed, g_b2, att_all, g_b1):
+    nz, _, tokens, units = act.shape
+    width = normed.shape[1]
+    part = width // 4
+    rows = width // (2 * nz)
+    ffn = pl.BlockSpec((1, 2, tokens, units), lambda i: (i, 0, 0, 0))
+    heads = pl.BlockSpec((tokens, 2 * rows), lambda i: (0, i))
+    up = pl.BlockSpec((1, part, units), lambda i: (i, 0, 0))
+    mix = pl.BlockSpec((1, units + rows, part), lambda i: (i, 0, 0))
+    flat = whole((tokens, width))
+    res = pl.pallas_call(
+        weight_grad_kernel,
+        grid=(nz,),
+        in_specs=[ffn, ffn, flat, flat, heads, flat],
+        out_specs=[up] * 8 + [mix] * 8,
+        out_shape=[jax.ShapeDtypeStruct((nz, part, units), BF16)] * 8
+        + [jax.ShapeDtypeStruct((nz, units + rows, part), BF16)] * 8,
+        scratch_shapes=[pltpu.VMEM((width, tokens), BF16)],
+        compiler_params=params(),
+        cost_estimate=cost(2 * tokens * width * (2 * nz * 2 * units + width), 40e6),
+        name="weight_grad",
+    )(act, g_up, normed, g_b2, att_all, g_b1)
+    return [res[2 * q : 2 * q + 2] for q in range(4)], [res[8 + 2 * q : 10 + 2 * q] for q in range(4)]
+
+
+def load_grads(pos, grads):
+    columns = []
+    for dx in range(2):
+        place = lax.bitwise_xor(pos[3], dx)
+        for kind in range(3):
+            columns.append(jnp.concatenate([g[0, place, kind] for g in grads], 0))
+    return jnp.concatenate(columns, 1)
+
+
+def qkv_grad_kernel(pos, *refs):
+    grads, normed = refs[0:3], refs[3]
+    outs = [refs[4 + 2 * q : 6 + 2 * q] for q in range(4)]
+    flipped = refs[12]
+    part = outs[0][0].shape[2]
+
+    @pl.when(pl.program_id(0) == 0)
+    def _():
+        flipped[...] = jnp.transpose(normed[...])
+
+    block = load_grads(pos, grads)
+    for q in range(4):
+        res = dot(flipped[q * part : (q + 1) * part], block).astype(BF16)
+        for dx in range(2):
+            for kind in range(3):
+                at = (dx * 3 + kind) * 128
+                outs[q][dx][0, kind] = res[:, at : at + 128]
+
+
+def call_qkv_grad(pos, grads, normed):
+    nz, _, _, count, cols = grads[0].shape
+    tokens, width = normed.shape
+    part = width // 4
+    grad = pl.BlockSpec((1, 2, 3, count, cols), ring_index(nz))
+    piece = pl.BlockSpec((1, 3, part, cols), lambda i, pos: (i, 0, 0, 0))
+    res = pl.pallas_call(
+        qkv_grad_kernel,
+        grid_spec=pltpu.PrefetchScalarGridSpec(
+            num_scalar_prefetch=1,
+            grid=(nz,),
+            in_specs=[grad] * 3 + [whole(normed.shape)],
+            out_specs=[piece] * 8,
+            scratch_shapes=[pltpu.VMEM((width, tokens), BF16)],
+        ),
+        out_shape=[jax.ShapeDtypeStruct((nz, 3, part, cols), BF16)] * 8,
+        compiler_params=params(),
+        cost_estimate=cost(2 * tokens * width * 3 * nz * 2 * cols, 12e6),
+        name="qkv_grad",
+    )(pos, *grads, normed)
+    return [res[2 * q : 2 * q + 2] for q in range(4)]
+
+
+def input_grad_kernel(pos, *refs):
+    grads, x, gains, g_hidden = refs[0:3], refs[3], refs[4], refs[5]
+    weights = [refs[6 + 2 * q : 8 + 2 * q] for q in range(4)]
+    out, sums, total = refs[14], refs[15], refs[16]
+    part = weights[0][0].shape[2]
+    step = pl.program_id(0)
+    block = load_grads(pos, grads)
+    for q in range(4):
+        side = jnp.concatenate([weights[q][dx][0, kind] for dx in range(2) for kind in range(3)], 1)
+        term = dot_nt(block, side)
+
+        @pl.when(step == 0)
+        def _():
+            total[:, q * part : (q + 1) * part] = term
+
+        @pl.when(step > 0)
+        def _():
+            total[:, q * part : (q + 1) * part] += term
+
+    @pl.when(step == pl.num_programs(0) - 1)
+    def _():
+        grad = total[...]
+        xhat, scale = row_stats(x[...].astype(F32))
+        sums[0:1] = column_sum(grad * xhat)
+        sums[1:2] = column_sum(grad)
+        value = g_hidden[...] + row_pull(grad, xhat, scale, gains[0:1])
+        store_columns(out, value, pos, part)
+
+
+def call_input_grad(pos, grads, x, gains, g_hidden, pieces):
+    nz, _, _, count, cols = grads[0].shape
+    tokens, width = x.shape
+    part = width // 4
+    grad = pl.BlockSpec((1, 2, 3, count, cols), ring_index(nz))
+    piece = pl.BlockSpec((1, 3, part, cols), lambda i, pos: (i, 0, 0, 0))
+    return pl.pallas_call(
+        input_grad_kernel,
+        grid_spec=pltpu.PrefetchScalarGridSpec(
+            num_scalar_prefetch=1,
+            grid=(nz,),
+            in_specs=[grad] * 3 + [whole(a.shape) for a in (x, gains, g_hidden)] + [piece] * 8,
+            out_specs=[whole((tokens, width)), whole((8, width))],
+            scratch_shapes=[pltpu.VMEM((tokens, width), F32)],
+        ),
+        out_shape=[
+            jax.ShapeDtypeStruct((tokens, width), F32),
+            jax.ShapeDtypeStruct((8, width), F32),
+        ],
+        compiler_params=params(),
+        cost_estimate=cost(2 * tokens * width * 3 * nz * 2 * cols, 16e6),
+        name="input_grad",
+    )(pos, *grads, x, gains, g_hidden, *[p for pair in pieces for p in pair])
+
+
+def swap(values, axis):
+    return lax.ppermute(values, axis, SWAP)
+
+
+def ring(values, step, size):
+    return lax.ppermute(values, "z", [(i, (i + step) % size) for i in range(size)])
+
+
+def spread(mine, via):
+    over_x, over_y = swap(mine, "x"), swap(mine, "y")
+    if via == "x":
+        both = swap(over_y, "x")
+    elif via == "y":
+        both = swap(over_x, "y")
+    else:
+        half = mine.shape[0] // 2
+        both = jnp.concatenate([swap(over_x[:half], "y"), swap(over_y[half:], "x")])
+    own = [[mine, over_x], [over_y, both]]
+    other = [[swap(p, "c") for p in pair] for pair in own]
+    return own + other
+
+
+def add(*values):
+    total = values[0].astype(F32)
+    for value in values[1:]:
+        total = total + value.astype(F32)
+    return total.astype(BF16)
+
+
+def collect(pieces, via):
+    own = [[add(pieces[dy][dx], swap(pieces[2 + dy][dx], "c")) for dx in range(2)] for dy in range(2)]
+    (mine, over_x), (over_y, both) = own
+    if via == "x":
+        over_y = add(over_y, swap(both, "x"))
+    elif via == "y":
+        over_x = add(over_x, swap(both, "y"))
+    else:
+        half = mine.shape[0] // 2
+        first, second = swap(both[:half], "y"), swap(both[half:], "x")
+        over_x = jnp.concatenate([add(over_x[:half], first), over_x[half:]])
+        over_y = jnp.concatenate([over_y[:half], add(over_y[half:], second)])
+    return add(mine, swap(over_x, "x"), swap(over_y, "y"))
+
+
+def total_norms(sums, part):
+    pieces = [sums[:, q * part : (q + 1) * part] for q in range(4)]
+    low, high = (pieces[dy] + swap(pieces[2 + dy], "c") for dy in range(2))
+    mine = low + swap(high, "y")
+    mine = mine + swap(mine, "x")
+    mine = mine + lax.ppermute(mine, "z", [(i, i ^ 1) for i in range(4)])
+    return mine + lax.ppermute(mine, "z", [(i, i ^ 2) for i in range(4)])
+
+
+def fast_shards(inputs, doc_starts, w_qkv, w_out, w_up, w_down, norm_gains, norm_biases, cotangent):
+    y, c, z, x_at = (lax.axis_index(name) for name in ("y", "c", "z", "x"))
+    pos = jnp.stack([y, c, z, x_at]).astype(jnp.int32)
+    nz = lax.axis_size("z")
+    parts = nz * 2
+    micro, _, shard_len, width = inputs.shape
+    tokens = micro * shard_len
+    seq_len = shard_len * parts
+    part = width // 4
+    cols = w_qkv.shape[2]
+
+    qkv_mine = jnp.stack([w_qkv] + [ring(w_qkv, nz - k, nz) for k in range(1, nz)])
+    qkv = spread(qkv_mine, "both")
+    mix_mine = lax.all_gather(jnp.concatenate([w_down, w_out]), "z", axis=0, tiled=False)
+    up_mine = lax.all_gather(w_up, "z", axis=0, tiled=False)
+    mixes = spread(mix_mine, "y")
+    ups = spread(up_mine, "x")
+
+    def to_own(values):
+        pieces = values.reshape(values.shape[:-1] + (2, 2, part))
+        pieces = jnp.where(y == 1, pieces[..., ::-1, :, :], pieces)
+        pieces = jnp.where(c == 1, pieces[..., ::-1, :], pieces)
+        return jnp.swapaxes(pieces, -3, -2).reshape(values.shape)
+
+    norms = lax.all_gather(jnp.concatenate([norm_gains, norm_biases]), ("y", "c"), axis=1, tiled=True)
+    norms = to_own(norms).astype(F32)
+    gains, shifts = norms[:4], norms[4:]
+    x = to_own(inputs.reshape(tokens, width))
+    cot = to_own(cotangent.reshape(tokens, width))
+
+    row = jnp.arange(seq_len, dtype=jnp.int32)
+    begins, cosines, sines = [], [], []
+    for index in range(micro):
+        starts = doc_starts[index, 0]
+        begin = jnp.max(jnp.where(row[:, None] >= starts[None, :], starts[None, :], 0), axis=1)
+        begins.append(begin)
+        cosine, sine = angles_of(row - begin)
+        cosines.append(jnp.concatenate([cosine, cosine, cosine, cosine], 1))
+        sines.append(jnp.concatenate([-sine, sine, -sine, sine], 1))
+    place = (z * 2 + x_at) * shard_len
+    cos_own = jnp.concatenate([lax.dynamic_slice_in_dim(t, place, shard_len) for t in cosines])
+    sin_own = jnp.concatenate([lax.dynamic_slice_in_dim(t, place, shard_len) for t in sines])
+
+    *projected, normed1 = call_proj(pos, x, gains, shifts, cos_own, sin_own, qkv, shard_len)
+
+    def exchange(values):
+        return lax.all_to_all(values, SEQ, 0, 0, tiled=True)
+
+    got, lses, att, att_local = [], [], [], []
+    for index in range(micro):
+        got.append(exchange(projected[index].reshape(parts, 3, shard_len, cols)))
+        out, lse = call_attend(jnp.broadcast_to(begins[index][:, None], (seq_len, 128)), got[index])
+        lses.append(lse)
+        att_local.append(out)
+        att.append(exchange(out))
+
+    res = call_layer(pos, att, x, cot, gains, shifts, ups, mixes)
+    outputs, att_all, normed2, act, g_up, g_b2, g_b1, g_hidden = res[:8]
+    g_att, sums = res[8:11], res[11]
+    up_parts, mix_parts = call_weight_grad(act, g_up, normed2, g_b2, att_all, g_b1)
+    up_sum = lax.psum_scatter(collect(up_parts, "x"), "z", scatter_dimension=0, tiled=False)
+    mix_sum = lax.psum_scatter(collect(mix_parts, "y"), "z", scatter_dimension=0, tiled=False)
+    units = w_down.shape[0]
+    down_sum, out_sum = mix_sum[:units], mix_sum[units:]
+
+    back = []
+    for index in range(micro):
+        grad = exchange(g_att[index])
+        res = call_attend_back(
+            jnp.broadcast_to(begins[index][None], (8, seq_len)),
+            cosines[index],
+            sines[index],
+            got[index],
+            grad,
+            att_local[index],
+            lses[index],
+        )
+        back.append(exchange(res).reshape(nz, 2, 3, shard_len, cols))
+    qkv_parts = collect(call_qkv_grad(pos, back, normed1), "both")
+    qkv_sum = qkv_parts[0].astype(F32)
+    for k in range(1, nz):
+        qkv_sum = qkv_sum + ring(qkv_parts[k], k, nz).astype(F32)
+    inputs_grad, sums0 = call_input_grad(pos, back, x, gains, g_hidden, qkv)
+    norm_sums = total_norms(sums[:6], part)
+    norm_sums0 = total_norms(sums0[:2], part)
+    return (
+        outputs.reshape(inputs.shape),
+        inputs_grad.reshape(inputs.shape),
+        qkv_sum,
+        out_sum.astype(F32),
+        up_sum.astype(F32),
+        down_sum.astype(F32),
+        jnp.concatenate([norm_sums0[:1], norm_sums[:3]]),
+        jnp.concatenate([norm_sums0[1:], norm_sums[3:]]),
+    )
+
+
+def fits_fast(mesh, inputs, w_qkv, w_up):
+    dp, tensor = mesh.shape["dp"], mesh.shape["tensor"]
+    return (
+        dp == 4
+        and tensor == 8
+        and inputs.shape[0] == 3
+        and inputs.shape[1] == dp
+        and inputs.shape[2] == 1024
+        and w_qkv.shape[1:] == (1024, 1024)
+        and w_up.shape[1] == 4096
+    )
+
+
 def solution(mesh):
     dp, tensor = mesh.shape["dp"], mesh.shape["tensor"]
     names = ("y", "c", "z", "x")
@@ -300,10 +1022,15 @@
     tokens = P(None, rows, seq, None)
     weights = (P(None, rows, seq), P(seq, rows), P(rows, seq), P(seq, rows))
     norm = P(None, rows)
-    return jax.shard_map(
-        shards,
-        mesh=fine,
-        in_specs=(tokens, P(None, rows, None)) + weights + (norm, norm, tokens),
-        out_specs=(tokens, tokens) + weights + (norm, norm),
-        check_vma=False,
-    )
+
+    def run(*arrays):
+        fast = fits_fast(mesh, arrays[0], arrays[2], arrays[4])
+        return jax.shard_map(
+            fast_shards if fast else shards,
+            mesh=fine,
+            in_specs=(tokens, P(None, rows, None)) + weights + (norm, norm, tokens),
+            out_specs=(tokens, tokens) + weights + (norm, norm),
+            check_vma=False,
+        )(*arrays)
+
+    return run

time: 1020 us -> 609 us (0.60)
  local copies, waits for them, and re-layouts: 270 us -> 42.2 us
  waiting for transfers between devices: 382 us -> 236 us
  matrix products: 134 us -> 0 us
  Pallas kernels: 0 us -> 128 us
  other arithmetic: 103 us -> 54.6 us
  starting transfers between devices: 62.1 us -> 97.1 us
  blocking collectives: 46.1 us -> 30 us
    all_gather x4 -> x2, waiting for transfers between devices: 187 us -> 1.32 us  [the longest x1 1.3 us: fast_shards(): up_mine = lax.all_gather(w_up, 'z', axis=0, tiled=False)]
    ppermute x8 -> x62, waiting for transfers between devices: 19.8 us -> 175 us  [the longest x52 164 us: swap(): return lax.ppermute(values, axis, SWAP)]
    dot_general x48 -> x0, matrix products: 134 us -> none  [the longest x6 15.7 us: attention_backward(): dp = jnp.einsum('hqe,hke->hqk', dob, vb, preferred_element_type=F32)]
    pallas_call x0 -> x11, Pallas kernels: none -> 128 us  [the longest x1 43.9 us: call_layer(): pl.pallas_call(layer_kernel, grid_spec=pltpu.PrefetchScalarGridSpec(num_s...]
    unnamed x16 -> x4, waiting for transfers between devices: 69.6 us -> 0.74 us
    transpose x13 -> x0, local copies, waits for them, and re-layouts: 66.6 us -> none  [the longest x1 16.2 us: shards(): qkv_all.transpose(0, 1, 4, 3, 2, 5).reshape(width, 3 * parts * hcols)]
    reshape x14 -> x3, local copies, waits for them, and re-layouts: 60.9 us -> 2.95 us  [the longest x2 2.93 us: to_own(): return jnp.swapaxes(pieces, -3, -2).reshape(values.shape)]
    unnamed x290 -> x99, local copies, waits for them, and re-layouts: 64.4 us -> 7.72 us
  transfers between devices with their start and end apart: 32 -> 76, of which waited for: 16 -> 25; matrix products, arithmetic and copies ran while one was open for 36% -> 14% of each run, Pallas kernels for 0% -> 14%
where the time goes in v2:
time: 609 us; the launch traced here: 603 us
  waiting for transfers between devices  236 us (39%)
  Pallas kernels  128 us (21%)
  starting transfers between devices  97.1 us (16%)
  other arithmetic  54.6 us (9%)
  local copies, waits for them, and re-layouts  42.2 us (7%)
  blocking collectives  30 us (5%)
  between operations  14.8 us (2%)
    ppermute x52, waiting for transfers between devices, swap(): return lax.ppermute(values, axis, SWAP)  164 us
    all_to_all x10, waiting for transfers between devices, exchange(): return lax.all_to_all(values, SEQ, 0, 0, tiled=True)  58.3 us
    all_to_all x10, starting transfers between devices, exchange(): return lax.all_to_all(values, SEQ, 0, 0, tiled=True)  48.6 us
    pallas_call x1, Pallas kernels, call_layer(): pl.pallas_call(layer_kernel, grid_spec=pltpu.PrefetchScalarGridSpec(num_s...  43.9 us
    ppermute x52, starting transfers between devices, swap(): return lax.ppermute(values, axis, SWAP)  27.4 us
    all_to_all x2, blocking collectives, exchange(): return lax.all_to_all(values, SEQ, 0, 0, tiled=True)  24.5 us
    convert_element_type x14, other arithmetic, add(): return total.astype(BF16)  24.4 us
    pallas_call x3, Pallas kernels, call_attend_back(): pl.pallas_call(attend_back_kernel, out_shape=jax.ShapeDtypeStruct((parts,...  20.6 us
  transfers between devices with their start and end apart: 76, of which 25 were waited for; matrix products, arithmetic and copies ran while one was open for 14% of the time, Pallas kernels for 14%

profile of v2, /device:TPU:0, one launch (start us, length us, event | category | flops | bytes accessed | tf_op | source)
XLA Modules:
  0.0 602.6 jit_solution(14122868620660466930)
XLA Ops:
  36.2 7.0 %fusion.5 = (f32[1024,32]{1,0:T(8,128)}, f32[1024,32]{1,0:T(8,128)}, f32[1024,32]{1,0:T(8,128)}, f32[1024,32]{1,0:T(8,128)S(1)}, f32[1024,32]{1,0:T(8,128)}, /*i...) fusion(f32[32]{0:T(128)S(1)} %multiply_exponential_fusion, ...), kind=kLoop, calls=%fused_computation.53 | loop fusion | flops 196608 | bytes 1192064 | tf_op jit(solution)/shard_map/neg | solution.py:945
  56.7 10.9 %collective-permute-done.3.refs_1_.refs_7_ = bf16[4,3,256,128]{3,2,1,0:T(8,128)(2,1)} collective-permute-done((bf16[4,3,256,128]{3,2,1,0:T(8,128)(2,1)S(1)}, bf16[4,3,256,128]{3,2,1,0:T(8,128)(2,1)}, u32[]{:S(2)}, u32[]{:S(2)}) %collective-permute-start.3) | collective-permute-done | bytes 786464 | tf_op jit(solution)/shard_map/ppermute | solution.py:855
  92.5 9.2 %project.1 = (bf16[4,2,3,128,128]{4,3,2,1,0:T(8,128)(2,1)}, bf16[4,2,3,128,128]{4,3,2,1,0:T(8,128)(2,1)}, bf16[4,2,3,128,128]{4,3,2,1,0:T(8,128)(2,1)}, bf16[384,1024]{1,0:T(8,128)(2,1)}) custom-call(s32[4]{0:T(128)} %pad_add_fusion.pos, bf16[384,1024]{1,0:T(8,128)(2,1)} %reshape.98.x.refs_3_, f32[4,1024]{1,0:T(4,128)} %slice.113.gains.refs_5_.refs_4_, ...), custom_call_target="tpu_custom_call" | custom-call | flops 2415919104 | bytes 12000000 | tf_op jit(solution)/shard_map/project/pallas_call | solution.py:398
  107.4 30.3 %all-to-all-done.2.got = bf16[8,3,128,128]{3,2,1,0:T(8,128)(2,1)S(1)} async-done(((bf16[8,3,128,128]{3,2,1,0:T(8,128)(2,1)}), bf16[8,3,128,128]{3,2,1,0:T(8,128)(2,1)S(1)}, u32[]{:S(2)}, u32[]{:S(2)}) %all-to-all-start.2) | async-done | bytes 786464 | tf_op jit(solution)/shard_map/all_to_all | solution.py:953
  146.9 14.1 %all-to-all-done.4.got = bf16[8,3,128,128]{3,2,1,0:T(8,128)(2,1)S(1)} async-done(((bf16[8,3,128,128]{3,2,1,0:T(8,128)(2,1)}), bf16[8,3,128,128]{3,2,1,0:T(8,128)(2,1)S(1)}, u32[]{:S(2)}, u32[]{:S(2)}) %all-to-all-start.4) | async-done | bytes 786464 | tf_op jit(solution)/shard_map/all_to_all | solution.py:953
  171.0 17.0 %collective-permute-done.18.refs_16_.refs_24_ = bf16[4,640,256]{2,1,0:T(8,128)(2,1)} collective-permute-done((bf16[4,640,256]{2,1,0:T(8,128)(2,1)}, bf16[4,640,256]{2,1,0:T(8,128)(2,1)}, u32[]{:S(2)}, u32[]{:S(2)}) %collective-permute-start.18) | collective-permute-done | bytes 1310752 | tf_op jit(solution)/shard_map/ppermute | solution.py:855
  188.2 21.3 %collective-permute-done.11.refs_8_ = bf16[4,256,512]{2,1,0:T(8,128)(2,1)} collective-permute-done((bf16[4,256,512]{2,1,0:T(8,128)(2,1)}, bf16[4,256,512]{2,1,0:T(8,128)(2,1)}, u32[]{:S(2)}, u32[]{:S(2)}) %collective-permute-start.11) | collective-permute-done | bytes 1048608 | tf_op jit(solution)/shard_map/ppermute | solution.py:855
  226.3 9.2 %collective-permute-done.13.refs_10_ = bf16[4,256,512]{2,1,0:T(8,128)(2,1)} collective-permute-done((bf16[4,256,512]{2,1,0:T(8,128)(2,1)}, bf16[4,256,512]{2,1,0:T(8,128)(2,1)}, u32[]{:S(2)}, u32[]{:S(2)}) %collective-permute-start.13) | collective-permute-done | bytes 1048608 | tf_op jit(solution)/shard_map/ppermute | solution.py:855
  263.3 6.2 %all-to-all-done.1.refs_0_ = bf16[8,128,128]{2,1,0:T(8,128)(2,1)S(1)} async-done(((bf16[8,128,128]{2,1,0:T(8,128)(2,1)}), bf16[8,128,128]{2,1,0:T(8,128)(2,1)S(1)}, u32[]{:S(2)}, u32[]{:S(2)}) %all-to-all-start.1) | async-done | bytes 262176 | tf_op jit(solution)/shard_map/all_to_all | solution.py:953
  270.2 43.9 %layer.1 = (bf16[384,1024]{1,0:T(8,128)(2,1)}, bf16[384,1024]{1,0:T(8,128)(2,1)}, bf16[384,1024]{1,0:T(8,128)(2,1)}, bf16[4,2,384,512]{3,2,1,0:T(8,128)(2,1)}, b...) custom-call(s32[4]{0:T(128)} %pad_add_fusion.pos, ...), custom_call_target="tpu_custom_call" | custom-call | flops 14495514624 | bytes 60000000 | tf_op jit(solution)/shard_map/layer/pallas_call | solution.py:666
  314.2 12.3 %all_to_all.60.grad = bf16[8,128,128]{2,1,0:T(8,128)(2,1)} all-to-all(bf16[8,128,128]{2,1,0:T(8,128)(2,1)} %get-tuple-element.67), channel_id=1, replica_groups=mesh['y'=2,'c'=2,'z'=4,'x'=2] {'z','x'}, dimensions={0} | all-to-all | bytes 524288 | tf_op jit(solution)/shard_map/all_to_all | solution.py:953
  326.4 12.3 %all_to_all.61.grad = bf16[8,128,128]{2,1,0:T(8,128)(2,1)} all-to-all(bf16[8,128,128]{2,1,0:T(8,128)(2,1)} %get-tuple-element.65), channel_id=1, replica_groups=mesh['y'=2,'c'=2,'z'=4,'x'=2] {'z','x'}, dimensions={0} | all-to-all | bytes 524288 | tf_op jit(solution)/shard_map/all_to_all | solution.py:953
  342.9 6.8 %attend_back.5 = bf16[8,3,128,128]{3,2,1,0:T(8,128)(2,1)} custom-call(s32[8,1024]{1,0:T(8,128)} %broadcast_in_dim.36.begins, f32[1024,128]{1,0:T(8,128)} %copy-done.35, f32[1024,128]{1,0:T(8,128)} %pad_maximum_fusion.8.sin, bf16[8,3,128,128]{3,2,1,0:T(8,128)(2,1)} %copy-done.24, bf16[8,128,128]{2,1,0:T(8,128)(2,1)} %all_to_all.60.grad, ...), custom_call_target="tpu_custom_call" | custom-call | flops 2684354560 | bytes 4000000 | tf_op jit(solution)/shard_map/attend_back/pallas_call | solution.py:516
  355.8 15.2 %weight_grad.1 = (bf16[4,256,512]{2,1,0:T(8,128)(2,1)}, bf16[4,256,512]{2,1,0:T(8,128)(2,1)}, bf16[4,256,512]{2,1,0:T(8,128)(2,1)}, bf16[4,256,512]{2,1,0:T(8,12...) custom-call(bf16[4,2,384,512]{3,2,1,0:T(8,128)(2,1)} %get-tuple-elem, ...), custom_call_target="tpu_custom_call" | custom-call | flops 7247757312 | bytes 40000000 | tf_op jit(solution)/shard_map/weight_grad/pallas_call | solution.py:734
  371.6 6.9 %attend_back.4 = bf16[8,3,128,128]{3,2,1,0:T(8,128)(2,1)} custom-call(s32[8,1024]{1,0:T(8,128)} %broadcast_in_dim.35.begins, f32[1024,128]{1,0:T(8,128)} %copy-done.34, f32[1024,128]{1,0:T(8,128)} %pad_maximum_fusion.7.sin, bf16[8,3,128,128]{3,2,1,0:T(8,128)(2,1)} %copy-done.23, bf16[8,128,128]{2,1,0:T(8,128)(2,1)} %all_to_all.61.grad, ...), custom_call_target="tpu_custom_call" | custom-call | flops 2684354560 | bytes 4000000 | tf_op jit(solution)/shard_map/attend_back/pallas_call | solution.py:516
  378.5 6.6 %all-to-all-start.9 = ((bf16[8,3,128,128]{3,2,1,0:T(8,128)(2,1)}), bf16[8,3,128,128]{3,2,1,0:T(8,128)(2,1)S(1)}, u32[]{:S(2)}, u32[]{:S(2)}) async-start(bf16[8,3,128,128]{3,2,1,0:T(8,128)(2,1)} %attend_back.4), calls=%async_computation.9 | async-start | bytes 1572864 | tf_op jit(solution)/shard_map/all_to_all | solution.py:953
  394.7 25.2 %collective-permute-done.59 = f32[6,256]{1,0:T(8,128)S(1)} collective-permute-done((f32[6,256]{1,0:T(8,128)S(1)}, f32[6,256]{1,0:T(8,128)S(1)}, u32[]{:S(2)}, u32[]{:S(2)}) %collective-permute-start.59) | collective-permute-done | bytes 6176 | tf_op jit(solution)/shard_map/ppermute | solution.py:855
  420.5 6.8 %attend_back.3 = bf16[8,3,128,128]{3,2,1,0:T(8,128)(2,1)} custom-call(s32[8,1024]{1,0:T(8,128)} %broadcast_in_dim.34.begins, f32[1024,128]{1,0:T(8,128)} %copy-done.33, f32[1024,128]{1,0:T(8,128)} %copy-done.32, bf16[8,3,128,128]{3,2,1,0:T(8,128)(2,1)} %copy-done.22, bf16[8,128,128]{2,1,0:T(8,128)(2,1)} %copy-done.36, ...), custom_call_target="tpu_custom_call" | custom-call | flops 2684354560 | bytes 4000000 | tf_op jit(solution)/shard_map/attend_back/pallas_call | solution.py:516
  454.6 7.8 %qkv_grad.1 = (bf16[4,3,256,128]{3,2,1,0:T(8,128)(2,1)}, bf16[4,3,256,128]{3,2,1,0:T(8,128)(2,1)}, bf16[4,3,256,128]{3,2,1,0:T(8,128)(2,1)}, bf16[4,3,256,128]{3...) custom-call(s32[4]{0:T(128)} %pad_add_fusion.pos, ...), custom_call_target="tpu_custom_call" | custom-call | flops 2415919104 | bytes 12000000 | tf_op jit(solution)/shard_map/qkv_grad/pallas_call | solution.py:783
  462.4 14.2 %input_grad.1 = (f32[384,1024]{1,0:T(8,128)}, f32[8,1024]{1,0:T(8,128)}) custom-call(s32[4]{0:T(128)} %pad_add_fusion.pos, bf16[4,2,3,128,128]{4,3,2,1,0:T(8,128)(2,1)} %bitcast.68, bf16[4,2,3,128,128]{4,3,2,1,0:T(8,128)(2,1)} %bitcast.66, bf16[4,2,3,128,128]{4,3,2,1,0:T(8,128)(2,1)} %bitcast.64, bf16[384,1024]{1,0:T(8,128)(2,1)} %reshape.98.x.refs_3_, ...), custom_call_target="tpu_custom_call" | custom-call | flops 2415919104 | bytes 16000000 | tf_op jit(solution)/shard_map/input_grad/pallas_call | solution.py:835
  482.8 13.0 %collective-permute-done.39 = bf16[4,640,256]{2,1,0:T(8,128)(2,1)} collective-permute-done((bf16[4,640,256]{2,1,0:T(8,128)(2,1)}, bf16[4,640,256]{2,1,0:T(8,128)(2,1)}, u32[]{:S(2)}, u32[]{:S(2)}) %collective-permute-start.39) | collective-permute-done | bytes 1310752 | tf_op jit(solution)/shard_map/ppermute | solution.py:855
  501.5 29.5 %collective-permute-done.28 = bf16[2,3,256,128]{3,2,1,0:T(8,128)(2,1)S(1)} collective-permute-done((bf16[2,3,256,128]{3,2,1,0:T(8,128)(2,1)S(1)}, bf16[2,3,256,128]{3,2,1,0:T(8,128)(2,1)S(1)}, u32[]{:S(2)}, u32[]{:S(2)}) %collective-permute-start.28) | collective-permute-done | bytes 393248 | tf_op jit(solution)/shard_map/ppermute | solution.py:855
  536.7 6.6 %collective-permute-done.31 = bf16[2,3,256,128]{3,2,1,0:T(8,128)(2,1)S(1)} collective-permute-done((bf16[2,3,256,128]{3,2,1,0:T(8,128)(2,1)S(1)}, bf16[2,3,256,128]{3,2,1,0:T(8,128)(2,1)S(1)}, u32[]{:S(2)}, u32[]{:S(2)}) %collective-permute-start.31) | collective-permute-done | bytes 393248 | tf_op jit(solution)/shard_map/ppermute | solution.py:855
  549.2 13.5 %collective-permute-done.52 = f32[2,256]{1,0:T(2,128)S(1)} collective-permute-done((f32[2,256]{1,0:T(2,128)S(1)}, f32[2,256]{1,0:T(2,128)S(1)}, u32[]{:S(2)}, u32[]{:S(2)}) %collective-permute-start.52) | collective-permute-done | bytes 2080 | tf_op jit(solution)/shard_map/ppermute | solution.py:855
  (339 shorter events, 242.0 us)
Async XLA Ops:
  7.2 134.1 %all-gather.7.cloned.1.call-start = ((), (), s32[]{:S(2)}) async-start(), calls=%async_computation.17 | async-start | bytes 1638400 | tf_op jit(solution)/shard_map/all_gather | solution.py:920
  141.3 46.7 %collective-permute-start.18 = (bf16[4,640,256]{2,1,0:T(8,128)(2,1)}, bf16[4,640,256]{2,1,0:T(8,128)(2,1)}, u32[]{:S(2)}, u32[]{:S(2)}) collective-permute-start(bf16[4,640,256]{2,1,0:T(8,128)(2,1)} %bitcast.77), channel_id=1, source_target_pairs={{0,1},{1,0},{2,3},{3,2},{4,5},{5,4},{6,7},{7,6},{8,9},{9,8},{10,11... | collective-permute-start | bytes 3932168 | tf_op jit(solution)/shard_map/ppermute | solution.py:855
  145.4 64.1 %collective-permute-start.11 = (bf16[4,256,512]{2,1,0:T(8,128)(2,1)}, bf16[4,256,512]{2,1,0:T(8,128)(2,1)}, u32[]{:S(2)}, u32[]{:S(2)}) collective-permute-start(bf16[4,256,512]{2,1,0:T(8,128)(2,1)} %bitcast.83), channel_id=1, source_target_pairs={{0,1},{1,0},{2,3},{3,2},{4,5},{5,4},{6,7},{7,6},{8,9},{9,8},{10,11... | collective-permute-start | bytes 3145736 | tf_op jit(solution)/shard_map/ppermute | solution.py:855
  146.9 63.3 %collective-permute-start.14 = (bf16[4,256,512]{2,1,0:T(8,128)(2,1)}, bf16[4,256,512]{2,1,0:T(8,128)(2,1)}, u32[]{:S(2)}, u32[]{:S(2)}) collective-permute-start(bf16[4,256,512]{2,1,0:T(8,128)(2,1)} %bitcast.84), channel_id=1, source_target_pairs={{0,8},{8,0},{1,9},{9,1},{2,10},{10,2},{3,11},{11,3},{4,12},{12,4},... | collective-permute-start | bytes 3145736 | tf_op jit(solution)/shard_map/ppermute | solution.py:855
  161.0 56.0 %all-to-all-start = ((bf16[8,3,128,128]{3,2,1,0:T(8,128)(2,1)}), bf16[8,3,128,128]{3,2,1,0:T(8,128)(2,1)S(1)}, u32[]{:S(2)}, u32[]{:S(2)}) async-start(bf16[8,3,128,128]{3,2,1,0:T(8,128)(2,1)} %bitcast.69), calls=%async_computation | async-start | bytes 1572864 | tf_op jit(solution)/shard_map/all_to_all | solution.py:953
  165.7 56.6 %collective-permute-start.19 = (bf16[4,640,256]{2,1,0:T(8,128)(2,1)}, bf16[4,640,256]{2,1,0:T(8,128)(2,1)}, u32[]{:S(2)}, u32[]{:S(2)}) collective-permute-start(bf16[4,640,256]{2,1,0:T(8,128)(2,1)} %bitcast.78), channel_id=1, source_target_pairs={{0,16},{16,0},{1,17},{17,1},{2,18},{18,2},{3,19},{19,3},{4,20},{20... | collective-permute-start | bytes 3932168 | tf_op jit(solution)/shard_map/ppermute | solution.py:855
  171.0 51.7 %collective-permute-start.21 = (bf16[4,640,256]{2,1,0:T(8,128)(2,1)}, bf16[4,640,256]{2,1,0:T(8,128)(2,1)}, u32[]{:S(2)}, u32[]{:S(2)}) collective-permute-start(bf16[4,640,256]{2,1,0:T(8,128)(2,1)} %bitcast.79), channel_id=1, source_target_pairs={{0,8},{8,0},{1,9},{9,1},{2,10},{10,2},{3,11},{11,3},{4,12},{12,4},... | collective-permute-start | bytes 3932168 | tf_op jit(solution)/shard_map/ppermute | solution.py:855
  222.3 47.2 %collective-permute-start.22 = (bf16[4,640,256]{2,1,0:T(8,128)(2,1)}, bf16[4,640,256]{2,1,0:T(8,128)(2,1)}, u32[]{:S(2)}, u32[]{:S(2)}) collective-permute-start(bf16[4,640,256]{2,1,0:T(8,128)(2,1)} %collective-permute-done.18.refs_16_.refs_24_), channel_id=1, source_target_pairs={{0,8},{8,0},{1,9},{9,1},{2,10},{10,2},{3,11},{11,3},{4,12},{12,4},... | collective-permute-start | bytes 3932168 | tf_op jit(solution)/shard_map/ppermute | solution.py:855
  222.6 46.9 %collective-permute-start.23 = (bf16[4,640,256]{2,1,0:T(8,128)(2,1)}, bf16[4,640,256]{2,1,0:T(8,128)(2,1)}, u32[]{:S(2)}, u32[]{:S(2)}) collective-permute-start(bf16[4,640,256]{2,1,0:T(8,128)(2,1)} %collective-permute-done.19.refs_17_.refs_25_), channel_id=1, source_target_pairs={{0,8},{8,0},{1,9},{9,1},{2,10},{10,2},{3,11},{11,3},{4,12},{12,4},... | collective-permute-start | bytes 3932168 | tf_op jit(solution)/shard_map/ppermute | solution.py:855
  226.3 43.2 %collective-permute-start.24 = (bf16[4,640,256]{2,1,0:T(8,128)(2,1)}, bf16[4,640,256]{2,1,0:T(8,128)(2,1)}, u32[]{:S(2)}, u32[]{:S(2)}) collective-permute-start(bf16[4,640,256]{2,1,0:T(8,128)(2,1)} %collective-permute-done.20.refs_18_.refs_26_), channel_id=1, source_target_pairs={{0,8},{8,0},{1,9},{9,1},{2,10},{10,2},{3,11},{11,3},{4,12},{12,4},... | collective-permute-start | bytes 3932168 | tf_op jit(solution)/shard_map/ppermute | solution.py:855
  378.5 48.9 %all-to-all-start.9 = ((bf16[8,3,128,128]{3,2,1,0:T(8,128)(2,1)}), bf16[8,3,128,128]{3,2,1,0:T(8,128)(2,1)S(1)}, u32[]{:S(2)}, u32[]{:S(2)}) async-start(bf16[8,3,128,128]{3,2,1,0:T(8,128)(2,1)} %attend_back.4), calls=%async_computation.9 | async-start | bytes 1572864 | tf_op jit(solution)/shard_map/all_to_all | solution.py:953
  385.7 47.3 %collective-permute-start.44 = (bf16[4,256,512]{2,1,0:T(8,128)(2,1)}, bf16[4,256,512]{2,1,0:T(8,128)(2,1)}, u32[]{:S(2)}, u32[]{:S(2)}) collective-permute-start(bf16[4,256,512]{2,1,0:T(8,128)(2,1)} %get-tuple-element.97), channel_id=1, source_target_pairs={{0,8},{8,0},{1,9},{9,1},{2,10},{10,2},{3,11},{11,3},{4,12},{12,4},... | collective-permute-start | bytes 3145736 | tf_op jit(solution)/shard_map/ppermute | solution.py:855
  385.9 50.0 %collective-permute-start.46 = (bf16[4,256,512]{2,1,0:T(8,128)(2,1)}, bf16[4,256,512]{2,1,0:T(8,128)(2,1)}, u32[]{:S(2)}, u32[]{:S(2)}) collective-permute-start(bf16[4,256,512]{2,1,0:T(8,128)(2,1)} %get-tuple-element.99), channel_id=1, source_target_pairs={{0,8},{8,0},{1,9},{9,1},{2,10},{10,2},{3,11},{11,3},{4,12},{12,4},... | collective-permute-start | bytes 3145736 | tf_op jit(solution)/shard_map/ppermute | solution.py:855
  386.2 55.2 %collective-permute-start.38 = (bf16[4,640,256]{2,1,0:T(8,128)(2,1)}, bf16[4,640,256]{2,1,0:T(8,128)(2,1)}, u32[]{:S(2)}, u32[]{:S(2)}) collective-permute-start(bf16[4,640,256]{2,1,0:T(8,128)(2,1)} %get-tuple-element.91), channel_id=1, source_target_pairs={{0,8},{8,0},{1,9},{9,1},{2,10},{10,2},{3,11},{11,3},{4,12},{12,4},... | collective-permute-start | bytes 3932168 | tf_op jit(solution)/shard_map/ppermute | solution.py:855
  389.0 47.3 %collective-permute-start.48 = (bf16[4,256,512]{2,1,0:T(8,128)(2,1)}, bf16[4,256,512]{2,1,0:T(8,128)(2,1)}, u32[]{:S(2)}, u32[]{:S(2)}) collective-permute-start(bf16[4,256,512]{2,1,0:T(8,128)(2,1)} %add_convert_fusion.8), channel_id=1, source_target_pairs={{0,1},{1,0},{2,3},{3,2},{4,5},{5,4},{6,7},{7,6},{8,9},{9,8},{10,11... | collective-permute-start | bytes 3145736 | tf_op jit(solution)/shard_map/ppermute | solution.py:855
  432.9 157.9 %reduce-scatter.5.cloned.1.call-start = ((), (), s32[]{:S(2)}) async-start(), calls=%async_computation.15 | async-start | bytes 1310720 | tf_op jit(solution)/shard_map/reduce_scatter | solution.py:967
  433.0 43.7 %collective-permute-start.43 = (bf16[4,256,512]{2,1,0:T(8,128)(2,1)}, bf16[4,256,512]{2,1,0:T(8,128)(2,1)}, u32[]{:S(2)}, u32[]{:S(2)}) collective-permute-start(bf16[4,256,512]{2,1,0:T(8,128)(2,1)} %get-tuple-element.95), channel_id=1, source_target_pairs={{0,8},{8,0},{1,9},{9,1},{2,10},{10,2},{3,11},{11,3},{4,12},{12,4},... | collective-permute-start | bytes 3145736 | tf_op jit(solution)/shard_map/ppermute | solution.py:855
  435.9 46.7 %collective-permute-start.37 = (bf16[4,640,256]{2,1,0:T(8,128)(2,1)}, bf16[4,640,256]{2,1,0:T(8,128)(2,1)S(1)}, u32[]{:S(2)}, u32[]{:S(2)}) collective-permute-start(bf16[4,640,256]{2,1,0:T(8,128)(2,1)} %get-tuple-element.89), channel_id=1, source_target_pairs={{0,8},{8,0},{1,9},{9,1},{2,10},{10,2},{3,11},{11,3},{4,12},{12,4},... | collective-permute-start | bytes 3932168 | tf_op jit(solution)/shard_map/ppermute | solution.py:855
  444.3 51.6 %collective-permute-start.39 = (bf16[4,640,256]{2,1,0:T(8,128)(2,1)}, bf16[4,640,256]{2,1,0:T(8,128)(2,1)}, u32[]{:S(2)}, u32[]{:S(2)}) collective-permute-start(bf16[4,640,256]{2,1,0:T(8,128)(2,1)} %add_convert_fusion.3), channel_id=1, source_target_pairs={{0,16},{16,0},{1,17},{17,1},{2,18},{18,2},{3,19},{19,3},{4,20},{20... | collective-permute-start | bytes 3932168 | tf_op jit(solution)/shard_map/ppermute | solution.py:855
  478.0 53.1 %collective-permute-start.36 = (bf16[4,640,256]{2,1,0:T(8,128)(2,1)}, bf16[4,640,256]{2,1,0:T(8,128)(2,1)}, u32[]{:S(2)}, u32[]{:S(2)}) collective-permute-start(bf16[4,640,256]{2,1,0:T(8,128)(2,1)} %get-tuple-element.87), channel_id=1, source_target_pairs={{0,8},{8,0},{1,9},{9,1},{2,10},{10,2},{3,11},{11,3},{4,12},{12,4},... | collective-permute-start | bytes 3932168 | tf_op jit(solution)/shard_map/ppermute | solution.py:855
  478.5 53.2 %collective-permute-start.42 = (bf16[4,640,256]{2,1,0:T(8,128)(2,1)}, bf16[4,640,256]{2,1,0:T(8,128)(2,1)}, u32[]{:S(2)}, u32[]{:S(2)}) collective-permute-start(bf16[4,640,256]{2,1,0:T(8,128)(2,1)} %add_convert_fusion.1), channel_id=1, source_target_pairs={{0,16},{16,0},{1,17},{17,1},{2,18},{18,2},{3,19},{19,3},{4,20},{20... | collective-permute-start | bytes 3932168 | tf_op jit(solution)/shard_map/ppermute | solution.py:855
  482.4 110.2 %reduce-scatter.3.cloned.1.call-start = ((), (), s32[]{:S(2)}) async-start(), calls=%async_computation.14 | async-start | bytes 1638400 | tf_op jit(solution)/shard_map/reduce_scatter | solution.py:968
  499.2 45.6 %collective-permute-start.60 = (f32[6,256]{1,0:T(8,128)S(1)}, f32[6,256]{1,0:T(8,128)S(1)}, u32[]{:S(2)}, u32[]{:S(2)}) collective-permute-start(f32[6,256]{1,0:T(8,128)S(1)} %add.162), channel_id=1, source_target_pairs={{0,2},{2,0},{4,6},{6,4},{1,3},{3,1},{5,7},{7,5},{8,10},{10,8},{12,... | collective-permute-start | bytes 18440 | tf_op jit(solution)/shard_map/ppermute | solution.py:903
  531.7 43.4 %collective-permute-start.25 = (bf16[4,3,256,128]{3,2,1,0:T(8,128)(2,1)}, bf16[4,3,256,128]{3,2,1,0:T(8,128)(2,1)S(1)}, u32[]{:S(2)}, u32[]{:S(2)}) collective-permute-start(bf16[4,3,256,128]{3,2,1,0:T(8,128)(2,1)} %get-tuple-element.73), channel_id=1, source_target_pairs={{0,8},{8,0},{1,9},{9,1},{2,10},{10,2},{3,11},{11,3},{4,12},{12,4},... | collective-permute-start | bytes 2359304 | tf_op jit(solution)/shard_map/ppermute | solution.py:855
  (102 other events, 1584.4 us)
Sparse Core Ops, SparseCore 0:
  15.2 35.4 all-gather.6
  109.0 35.5 all-gather.4
  482.5 26.9 reduce-scatter.4
  535.7 31.5 reduce-scatter.2

commit v3 on v1

--- a/solution.py
+++ b/solution.py
@@ -1,8 +1,12 @@
+import functools
 import math
 
 import jax
 import jax.numpy as jnp
+import numpy as np
 from jax import lax
+from jax.experimental import pallas as pl
+from jax.experimental.pallas import tpu as pltpu
 from jax.sharding import Mesh, PartitionSpec as P
 
 HD = 64
@@ -292,6 +296,1039 @@
     return full
 
 
+NT = (((1,), (1,)), ((), ()))
+GELU_A = 0.7978845608
+GELU_B = 0.044715
+
+
+O = dict(cost=0.2, fcut=3, bcut=3, gate_mix=0, gate_up=0, gate_grad=1, gate_ab=1, gate_b1=1, qkv_half=2, up_z=0, order=0, gate_add=0, norm=1, gate_us=1)
+O.update({})
+COST = O["cost"]
+
+
+def dot(a, b):
+    return jnp.dot(a, b, preferred_element_type=F32)
+
+
+def dot_nt(a, b):
+    return lax.dot_general(a, b, NT, preferred_element_type=F32)
+
+
+def params(semantics=1):
+    return pltpu.CompilerParams(
+        dimension_semantics=("arbitrary",) * semantics, vmem_limit_bytes=60 * 1024 * 1024
+    )
+
+
+def cost(flops, size, transcendentals=0):
+    return pl.CostEstimate(
+        flops=int(flops * COST), bytes_accessed=int(size * COST), transcendentals=int(transcendentals * COST)
+    )
+
+
+def whole(shape):
+    return pl.BlockSpec(shape, lambda *_: (0,) * len(shape))
+
+
+def swap_halves(values):
+    lane = lax.broadcasted_iota(jnp.int32, values.shape, 1)
+    low = lax.rem(lane, HD) < HD // 2
+    return jnp.where(low, pltpu.roll(values, 96, 1), pltpu.roll(values, 32, 1))
+
+
+def row_stats(values):
+    average = jnp.mean(values, axis=-1, keepdims=True)
+    centred = values - average
+    variance = jnp.mean(centred * centred, axis=-1, keepdims=True)
+    scale = lax.rsqrt(variance + EPSILON)
+    return centred * scale, scale
+
+
+def row_pull(grad, xhat, scale, gain):
+    e = grad * gain
+    return scale * (
+        e - jnp.mean(e, axis=-1, keepdims=True) - xhat * jnp.mean(e * xhat, axis=-1, keepdims=True)
+    )
+
+
+def column_sum(values):
+    return jnp.sum(values, axis=0, keepdims=True)
+
+
+def own_place(pos, q, part):
+    place = lax.bitwise_xor(pos[0], q % 2) * 2 + lax.bitwise_xor(pos[1], q // 2)
+    return pl.multiple_of(place * part, part)
+
+
+def load_columns(ref, pos, part):
+    return jnp.concatenate([ref[:, pl.ds(own_place(pos, q, part), part)] for q in range(4)], 1)
+
+
+def store_columns(ref, values, pos, part):
+    for q in range(4):
+        ref[:, pl.ds(own_place(pos, q, part), part)] = values[:, q * part : (q + 1) * part].astype(
+            ref.dtype
+        )
+
+
+def tables(seq_len):
+    lane = np.arange(128)
+    frequency = np.exp((lane % (HD // 2)) * (-2.0 * math.log(10000.0) / HD))
+    angle = np.arange(seq_len)[:, None] * frequency.astype(np.float32).astype(np.float64)
+    sign = np.where(lane % HD < HD // 2, -1.0, 1.0)
+    return np.cos(angle).astype(np.float32), (np.sin(angle) * sign).astype(np.float32)
+
+
+def start_tables(starts):
+    lane = jnp.arange(128)
+    frequency = jnp.exp((lane % (HD // 2)).astype(F32) * (-2.0 * math.log(10000.0) / HD))
+    angle = starts.astype(F32)[..., None] * frequency
+    return jnp.cos(angle), jnp.sin(angle) * jnp.where(lane % HD < HD // 2, -1.0, 1.0)
+
+
+def angle_rows(rows, starts, base, table, start_cos, start_sin):
+    cb, sb = start_cos[0:1], start_sin[0:1]
+    for d in range(1, 4):
+        inside = rows >= starts[base + d]
+        cb = jnp.where(inside, start_cos[d : d + 1], cb)
+        sb = jnp.where(inside, start_sin[d : d + 1], sb)
+    tc, ts = table
+    return tc * cb + ts * sb, ts * cb - tc * sb
+
+
+def begin_of(rows, starts, base):
+    begin = jnp.zeros(rows.shape, jnp.int32)
+    for d in range(1, 4):
+        begin = jnp.where(rows >= starts[base + d], starts[base + d], begin)
+    return begin
+
+
+def proj_kernel(pos, starts, x, gains, shifts, tcos, tsin, start_cos, start_sin, *refs):
+    weights = [refs[2 * q : 2 * q + 2] for q in range(4)]
+    first, last, keep, send = refs[8:12]
+    normed, cos, sin = refs[12:15]
+    outs = [first.at[0, :, 0], first.at[0, :, 1], last.at[0, :, 0]]
+    part = weights[0][0].shape[2]
+    count = first.shape[4]
+
+    @pl.when(pl.program_id(0) == 0)
+    def _():
+        xhat, _ = row_stats(load_columns(x, pos, part).astype(F32))
+        value = (xhat * gains[0:1] + shifts[0:1]).astype(BF16)
+        normed[...] = value
+        keep[...] = value[:, : 2 * part]
+        send[...] = value[:, 2 * part :]
+        rows = lax.broadcasted_iota(jnp.int32, (count, 128), 0) + (pos[2] * 2 + pos[3]) * count
+        for m in range(3):
+            at = slice(m * count, (m + 1) * count)
+            cos[at], sin[at] = angle_rows(
+                rows, starts, 4 * m, (tcos[...], tsin[...]), start_cos.at[m], start_sin.at[m]
+            )
+
+    total = None
+    for q in range(4):
+        block = jnp.concatenate([weights[q][dx][0, kind] for dx in range(2) for kind in range(3)], 1)
+        term = dot(normed[:, q * part : (q + 1) * part], block)
+        total = term if total is None else total + term
+    for dx in range(2):
+        place = lax.bitwise_xor(pos[3], dx)
+        for kind in range(3):
+            at = (dx * 3 + kind) * 128
+            u = total[:, at : at + 128]
+            if kind < 2:
+                u = u * cos[...] + swap_halves(u) * sin[...]
+            u = u.astype(BF16)
+            for m in range(3):
+                outs[m][place, kind] = u[m * count : (m + 1) * count]
+
+
+def ring_place(pos, i, nz):
+    return lax.rem(pos[2] + i, nz)
+
+
+def head_index(nz):
+    return lambda i, pos, *_: (ring_place(pos, i, nz), 0, 0, 0, 0, 0)
+
+
+def call_proj(pos, starts, x, gains, shifts, table, start_table, pieces, shard_len):
+    tokens, width = x.shape
+    nz, _, part, cols = pieces[0][0].shape
+    piece = pl.BlockSpec((1, 3, part, cols), lambda i, *_: (i, 0, 0, 0))
+    outs = [pl.BlockSpec((1, 2, n, 3, shard_len, cols), head_index(nz)) for n in (2, 1)]
+    shapes = [jax.ShapeDtypeStruct((nz, 2, n, 3, shard_len, cols), BF16) for n in (2, 1)]
+    half = (tokens, width // 2)
+    rows = pl.BlockSpec((shard_len, 128), lambda i, pos, _: (pos[2] * 2 + pos[3], 0))
+    return pl.pallas_call(
+        proj_kernel,
+        grid_spec=pltpu.PrefetchScalarGridSpec(
+            num_scalar_prefetch=2,
+            grid=(nz,),
+            in_specs=[whole(a.shape) for a in (x, gains, shifts)]
+            + [rows] * 2
+            + [whole(a.shape) for a in start_table]
+            + [piece] * 8,
+            out_specs=outs + [whole(half)] * 2,
+            scratch_shapes=[
+                pltpu.VMEM((tokens, width), BF16),
+                pltpu.VMEM((tokens, 128), F32),
+                pltpu.VMEM((tokens, 128), F32),
+            ],
+        ),
+        out_shape=shapes + [jax.ShapeDtypeStruct(half, BF16)] * 2,
+        compiler_params=params(),
+        cost_estimate=cost(2 * tokens * width * 3 * nz * 2 * cols, 12e6),
+        name="project",
+    )(pos, starts, x, gains, shifts, *table, *start_table, *[p for pair in pieces for p in pair])
+
+
+def head_mask(shape, head):
+    lane = lax.broadcasted_iota(jnp.int32, shape, 1)
+    return (lane < HD) if head == 0 else (lane >= HD)
+
+
+def attend_kernel(first, starts, got, out, lse_out):
+    micro = first + pl.program_id(0)
+    shards_n, _, count, lanes = got.shape
+    seq_len = shards_n * count
+    block = min(256, seq_len)
+    q_all = (got[:, 0] * 0.125).reshape(seq_len, lanes)
+    k_all = got[:, 1].reshape(seq_len, lanes)
+    v_all = got[:, 2].reshape(seq_len, lanes)
+    per = block // count
+    for start in range(0, seq_len, block):
+        end = start + block
+        qb = q_all[start:end]
+        key = lax.broadcasted_iota(jnp.int32, (block, end), 1)
+        query = start + lax.broadcasted_iota(jnp.int32, (block, end), 0)
+        begin = begin_of(start + lax.broadcasted_iota(jnp.int32, (block, 1), 0), starts, 4 * micro)
+        allowed = (key <= query) & (key >= begin)
+        results = []
+        for head in range(2):
+            mask = head_mask(qb.shape, head)
+            scores = dot_nt(jnp.where(mask, qb, 0), k_all[:end])
+            scores = jnp.where(allowed, scores, -1e30)
+            peak = jnp.max(scores, axis=-1, keepdims=True)
+            e = jnp.exp(scores - peak)
+            total = jnp.sum(e, axis=-1, keepdims=True)
+            results.append(dot(e.astype(BF16), v_all[:end]) / total)
+            lse = jnp.broadcast_to(peak + jnp.log(total), (block, 128))
+            lse_out[head : head + 1, start:end] = jnp.transpose(lse)[0:1]
+        mixed = jnp.where(head_mask(results[0].shape, 0), results[0], results[1]).astype(BF16)
+        out[start // count : end // count] = mixed.reshape(per, count, lanes)
+
+
+def call_attend(first, starts, got):
+    parts, number, _, count, lanes = got.shape
+    seq_len = parts * count
+    return pl.pallas_call(
+        functools.partial(attend_kernel, first),
+        grid_spec=pltpu.PrefetchScalarGridSpec(
+            num_scalar_prefetch=1,
+            grid=(number,),
+            in_specs=[pl.BlockSpec((parts, None, 3, count, lanes), lambda i, _: (0, i, 0, 0, 0))],
+            out_specs=[
+                pl.BlockSpec((parts, None, count, lanes), lambda i, _: (0, i, 0, 0)),
+                pl.BlockSpec((None, 8, seq_len), lambda i, _: (i, 0, 0)),
+            ],
+        ),
+        out_shape=[
+            jax.ShapeDtypeStruct((parts, number, count, lanes), BF16),
+            jax.ShapeDtypeStruct((number, 8, seq_len), F32),
+        ],
+        compiler_params=params(),
+        cost_estimate=cost(
+            number * 8 * seq_len * seq_len * lanes, number * 2e6, number * 2 * seq_len * seq_len
+        ),
+        name="attend",
+    )(starts, got)
+
+
+def attend_back_kernel(
+    first, starts, tcos, tsin, start_cos, start_sin, got, grad, att, lse, out, dq_ref, dk_ref, dv_ref
+):
+    micro = first + pl.program_id(0)
+    shards_n, _, count, lanes = got.shape
+    seq_len = shards_n * count
+    block = min(256, seq_len)
+    q_all = (got[:, 0] * 0.125).reshape(seq_len, lanes)
+    k_all = got[:, 1].reshape(seq_len, lanes)
+    v_all = got[:, 2].reshape(seq_len, lanes)
+    do_all = grad[...].reshape(seq_len, lanes)
+    prod = do_all.astype(F32) * att[...].reshape(seq_len, lanes).astype(F32)
+    prod = jnp.transpose(prod)
+    deltas = [
+        jnp.sum(prod[:HD], axis=0, keepdims=True),
+        jnp.sum(prod[HD:], axis=0, keepdims=True),
+    ]
+    begins = begin_of(lax.broadcasted_iota(jnp.int32, (1, seq_len), 1), starts, 4 * micro)
+    for start in range(0, seq_len, block):
+        end = start + block
+        kb, vb = k_all[start:end], v_all[start:end]
+        qs, dos = q_all[start:], do_all[start:]
+        span = seq_len - start
+        key = start + lax.broadcasted_iota(jnp.int32, (block, span), 0)
+        query = start + lax.broadcasted_iota(jnp.int32, (block, span), 1)
+        allowed = (key <= query) & (key >= begins[:, start:])
+        dks, dvs, dqs = [], [], []
+        for head in range(2):
+            mask = head_mask(kb.shape, head)
+            scores = dot_nt(jnp.where(mask, kb, 0), qs)
+            soft = jnp.exp(jnp.where(allowed, scores, -1e30) - lse[head : head + 1, start:])
+            pull = dot_nt(jnp.where(mask, vb, 0), dos)
+            ds = (soft * (pull - deltas[head][:, start:])).astype(BF16)
+            dvs.append(dot(soft.astype(BF16), dos))
+            dks.append(dot(ds, qs))
+            dqs.append(
+                lax.dot_general(ds, kb, (((0,), (0,)), ((), ())), preferred_element_type=F32)
+            )
+        low = head_mask(kb.shape, 0)
+        dk_ref[start:end] = jnp.where(low, dks[0], dks[1])
+        dv_ref[start:end] = jnp.where(low, dvs[0], dvs[1])
+        dq = jnp.where(head_mask(dqs[0].shape, 0), dqs[0], dqs[1])
+        if start == 0:
+            dq_ref[...] = dq
+        else:
+            dq_ref[start:] += dq
+    rows = lax.broadcasted_iota(jnp.int32, (seq_len, lanes), 0)
+    cos, sin = angle_rows(
+        rows, starts, 4 * micro, (tcos[...], tsin[...]), start_cos.at[micro], start_sin.at[micro]
+    )
+    for kind, ref in enumerate((dq_ref, dk_ref, dv_ref)):
+        u = ref[...]
+        if kind == 0:
+            u = u * 0.125
+        if kind < 2:
+            u = u * cos - swap_halves(u) * sin
+        out[:, kind] = u.astype(BF16).reshape(shards_n, count, lanes)
+
+
+def call_attend_back(first, starts, table, start_table, got, grads, att, lse):
+    parts, number, _, count, lanes = got.shape
+    seq_len = parts * count
+    return pl.pallas_call(
+        functools.partial(attend_back_kernel, first),
+        grid_spec=pltpu.PrefetchScalarGridSpec(
+            num_scalar_prefetch=1,
+            grid=(number,),
+            in_specs=[whole(a.shape) for a in (*table, *start_table)]
+            + [
+                pl.BlockSpec((parts, None, 3, count, lanes), lambda i, _: (0, i, 0, 0, 0)),
+                pl.BlockSpec((parts, None, count, lanes), lambda i, _: (0, first + i, 0, 0)),
+                pl.BlockSpec((parts, None, count, lanes), lambda i, _: (0, i, 0, 0)),
+                pl.BlockSpec((None, 8, seq_len), lambda i, _: (i, 0, 0)),
+            ],
+            out_specs=pl.BlockSpec((parts, None, 3, count, lanes), lambda i, _: (0, i, 0, 0, 0)),
+            scratch_shapes=[pltpu.VMEM((seq_len, lanes), F32)] * 3,
+        ),
+        out_shape=jax.ShapeDtypeStruct((parts, number, 3, count, lanes), BF16),
+        compiler_params=params(),
+        cost_estimate=cost(
+            number * 20 * seq_len * seq_len * lanes, number * 4e6, number * 2 * seq_len * seq_len
+        ),
+        name="attend_back",
+    )(starts, *table, *start_table, got, grads, att, lse)
+
+
+def mix_block(mixes, q, k):
+    return jnp.concatenate([mixes[q][0][k], mixes[q][1][k]], 0)
+
+
+def add_into(ref, cols, first, value):
+    @pl.when(first)
+    def _():
+        ref[:, cols] = value
+
+    @pl.when(jnp.logical_not(first))
+    def _():
+        ref[:, cols] += value
+
+
+def layer_kernel(pos, *refs):
+    att = [refs[0].at[:, 0], refs[0].at[:, 1], refs[1].at[:, 0]]
+    x, cot, gains, shifts = refs[2:6]
+    ups = [refs[6 + 2 * q : 8 + 2 * q] for q in range(4)]
+    downs = [refs[14 + 2 * q : 16 + 2 * q] for q in range(4)]
+    mixes = [refs[22 + 2 * q : 24 + 2 * q] for q in range(4)]
+    outputs, att_all, act, slope, keep, send, xhat1, scale1, xhat2, scale2, sums = refs[30:41]
+    normed, hidden, total = refs[41:44]
+    nz = mixes[0][0].shape[0]
+    count = refs[0].shape[2]
+    part = downs[0][0].shape[2]
+    step = pl.program_id(0)
+
+    def hand_out(index, value):
+        keep[index] = value[:, : 2 * part]
+        send[index] = value[:, 2 * part :]
+
+    @pl.when(step == 0)
+    def _():
+        for k in range(nz):
+            for dx in range(2):
+                place = ring_place(pos, k, nz) * 2 + lax.bitwise_xor(pos[3], dx)
+                for m in range(3):
+                    at = (k * 2 + dx) * 128
+                    att_all[m * count : (m + 1) * count, at : at + 128] = att[m][place]
+        for q in range(4):
+            acc = None
+            for k in range(nz):
+                term = dot(att_all[:, k * 256 : (k + 1) * 256], mix_block(mixes, q, k))
+                acc = term if acc is None else acc + term
+            total[:, q * part : (q + 1) * part] = acc
+        xhat, scale = row_stats(total[...])
+        xhat1[...] = xhat
+        scale1[...] = jnp.broadcast_to(scale, scale1.shape)
+        value = load_columns(x, pos, part).astype(F32) + xhat * gains[1:2] + shifts[1:2]
+        hidden[...] = value
+        xhat, scale = row_stats(value)
+        xhat2[...] = xhat
+        scale2[...] = jnp.broadcast_to(scale, scale2.shape)
+        value = (xhat * gains[2:3] + shifts[2:3]).astype(BF16)
+        normed[...] = value
+        hand_out(0, value)
+
+    for dx in range(2):
+        u = None
+        for q in range(4):
+            term = dot(normed[:, q * part : (q + 1) * part], ups[q][dx][...])
+            u = term if u is None else u + term
+        square = u * u
+        t = jnp.tanh(GELU_A * (u * (1.0 + GELU_B * square)))
+        half = 0.5 * (1.0 + t)
+        act[0, dx] = (u * half).astype(BF16)
+        bend = half + (0.5 * GELU_A) * u * (1.0 - t * t) * (1.0 + 3.0 * GELU_B * square)
+        slope[0, dx] = bend.astype(BF16)
+    for q in range(4):
+        term = dot(act[0, 0], downs[q][0][0]) + dot(act[0, 1], downs[q][1][0])
+        add_into(total, slice(q * part, (q + 1) * part), step == 0, term)
+
+    @pl.when(step == nz - 1)
+    def _():
+        xhat, scale = row_stats(total[...])
+        value = hidden[...] + xhat * gains[3:4] + shifts[3:4]
+        store_columns(outputs, value, pos, part)
+        grad = load_columns(cot, pos, part).astype(F32)
+        sums[0:1] = column_sum(grad * xhat)
+        sums[1:2] = column_sum(grad)
+        hand_out(1, row_pull(grad, xhat, scale, gains[3:4]).astype(BF16))
+
+
+def layer_specs(units, part, rows, nz, order):
+    def up_spec(dy, dx):
+        def index(i, pos):
+            place = lax.bitwise_xor(pos[0], dy) * 2 + lax.bitwise_xor(pos[3], dx)
+            return (place, ring_place(pos, order(i), nz), 0, 0)
+
+        return pl.BlockSpec((None, None, part, units), index)
+
+    ups = [up_spec(dy, dx) for _ in range(2) for dy in range(2) for dx in range(2)]
+    down = pl.BlockSpec((1, units, part), lambda i, pos: (order(i), 0, 0))
+    mix = pl.BlockSpec((nz, rows, part), lambda i, pos: (0, units // rows, 0))
+    return ups + [down] * 8 + [mix] * 8
+
+
+def layer_weights(ups, mixes):
+    mixes_flat = [p for pair in mixes for p in pair]
+    return [ups[0]] * 4 + [ups[1]] * 4 + mixes_flat * 2
+
+
+def call_layer(pos, att, x, cot, gains, shifts, ups, mixes):
+    tokens, width = x.shape
+    _, nz, part, units = ups[0].shape
+    rows = mixes[0][0].shape[1] - units
+    act = pl.BlockSpec((1, 2, tokens, units), lambda i, pos: (i, 0, 0, 0))
+    flat, column = (tokens, width), (tokens, 128)
+    side = (2, tokens, width // 2)
+    ffn = jax.ShapeDtypeStruct((nz, 2, tokens, units), BF16)
+    low = jax.ShapeDtypeStruct(flat, BF16)
+    return pl.pallas_call(
+        layer_kernel,
+        grid_spec=pltpu.PrefetchScalarGridSpec(
+            num_scalar_prefetch=1,
+            grid=(nz,),
+            in_specs=[whole(a.shape) for a in (*att, x, cot, gains, shifts)]
+            + layer_specs(units, part, rows, nz, lambda i: i),
+            out_specs=[whole(flat)] * 2
+            + [act] * 2
+            + [whole(side)] * 2
+            + [whole(flat), whole(column)] * 2
+            + [whole((8, width))],
+            scratch_shapes=[pltpu.VMEM(flat, BF16), pltpu.VMEM(flat, F32), pltpu.VMEM(flat, F32)],
+        ),
+        out_shape=[low, low, ffn, ffn]
+        + [jax.ShapeDtypeStruct(side, BF16)] * 2
+        + [jax.ShapeDtypeStruct(flat, F32), jax.ShapeDtypeStruct(column, F32)] * 2
+        + [jax.ShapeDtypeStruct((8, width), F32)],
+        compiler_params=params(),
+        cost_estimate=cost(
+            2 * tokens * width * (2 * nz * 2 * units + width), 40e6, tokens * nz * 2 * units
+        ),
+        name="layer",
+    )(pos, *att, x, cot, gains, shifts, *layer_weights(ups, mixes))
+
+
+def layer_back_kernel(pos, *refs):
+    cot, gains, xhat1, scale1, xhat2, scale2, slope, keep, send = refs[0:9]
+    ups = [refs[9 + 2 * q : 11 + 2 * q] for q in range(4)]
+    downs = [refs[17 + 2 * q : 19 + 2 * q] for q in range(4)]
+    mixes = [refs[25 + 2 * q : 27 + 2 * q] for q in range(4)]
+    g_up, keep_out, send_out, g_hidden, g_att, sums, total = refs[33:40]
+    nz = mixes[0][0].shape[0]
+    count = g_att.shape[2]
+    part = downs[0][0].shape[2]
+    step = pl.program_id(0)
+    g_b2 = [keep[1, :, :part], keep[1, :, part:], send[1, :, :part], send[1, :, part:]]
+    for dx in range(2):
+        g = None
+        for q in range(4):
+            term = dot_nt(g_b2[q], downs[q][dx][0])
+            g = term if g is None else g + term
+        g_up[0, dx] = (g * slope[0, dx].astype(F32)).astype(BF16)
+    for q in range(4):
+        term = dot_nt(g_up[0, 0], ups[q][0][...]) + dot_nt(g_up[0, 1], ups[q][1][...])
+        add_into(total, slice(q * part, (q + 1) * part), step == 0, term)
+
+    @pl.when(step == nz - 1)
+    def _():
+        grad = total[...]
+        xhat = xhat2[...]
+        sums[1:2] = column_sum(grad * xhat)
+        sums[3:4] = column_sum(grad)
+        grad = load_columns(cot, pos, part).astype(F32) + row_pull(
+            grad, xhat, scale2[:, 0:1], gains[2:3]
+        )
+        g_hidden[...] = grad
+        xhat = xhat1[...]
+        sums[0:1] = column_sum(grad * xhat)
+        sums[2:3] = column_sum(grad)
+        g_b1 = row_pull(grad, xhat, scale1[:, 0:1], gains[1:2]).astype(BF16)
+        keep_out[...] = g_b1[:, : 2 * part]
+        send_out[...] = g_b1[:, 2 * part :]
+        for k in range(nz):
+            acc = None
+            for q in range(4):
+                term = dot_nt(g_b1[:, q * part : (q + 1) * part], mix_block(mixes, q, k))
+                acc = term if acc is None else acc + term
+            acc = acc.astype(BF16)
+            for dx in range(2):
+                place = ring_place(pos, k, nz) * 2 + lax.bitwise_xor(pos[3], dx)
+                for m in range(3):
+                    g_att[place, m] = acc[m * count : (m + 1) * count, dx * 128 : (dx + 1) * 128]
+
+
+def call_layer_back(pos, cot, gains, kept, slope, keep, send, ups, mixes, count):
+    tokens, width = cot.shape
+    _, nz, part, units = ups[0].shape
+    rows = mixes[0][0].shape[1] - units
+    turn = nz - 1
+    act = pl.BlockSpec((1, 2, tokens, units), lambda i, pos: (turn - i, 0, 0, 0))
+    flat, half = (tokens, width), (tokens, width // 2)
+    heads = (2 * nz, tokens // count, count, rows)
+    return pl.pallas_call(
+        layer_back_kernel,
+        grid_spec=pltpu.PrefetchScalarGridSpec(
+            num_scalar_prefetch=1,
+            grid=(nz,),
+            in_specs=[whole(a.shape) for a in (cot, gains, *kept)]
+            + [act, whole(keep.shape), whole(send.shape)]
+            + layer_specs(units, part, rows, nz, lambda i: turn - i),
+            out_specs=[act, whole(half), whole(half), whole(flat), whole(heads), whole((8, width))],
+            scratch_shapes=[pltpu.VMEM(flat, F32)],
+        ),
+        out_shape=[
+            jax.ShapeDtypeStruct(slope.shape, BF16),
+            jax.ShapeDtypeStruct(half, BF16),
+            jax.ShapeDtypeStruct(half, BF16),
+            jax.ShapeDtypeStruct(flat, F32),
+            jax.ShapeDtypeStruct(heads, BF16),
+            jax.ShapeDtypeStruct((8, width), F32),
+        ],
+        compiler_params=params(),
+        cost_estimate=cost(2 * tokens * width * (2 * nz * 2 * units + width), 40e6),
+        name="layer_back",
+    )(pos, cot, gains, *kept, slope, keep, send, *layer_weights(ups, mixes))
+
+
+def place_piece(outs, dy, dx, cut, index, value):
+    if dy == 0 and dx == 0:
+        outs[0][index] = value
+        return
+    low, high = outs[1 + 2 * (2 * dy + dx - 1) :][:2]
+    step = pl.program_id(0)
+
+    @pl.when(step < cut)
+    def _():
+        low[index] = value
+
+    @pl.when(step >= cut)
+    def _():
+        high[index] = value
+
+
+def piece_specs(block, nz, cut):
+    zeros = (0,) * (len(block) - 1)
+    low = pl.BlockSpec(block, lambda i, *_: (jnp.minimum(i, cut - 1),) + zeros)
+    high = pl.BlockSpec(block, lambda i, *_: (jnp.maximum(i - cut, 0),) + zeros)
+    specs = [pl.BlockSpec(block, lambda i, *_: (i,) + zeros)] + [low, high] * 3
+    shapes = [nz] + [cut, nz - cut] * 3
+    return specs, [jax.ShapeDtypeStruct((n,) + block[1:], BF16) for n in shapes]
+
+
+def down_grad_kernel(cut, act, act2, keep, recv, *outs):
+    part = outs[0].shape[2]
+    for dx in range(2):
+        side = jnp.concatenate([jnp.transpose(act[0, dx]), jnp.transpose(act2[0, dx])], 1)
+        for dy in range(2):
+            cols = slice(dy * part, (dy + 1) * part)
+            grad = jnp.concatenate([keep[0, :, cols], recv[0, :, cols]], 0)
+            place_piece(outs, dy, dx, cut, 0, dot(side, grad).astype(BF16))
+
+
+def call_down_grad(cut, act, act2, keep, recv):
+    nz, _, tokens, units = act.shape
+    half = keep.shape[2]
+    ffn = pl.BlockSpec((1, 2, tokens, units), lambda i: (i, 0, 0, 0))
+    specs, shapes = piece_specs((1, units, half // 2), nz, cut)
+    side = pl.BlockSpec((1, tokens, half), lambda i: (1, 0, 0))
+    return pl.pallas_call(
+        functools.partial(down_grad_kernel, cut),
+        grid=(nz,),
+        in_specs=[ffn, ffn, side, side],
+        out_specs=specs,
+        out_shape=shapes,
+        compiler_params=params(),
+        cost_estimate=cost(2 * tokens * 2 * half * nz * 2 * units, 16e6),
+        name="down_grad",
+    )(act, act2, keep, recv)
+
+
+def up_grad_kernel(pos, g_up, g_up2, keep, recv, keep1, recv1, att, att2, out, flipped):
+    part, units = g_up.shape[3] // 2, g_up.shape[3]
+    tokens = g_up.shape[2]
+
+    @pl.when(pl.program_id(0) == 0)
+    def _():
+        flipped[:, :tokens] = jnp.transpose(keep[0])
+        flipped[:, tokens:] = jnp.transpose(recv[0])
+
+    side = jnp.concatenate([jnp.transpose(att[...]), jnp.transpose(att2[...])], 1)
+    for dy in range(2):
+        cols = slice(dy * part, (dy + 1) * part)
+        both = dot(side, jnp.concatenate([keep1[:, cols], recv1[:, cols]], 0)).astype(BF16)
+        for dx in range(2):
+            place = lax.bitwise_xor(pos[0], dy) * 2 + lax.bitwise_xor(pos[3], dx)
+            grad = jnp.concatenate([g_up[0, dx], g_up2[0, dx]], 0)
+            out[place, 0, :part] = dot(flipped[cols], grad).astype(BF16)
+            rows = both[dx * 128 : (dx + 1) * 128]
+            out[place, 0, part:] = jnp.concatenate([rows[:64], rows[64:]], 1)
+
+
+def call_up_grad(pos, g_up, g_up2, keep, recv, keep1, recv1, att, att2):
+    nz, _, tokens, units = g_up.shape
+    half = keep.shape[2]
+    part = half // 2
+    heads = att.shape[1] // nz
+    rows = part + heads // 4
+    ffn = pl.BlockSpec((1, 2, tokens, units), lambda i, pos: (i, 0, 0, 0))
+    side = pl.BlockSpec((1, tokens, half), lambda i, pos: (0, 0, 0))
+    head = pl.BlockSpec((tokens, heads), lambda i, pos: (0, i))
+    return pl.pallas_call(
+        up_grad_kernel,
+        grid_spec=pltpu.PrefetchScalarGridSpec(
+            num_scalar_prefetch=1,
+            grid=(nz,),
+            in_specs=[ffn, ffn, side, side, whole(keep1.shape), whole(keep1.shape), head, head],
+            out_specs=pl.BlockSpec(
+                (4, 1, rows, units), lambda i, pos: (0, ring_place(pos, i, nz), 0, 0)
+            ),
+            scratch_shapes=[pltpu.VMEM((half, 2 * tokens), BF16)],
+        ),
+        out_shape=jax.ShapeDtypeStruct((4, nz, rows, units), BF16),
+        compiler_params=params(),
+        cost_estimate=cost(2 * tokens * 2 * half * nz * 2 * units, 16e6),
+        name="up_grad",
+    )(pos, g_up, g_up2, keep, recv, keep1, recv1, att, att2)
+
+
+def load_grads(pos, grads):
+    columns = []
+    for dx in range(2):
+        place = lax.bitwise_xor(pos[3], dx)
+        for kind in range(3):
+            rows = [g[0, place, m, kind] for g in grads for m in range(g.shape[2])]
+            columns.append(jnp.concatenate(rows, 0))
+    return jnp.concatenate(columns, 1)
+
+
+def qkv_grad_kernel(cut, pos, *refs):
+    grads, keep, recv = refs[0:4], refs[4], refs[5]
+    outs, flipped = refs[6:13], refs[13]
+    part = outs[0].shape[2]
+    tokens = keep.shape[0]
+
+    @pl.when(pl.program_id(0) == 0)
+    def _():
+        flipped[:, :tokens] = jnp.transpose(keep[...])
+        flipped[:, tokens:] = jnp.transpose(recv[...])
+
+    block = load_grads(pos, grads)
+    for dy in range(2):
+        res = dot(flipped[dy * part : (dy + 1) * part], block).astype(BF16)
+        for dx in range(2):
+            for kind in range(3):
+                at = (dx * 3 + kind) * 128
+                place_piece(outs, dy, dx, cut, (0, kind), res[:, at : at + 128])
+
+
+def call_qkv_grad(cut, pos, grads, grads2, keep, recv):
+    nz, _, _, _, count, cols = grads[0].shape
+    tokens, half = keep.shape
+    part = half // 2
+    grad_specs = [pl.BlockSpec((1,) + g.shape[1:], head_index(nz)) for g in grads]
+    specs, shapes = piece_specs((1, 3, part, cols), nz, cut)
+    return pl.pallas_call(
+        functools.partial(qkv_grad_kernel, cut),
+        grid_spec=pltpu.PrefetchScalarGridSpec(
+            num_scalar_prefetch=1,
+            grid=(nz,),
+            in_specs=grad_specs * 2 + [whole(keep.shape)] * 2,
+            out_specs=specs,
+            scratch_shapes=[pltpu.VMEM((half, 2 * tokens), BF16)],
+        ),
+        out_shape=shapes,
+        compiler_params=params(),
+        cost_estimate=cost(2 * tokens * 2 * half * 3 * nz * 2 * cols, 12e6),
+        name="qkv_grad",
+    )(pos, *grads, *grads2, keep, recv)
+
+
+def input_grad_kernel(pos, *refs):
+    grads, x, gains, g_hidden = refs[0:2], refs[2], refs[3], refs[4]
+    weights = [refs[5 + 2 * q : 7 + 2 * q] for q in range(4)]
+    out, sums, total = refs[13:16]
+    part = weights[0][0].shape[2]
+    step = pl.program_id(0)
+    block = load_grads(pos, grads)
+    for q in range(4):
+        side = jnp.concatenate([weights[q][dx][0, kind] for dx in range(2) for kind in range(3)], 1)
+        term = dot_nt(block, side)
+
+        @pl.when(step == 0)
+        def _():
+            total[:, q * part : (q + 1) * part] = term
+
+        @pl.when(step > 0)
+        def _():
+            total[:, q * part : (q + 1) * part] += term
+
+    @pl.when(step == pl.num_programs(0) - 1)
+    def _():
+        grad = total[...]
+        xhat, scale = row_stats(load_columns(x, pos, part).astype(F32))
+        sums[0:1] = column_sum(grad * xhat)
+        sums[1:2] = column_sum(grad)
+        value = g_hidden[...] + row_pull(grad, xhat, scale, gains[0:1])
+        store_columns(out, value, pos, part)
+
+
+def call_input_grad(pos, grads, x, gains, g_hidden, pieces):
+    nz, _, _, _, count, cols = grads[0].shape
+    tokens, width = x.shape
+    part = width // 4
+    grad_specs = [pl.BlockSpec((1,) + g.shape[1:], head_index(nz)) for g in grads]
+    piece = pl.BlockSpec((1, 3, part, cols), lambda i, pos: (i, 0, 0, 0))
+    return pl.pallas_call(
+        input_grad_kernel,
+        grid_spec=pltpu.PrefetchScalarGridSpec(
+            num_scalar_prefetch=1,
+            grid=(nz,),
+            in_specs=grad_specs + [whole(a.shape) for a in (x, gains, g_hidden)] + [piece] * 8,
+            out_specs=[whole((tokens, width)), whole((8, width))],
+            scratch_shapes=[pltpu.VMEM((tokens, width), F32)],
+        ),
+        out_shape=[
+            jax.ShapeDtypeStruct((tokens, width), F32),
+            jax.ShapeDtypeStruct((8, width), F32),
+        ],
+        compiler_params=params(),
+        cost_estimate=cost(2 * tokens * width * 3 * nz * 2 * cols, 16e6),
+        name="input_grad",
+    )(pos, *grads, x, gains, g_hidden, *[p for pair in pieces for p in pair])
+
+
+def sum_kernel(*refs):
+    total = refs[0][...].astype(F32)
+    for ref in refs[1:-1]:
+        total = total + ref[...].astype(F32)
+    refs[-1][...] = total.astype(BF16)
+
+
+def add(*values):
+    shape = values[0].shape
+    block = pl.BlockSpec((1,) + shape[1:], lambda i: (i,) + (0,) * (len(shape) - 1))
+    return pl.pallas_call(
+        sum_kernel,
+        grid=(shape[0],),
+        in_specs=[block] * len(values),
+        out_specs=block,
+        out_shape=jax.ShapeDtypeStruct(shape, BF16),
+        compiler_params=params(),
+        cost_estimate=cost(values[0].size * len(values), 2 * values[0].size * (len(values) + 1)),
+        name="add",
+    )(*values)
+
+
+def sum_cut_kernel(cut, pos, mine, low_x, high_x, low_y, high_y, out):
+    step = pl.program_id(0)
+
+    @pl.when(step < cut)
+    def _():
+        total = mine[...].astype(F32) + low_x[...].astype(F32) + low_y[...].astype(F32)
+        out[...] = total.astype(BF16)
+
+    @pl.when(step >= cut)
+    def _():
+        total = mine[...].astype(F32) + high_x[...].astype(F32) + high_y[...].astype(F32)
+        out[...] = total.astype(BF16)
+
+
+def add_sides(cut, pos, mine, sides):
+    nz = mine.shape[0]
+    block = (1,) + mine.shape[1:]
+    specs, _ = piece_specs(block, nz, cut)
+    zeros = (0,) * (len(block) - 1)
+    return pl.pallas_call(
+        functools.partial(sum_cut_kernel, cut),
+        grid_spec=pltpu.PrefetchScalarGridSpec(
+            num_scalar_prefetch=1,
+            grid=(nz,),
+            in_specs=specs[:5],
+            out_specs=pl.BlockSpec(block, lambda i, pos: (ring_place(pos, i, nz),) + zeros),
+        ),
+        out_shape=jax.ShapeDtypeStruct(mine.shape, BF16),
+        compiler_params=params(),
+        cost_estimate=cost(mine.size * 2, 8 * mine.size),
+        name="add_sides",
+    )(pos, mine, *sides)
+
+
+def after(values, *others):
+    return lax.optimization_barrier((values, others))[0]
+
+
+def swap(values, axis):
+    return lax.ppermute(values, axis, SWAP)
+
+
+def ring(values, step, size):
+    return lax.ppermute(values, "z", [(i, (i + step) % size) for i in range(size)])
+
+
+def gather_sides(mine):
+    return swap(mine, "x"), swap(mine, "y")
+
+
+def gather_corner(over_x, over_y, cut):
+    return jnp.concatenate([swap(over_x[:cut], "y"), swap(over_y[cut:], "x")])
+
+
+def pair_up(mine, over_x, over_y, corner):
+    return [[mine, over_x], [over_y, corner]]
+
+
+def send_corner(parts):
+    return swap(parts[5], "y"), swap(parts[6], "x")
+
+
+def corner_sums(parts, corner):
+    return add(parts[1], corner[0]), add(parts[4], corner[1])
+
+
+def send_sides(parts, sums):
+    high_x, low_y = after((parts[2], parts[3]), sums)
+    return swap(sums[0], "x"), swap(high_x, "x"), swap(low_y, "y"), swap(sums[1], "y")
+
+
+def plane_norms(sums, part):
+    pieces = [sums[:, q * part : (q + 1) * part] for q in range(4)]
+    low, high = (pieces[dy] + swap(pieces[2 + dy], "c") for dy in range(2))
+    mine = low + swap(high, "y")
+    return mine + swap(mine, "x")
+
+
+def line_norms(mine):
+    mine = mine + lax.ppermute(mine, "z", [(i, i ^ 1) for i in range(4)])
+    return mine + lax.ppermute(mine, "z", [(i, i ^ 2) for i in range(4)])
+
+
+def fast_shards(inputs, doc_starts, w_qkv, w_out, w_up, w_down, norm_gains, norm_biases, cotangent):
+    pos = jnp.stack([lax.axis_index(name) for name in ("y", "c", "z", "x")]).astype(jnp.int32)
+    nz = lax.axis_size("z")
+    parts = nz * 2
+    micro, _, shard_len, width = inputs.shape
+    tokens = micro * shard_len
+    seq_len = shard_len * parts
+    part = width // 4
+    cols = w_qkv.shape[2]
+    half = nz // 2
+    starts = doc_starts.reshape(-1)
+    x = inputs.reshape(tokens, width)
+    cot = cotangent.reshape(tokens, width)
+
+    def exchange(values):
+        return lax.all_to_all(values, SEQ, 0, 0, tiled=True)
+
+    rings = [ring(w_qkv, nz - k, nz) for k in range(1, nz)]
+    norms = jnp.concatenate([norm_gains, norm_biases])
+    norms_y, norms_c = swap(norms, "y"), swap(norms, "c")
+    norms = jnp.concatenate([norms, norms_y, norms_c, swap(norms_y, "c")], 1).astype(F32)
+    gains, shifts = norms[:4], norms[4:]
+    start_table = start_tables(doc_starts[:, 0])
+    table = tables(seq_len)
+    mix = jnp.concatenate([w_down, w_out])
+    qkv_mine, mix = after((jnp.stack([w_qkv] + rings), mix), norms, start_table)
+    mix1, mix3 = (ring(after(mix, qkv_mine), k, nz) for k in (nz - 1, 1))
+    qkv_sides = after(gather_sides(qkv_mine), mix1, mix3)
+    mix2 = ring(after(mix, qkv_sides), nz - 2, nz)
+    qkv_corner = gather_corner(*qkv_sides, half)
+    qkv_other = [swap(p, "c") for p in (qkv_mine, *qkv_sides)]
+    qkv_corner = after(qkv_corner, qkv_other)
+    if O["up_z"] == 0:
+        up_mine = lax.all_gather(after(w_up, qkv_corner), "z", axis=0, tiled=False)
+    else:
+        up_mine = lax.all_gather(after(w_up, qkv_sides), "z", axis=0, tiled=False)
+    mix_mine = jnp.stack([mix, mix1, mix2, mix3])
+    if O["gate_mix"]:
+        qkv_other.append(after(swap(qkv_corner, "c"), mix_mine))
+    else:
+        qkv_other.append(swap(qkv_corner, "c"))
+    qkv = pair_up(qkv_mine, *qkv_sides, qkv_corner) + pair_up(*qkv_other)
+    first, last, keep0, send1 = call_proj(
+        pos, starts, x, gains, shifts, table, start_table, qkv, shard_len
+    )
+    if O["gate_mix"] == 0:
+        mix_mine = after(mix_mine, first)
+    mix_sides = gather_sides(mix_mine)
+    got = [None, None]
+    got[0] = exchange(first.reshape(parts, 2, 3, shard_len, cols))
+    got[1] = exchange(after(last.reshape(parts, 1, 3, shard_len, cols), got[0]))
+    mix_corner = gather_corner(*mix_sides, O["fcut"])
+    mix_other = [swap(p, "c") for p in (mix_mine, *mix_sides)]
+    att_local, lses, att = [None, None], [None, None], [None, None]
+    if O["gate_up"] == 0:
+        got[0] = after(got[0], mix_other, mix_corner)
+        up_own = lax.all_gather(after(up_mine, got[0]), ("y", "x"), axis=0, tiled=False)
+    elif O["gate_up"] == 1:
+        got[0] = after(got[0], mix_other, mix_corner, up_mine)
+        up_own = lax.all_gather(after(up_mine, mix_corner), ("y", "x"), axis=0, tiled=False)
+    elif O["gate_up"] == 2:
+        got[0] = after(got[0], mix_other, up_mine)
+        up_own = lax.all_gather(after(up_mine, mix_sides), ("y", "x"), axis=0, tiled=False)
+    elif O["gate_up"] == 3:
+        got[0] = after(got[0], mix_sides, up_mine)
+        up_own = lax.all_gather(after(up_mine, first), ("y", "x"), axis=0, tiled=False)
+    mix_other.append(swap(mix_corner, "c"))
+    att_local[0], lses[0] = call_attend(0, starts, got[0])
+    got[1] = after(got[1], att_local[0], mix_corner)
+    att[0] = exchange(att_local[0])
+    att_local[1], lses[1] = call_attend(2, starts, got[1])
+    att[0] = after(att[0], att_local[1], mix_other)
+    att[1] = exchange(after(att_local[1], att[0]))
+    mixes = pair_up(mix_mine, *mix_sides, mix_corner) + pair_up(*mix_other)
+    up_own = after(up_own, att[0])
+    ups = [up_own, swap(up_own, "c")]
+
+    res = call_layer(pos, att, x, cot, gains, shifts, ups, mixes)
+    outputs, att_all, act, slope, keep, send = res[:6]
+    kept, sums3 = res[6:10], res[10]
+    recv, act2, att_all2, recv0 = (swap(v, "c") for v in (send, act, att_all, send1))
+    res = call_layer_back(pos, cot, gains, kept, slope, keep, send, ups, mixes, shard_len)
+    g_up, keep1, send1, g_hidden, g_att, sums = res
+    act2 = after(act2, g_up)
+    grad = exchange(g_att)
+    recv1, g_up2 = swap(send1, "c"), swap(g_up, "c")
+    cut = O["bcut"]
+    down_parts = call_down_grad(cut, act, act2, keep, recv)
+    down_corner = send_corner(down_parts)
+    g_up = after(g_up, down_parts)
+    up_parts = call_up_grad(pos, g_up, g_up2, keep, recv, keep1, recv1, att_all, att_all2)
+    up_sum = lax.psum_scatter(up_parts, ("y", "x"), scatter_dimension=0, tiled=True)
+    up_sum = up_sum.reshape(up_parts.shape[1:])
+
+    back, back2 = [None, None], [None, None]
+    if O["gate_grad"] == 1:
+        grad = after(grad, up_parts)
+    elif O["gate_grad"] == 2:
+        grad = after(grad, down_parts)
+    res = call_attend_back(2, starts, table, start_table, got[1], grad, att_local[1], lses[1])
+    if O["gate_grad"] == 3:
+        res = after(res, up_parts)
+    back[1] = exchange(res)
+    grad = after(grad, res)
+    if O["gate_grad"] == 4:
+        grad = after(grad, up_parts)
+    res = call_attend_back(0, starts, table, start_table, got[0], grad, att_local[0], lses[0])
+    if O["gate_ab"]:
+        down_corner = after(down_corner, res)
+    down_sums = corner_sums(down_parts, down_corner)
+    down_sides = send_sides(down_parts, down_sums)
+    if O["gate_b1"]:
+        back[1] = after(back[1], down_sums)
+    back[0] = exchange(after(res, back[1]))
+    up_sum = lax.psum_scatter(up_sum, "z", scatter_dimension=0, tiled=False)
+    down_mine = down_parts[0]
+    if O["gate_add"]:
+        down_mine = after(down_mine, up_sum)
+    down_sum = add_sides(cut, pos, down_mine, down_sides)
+    back2[1] = swap(back[1].reshape((nz, 2) + back[1].shape[1:]), "c")
+    back[0] = after(back[0], down_sum, back2[1])
+    down_sum = lax.psum_scatter(down_sum, "z", scatter_dimension=0, tiled=False)
+
+    back = [b.reshape((nz, 2) + b.shape[1:]) for b in back]
+    back2[0] = swap(back[0], "c")
+    qkv_parts = call_qkv_grad(half, pos, back, back2, keep0, recv0)
+    back = after(back, qkv_parts)
+    qkv_corner = send_corner(qkv_parts)
+    if O["gate_us"]:
+        qkv_corner = after(qkv_corner, down_sum)
+    qkv_sums = corner_sums(qkv_parts, qkv_corner)
+    qkv_sides = send_sides(qkv_parts, qkv_sums)
+    inputs_grad, sums0 = call_input_grad(pos, after(back, qkv_sums), x, gains, g_hidden, qkv)
+    norm_sums = [sums0[:1], sums[:2], sums3[:1], sums0[1:2], sums[2:4], sums3[1:2]]
+    norm_sums = jnp.concatenate(norm_sums)
+    if O["gate_us"]:
+        qkv_sides, norm_sums = after((qkv_sides, norm_sums), norm_sums, up_sum)
+    qkv_sum = add_sides(half, pos, qkv_parts[0], qkv_sides)
+    norm_sums = line_norms(plane_norms(after(norm_sums, qkv_sum), part))
+    qkv_sum = lax.psum_scatter(qkv_sum, "z", scatter_dimension=0, tiled=False)
+    down_sum = down_sum.astype(F32)
+    up_sum, out_sum = up_sum[:part].astype(F32), up_sum[part:].astype(F32)
+    out_sum = jnp.concatenate([out_sum[:, :part], out_sum[:, part:]], 0)
+    qkv_sum = after(qkv_sum, norm_sums, down_sum, out_sum, up_sum)
+    return (
+        outputs.reshape(inputs.shape),
+        inputs_grad.reshape(inputs.shape),
+        qkv_sum.astype(F32),
+        out_sum,
+        up_sum,
+        down_sum,
+        norm_sums[:4],
+        norm_sums[4:],
+    )
+
+
+def fits_fast(mesh, inputs, w_qkv, w_up):
+    dp, tensor = mesh.shape["dp"], mesh.shape["tensor"]
+    return (
+        dp == 4
+        and tensor == 8
+        and inputs.shape[0] == 3
+        and inputs.shape[1] == dp
+        and inputs.shape[2] == 1024
+        and w_qkv.shape[1:] == (1024, 1024)
+        and w_up.shape[1] == 4096
+    )
+
+
 def solution(mesh):
     dp, tensor = mesh.shape["dp"], mesh.shape["tensor"]
     names = ("y", "c", "z", "x")
@@ -300,10 +1337,15 @@
     tokens = P(None, rows, seq, None)
     weights = (P(None, rows, seq), P(seq, rows), P(rows, seq), P(seq, rows))
     norm = P(None, rows)
-    return jax.shard_map(
-        shards,
-        mesh=fine,
-        in_specs=(tokens, P(None, rows, None)) + weights + (norm, norm, tokens),
-        out_specs=(tokens, tokens) + weights + (norm, norm),
-        check_vma=False,
-    )
+
+    def run(*arrays):
+        fast = fits_fast(mesh, arrays[0], arrays[2], arrays[4])
+        return jax.shard_map(
+            fast_shards if fast else shards,
+            mesh=fine,
+            in_specs=(tokens, P(None, rows, None)) + weights + (norm, norm, tokens),
+            out_specs=(tokens, tokens) + weights + (norm, norm),
+            check_vma=False,
+        )(*arrays)
+
+    return run

time: 1020 us -> 541 us (0.53)
  local copies, waits for them, and re-layouts: 270 us -> 15.7 us
  Pallas kernels: 0 us -> 168 us
  waiting for transfers between devices: 382 us -> 220 us
  matrix products: 134 us -> 0 us
  other arithmetic: 103 us -> 13.6 us
    all_gather x4 -> x2, waiting for transfers between devices: 187 us -> 17 us  [the longest x1 17 us: fast_shards(): lax.all_gather(after(up_mine, got[0]), ('y', 'x'), axis=0, tiled=False)]
    pallas_call x0 -> x17, Pallas kernels: none -> 168 us  [the longest x1 27.6 us: call_layer(): pl.pallas_call(layer_kernel, grid_spec=pltpu.PrefetchScalarGridSpec(num_s...]
    ppermute x8 -> x52, waiting for transfers between devices: 19.8 us -> 182 us  [the longest x44 153 us: swap(): return lax.ppermute(values, axis, SWAP)]
    dot_general x48 -> x0, matrix products: 134 us -> none  [the longest x6 15.7 us: attention_backward(): dp = jnp.einsum('hqe,hke->hqk', dob, vb, preferred_element_type=F32)]
    unnamed x16 -> x7, waiting for transfers between devices: 69.6 us -> 0.1 us
    transpose x13 -> x0, local copies, waits for them, and re-layouts: 66.6 us -> none  [the longest x1 16.2 us: shards(): qkv_all.transpose(0, 1, 4, 3, 2, 5).reshape(width, 3 * parts * hcols)]
    reshape x14 -> x1, local copies, waits for them, and re-layouts: 60.9 us -> 0.83 us  [fast_shards(): starts = doc_starts.reshape(-1)]
    unnamed x290 -> x90, local copies, waits for them, and re-layouts: 64.4 us -> 10.8 us
  transfers between devices with their start and end apart: 32 -> 63, of which waited for: 16 -> 30; matrix products, arithmetic and copies ran while one was open for 36% -> 3% of each run, Pallas kernels for 0% -> 24%
where the time goes in v3:
time: 541 us; the launch traced here: 536 us
  waiting for transfers between devices  220 us (41%)
  Pallas kernels  168 us (31%)
  starting transfers between devices  66.8 us (12%)
  blocking collectives  37.9 us (7%)
  local copies, waits for them, and re-layouts  15.7 us (3%)
  between operations  14.9 us (3%)
  other arithmetic  13.6 us (3%)
    ppermute x44, waiting for transfers between devices, swap(): return lax.ppermute(values, axis, SWAP)  153 us
    all_to_all x2, blocking collectives, exchange(): return lax.all_to_all(values, SEQ, 0, 0, tiled=True)  37.9 us
    ppermute x44, starting transfers between devices, swap(): return lax.ppermute(values, axis, SWAP)  30.4 us
    pallas_call x1, Pallas kernels, call_layer(): pl.pallas_call(layer_kernel, grid_spec=pltpu.PrefetchScalarGridSpec(num_s...  27.6 us
    ppermute x6, waiting for transfers between devices, ring(): lax.ppermute(values, 'z', [(i, (i + step) % size) for i in range(size)])  26.3 us
    pallas_call x1, Pallas kernels, call_layer_back(): pl.pallas_call(layer_back_kernel, grid_spec=pltpu.PrefetchScalarGridSpec(...  24.3 us
    all_to_all x5, starting transfers between devices, exchange(): return lax.all_to_all(values, SEQ, 0, 0, tiled=True)  22.9 us
    pallas_call x2, Pallas kernels, call_attend_back(): pl.pallas_call(functools.partial(attend_back_kernel, first), grid_spec=pl...  19.8 us
  transfers between devices with their start and end apart: 63, of which 30 were waited for; matrix products, arithmetic and copies ran while one was open for 3% of the time, Pallas kernels for 24%

profile of v3, /device:TPU:0, one launch (start us, length us, event | category | flops | bytes accessed | tf_op | source)
XLA Modules:
  0.0 536.4 jit_solution(10809093779833560490)
XLA Ops:
  25.2 6.5 %collective-permute-done.4 = bf16[3,256,128]{2,1,0:T(8,128)(2,1)S(1)} collective-permute-done((bf16[3,256,128]{2,1,0:T(8,128)(2,1)}, bf16[3,256,128]{2,1,0:T(8,128)(2,1)S(1)}, u32[]{:S(2)}, u32[]{:S(2)}) %collective-permute-start.4) | collective-permute-done | bytes 196640 | tf_op jit(solution)/shard_map/ppermute | solution.py:1123
  38.7 8.6 %collective-permute-done.9 = bf16[640,256]{1,0:T(8,128)(2,1)S(1)} collective-permute-done((bf16[640,256]{1,0:T(8,128)(2,1)S(1)}, bf16[640,256]{1,0:T(8,128)(2,1)S(1)}, u32[]{:S(2)}, u32[]{:S(2)}) %collective-permute-start.9) | collective-permute-done | bytes 327712 | tf_op jit(solution)/shard_map/ppermute | solution.py:1123
  55.5 8.0 %collective-permute-done.11 = bf16[2,3,256,128]{3,2,1,0:T(8,128)(2,1)S(1)} collective-permute-done((bf16[2,3,256,128]{3,2,1,0:T(8,128)(2,1)S(1)}, bf16[2,3,256,128]{3,2,1,0:T(8,128)(2,1)S(1)}, u32[]{:S(2)}, u32[]{:S(2)}) %collective-permute-start.11) | collective-permute-done | bytes 393248 | tf_op jit(solution)/shard_map/ppermute | solution.py:1119
  67.8 9.3 %project.1 = (bf16[4,2,2,3,128,128]{5,4,3,2,1,0:T(8,128)(2,1)}, bf16[4,2,1,3,128,128]{5,4,3,2,1,0:T(8,128)(2,1)}, bf16[384,512]{1,0:T(8,128)(2,1)}, bf16[384,512]{1,0:T(8,128)(2,1)}) custom-call(s32[4]{0:T(128)} %pad_add_fusion.pos, s32[12]{0:T(128)} %reshape.82.starts, bf16[384,1024]{1,0:T(8,128)(2,1)} %bitcast.59, ...), custom_call_target="tpu_custom_call" | custom-call | flops 483183808 | bytes 2400000 | tf_op jit(solution)/shard_map/project/pallas_call | solution.py:461
  87.2 28.3 %collective-permute-done.20.refs_16_.refs_24_.refs_19_.refs_27_ = bf16[4,640,256]{2,1,0:T(8,128)(2,1)} collective-permute-done((bf16[4,640,256]{2,1,0:T(8,128)(2,1)S(1)}, bf16[4,640,256]{2,1,0:T(8,128)(2,1)}, u32[]{:S(2)}, u32[]{:S(2)}) %collective-permute-start.20) | collective-permute-done | bytes 1310752 | tf_op jit(solution)/shard_map/ppermute | solution.py:1119
  115.5 13.6 %collective-permute-done.18.refs_15_.refs_23_.refs_18_.refs_26_ = bf16[4,640,256]{2,1,0:T(8,128)(2,1)S(1)} collective-permute-done((bf16[4,640,256]{2,1,0:T(8,128)(2,1)S(1)}, bf16[4,640,256]{2,1,0:T(8,128)(2,1)S(1)}, u32[]{:S(2)}, u32[]{:S(2)}) %collective-permute-start.18) | collective-permute-done | bytes 1310752 | tf_op jit(solution)/shard_map/ppermute | solution.py:1119
  131.9 21.5 %collective-permute-done.22 = bf16[3,640,256]{2,1,0:T(8,128)(2,1)S(1)} collective-permute-done((bf16[3,640,256]{2,1,0:T(8,128)(2,1)S(1)}, bf16[3,640,256]{2,1,0:T(8,128)(2,1)S(1)}, u32[]{:S(2)}, u32[]{:S(2)}) %collective-permute-start.22) | collective-permute-done | bytes 983072 | tf_op jit(solution)/shard_map/ppermute | solution.py:1119
  161.7 10.0 %attend.2 = (bf16[8,2,128,128]{3,2,1,0:T(8,128)(2,1)}, f32[2,8,1024]{2,1,0:T(8,128)}) custom-call(s32[12]{0:T(128)} %reshape.82.starts, bf16[8,2,3,128,128]{4,3,2,1,0:T(8,128)(2,1)} %all-to-all-done.got), custom_call_target="tpu_custom_call" | custom-call | flops 429496736 | bytes 800000 | tf_op jit(solution)/shard_map/attend/pallas_call | solution.py:523
  171.7 10.1 %all-to-all-done.2.got = bf16[8,1,3,128,128]{4,3,2,1,0:T(8,128)(2,1)S(1)} async-done(((bf16[8,1,3,128,128]{4,3,2,1,0:T(8,128)(2,1)}), bf16[8,1,3,128,128]{4,3,2,1,0:T(8,128)(2,1)S(1)}, u32[]{:S(2)}, u32[]{:S(2)}) %all-to-all-start.2) | async-done | bytes 786464 | tf_op jit(solution)/shard_map/all_to_all | solution.py:1178
  192.4 7.7 %all-to-all-done.1.refs_0_ = bf16[8,2,128,128]{3,2,1,0:T(8,128)(2,1)} async-done(((bf16[8,2,128,128]{3,2,1,0:T(8,128)(2,1)}), bf16[8,2,128,128]{3,2,1,0:T(8,128)(2,1)}, u32[]{:S(2)}, u32[]{:S(2)}) %all-to-all-start.1) | async-done | bytes 524320 | tf_op jit(solution)/shard_map/all_to_all | solution.py:1178
  200.1 17.0 %all-gather.7.cloned.1.call-done = bf16[16,256,512]{2,1,0:T(8,128)(2,1)} async-done(((bf16[4,256,512]{2,1,0:T(8,128)(2,1)}), bf16[16,256,512]{2,1,0:T(8,128)(2,1)}) %all-gather.7.cloned.1.call-update) | async-done | bytes 4194320 | tf_op jit(solution)/shard_map/all_gather | solution.py:1219
  217.2 14.0 %all_to_all.35.refs_1_ = bf16[8,1,128,128]{3,2,1,0:T(8,128)(2,1)} all-to-all(bf16[8,1,128,128]{3,2,1,0:T(8,128)(2,1)} %get-tuple-element.107.att), channel_id=1, replica_groups=mesh['y'=2,'c'=2,'z'=4,'x'=2] {'z','x'}, dimensions={0} | all-to-all | bytes 524288 | tf_op jit(solution)/shard_map/all_to_all | solution.py:1178
  231.1 27.6 %layer.1 = (bf16[384,1024]{1,0:T(8,128)(2,1)}, bf16[384,1024]{1,0:T(8,128)(2,1)}, bf16[4,2,384,512]{3,2,1,0:T(8,128)(2,1)}, bf16[4,2,384,512]{3,2,1,0:T(8,128)(2...) custom-call(s32[4]{0:T(128)} %pad_add_fusion.pos, ...), custom_call_target="tpu_custom_call" | custom-call | flops 1449551488 | bytes 8000000 | tf_op jit(solution)/shard_map/layer/pallas_call | solution.py:743
  258.8 24.3 %layer_back.1 = (bf16[4,2,384,512]{3,2,1,0:T(8,128)(2,1)}, bf16[384,512]{1,0:T(8,128)(2,1)}, bf16[384,512]{1,0:T(8,128)(2,1)}, f32[384,1024]{1,0:T(8,128)}, bf16...) custom-call(s32[4]{0:T(128)} %pad_add_fusion.pos, bf16[384,1024]{1,0:T(8,128)(2,1)} %bitcast.63, ...), custom_call_target="tpu_custom_call" | custom-call | flops 1449551488 | bytes 8000000 | tf_op jit(solution)/shard_map/layer_back/pallas_call | solution.py:826
  284.2 6.9 %collective-permute-done.27.recv = bf16[2,384,512]{2,1,0:T(8,128)(2,1)S(1)} collective-permute-done((bf16[2,384,512]{2,1,0:T(8,128)(2,1)}, bf16[2,384,512]{2,1,0:T(8,128)(2,1)S(1)}, u32[]{:S(2)}, u32[]{:S(2)}) %collective-permute-start.27) | collective-permute-done | bytes 786464 | tf_op jit(solution)/shard_map/ppermute | solution.py:1119
  292.0 18.5 %down_grad.1 = (bf16[4,512,256]{2,1,0:T(8,128)(2,1)}, bf16[3,512,256]{2,1,0:T(8,128)(2,1)}, bf16[1,512,256]{2,1,0:T(8,128)(2,1)}, bf16[3,512,256]{2,1,0:T(8,128)...) custom-call(bf16[4,2,384,512]{3,2,1,0:T(8,128)(2,1)} %get-tuple-element.121.act, ...), custom_call_target="tpu_custom_call" | custom-call | flops 644245120 | bytes 3200000 | tf_op jit(solution)/shard_map/down_grad/pallas_call | solution.py:892
  310.5 10.0 %up_grad.1 = bf16[4,4,320,512]{3,2,1,0:T(8,128)(2,1)} custom-call(s32[4]{0:T(128)} %pad_add_fusion.pos, bf16[4,2,384,512]{3,2,1,0:T(8,128)(2,1)} %get-tuple-element.130.g_up, bf16[4,2,384,512]{3,2,1,0:T(8,128)(2,1)} %collective-permute-done.28.g_up2, bf16[2,384,512]{2,1,0:T(8,128)(2,1)} %get-tuple-element.117.refs_7_.keep, bf16[2,384,512]{2,1,0:T(8,128)(2,1)} %copy-done.13, ...), custom_call_target="tpu_custom_call" | custom-call | flops 644245120 | bytes 3200000 | tf_op jit(solution)/shard_map/up_grad/pallas_call | solution.py:934
  321.6 23.9 %all_to_all.36.grad = bf16[8,3,128,128]{3,2,1,0:T(8,128)(2,1)} all-to-all(bf16[8,3,128,128]{3,2,1,0:T(8,128)(2,1)S(1)} %copy-done.21), channel_id=1, replica_groups=mesh['y'=2,'c'=2,'z'=4,'x'=2] {'z','x'}, dimensions={0} | all-to-all | bytes 1572864 | tf_op jit(solution)/shard_map/all_to_all | solution.py:1178
  345.6 7.6 %attend_back.2 = bf16[8,1,3,128,128]{4,3,2,1,0:T(8,128)(2,1)} custom-call(s32[12]{0:T(128)} %reshape.82.starts, f32[1024,128]{1,0:T(8,128)} %constant.54.clone.tcos, f32[1024,128]{1,0:T(8,128)} %constant.55.clone.tsin, f32[3,4,128]{2,1,0:T(4,128)} %get-tuple-element.205.start_cos, f32[3,4,128]{2,1,0:T(4,128)} %get-tuple-element.204.start_sin, ...), custom_call_target="tpu_custom_call" | custom-call | flops 536870912 | bytes 800000 | tf_op jit(solution)/shard_map/attend_back/pallas_call | solution.py:608
  360.5 12.2 %attend_back.3 = bf16[8,2,3,128,128]{4,3,2,1,0:T(8,128)(2,1)} custom-call(s32[12]{0:T(128)} %reshape.82.starts, f32[1024,128]{1,0:T(8,128)} %constant.54.clone.tcos, f32[1024,128]{1,0:T(8,128)} %constant.55.clone.tsin, f32[3,4,128]{2,1,0:T(4,128)} %get-tuple-element.205.start_cos, f32[3,4,128]{2,1,0:T(4,128)} %get-tuple-element.204.start_sin, ...), custom_call_target="tpu_custom_call" | custom-call | flops 1073741824 | bytes 1600000 | tf_op jit(solution)/shard_map/attend_back/pallas_call | solution.py:608
  394.3 43.4 %collective-permute-done.34.high_x = bf16[1,512,256]{2,1,0:T(8,128)(2,1)S(1)} collective-permute-done((bf16[1,512,256]{2,1,0:T(8,128)(2,1)}, bf16[1,512,256]{2,1,0:T(8,128)(2,1)S(1)}, u32[]{:S(2)}, u32[]{:S(2)}) %collective-permute-start.34) | collective-permute-done | bytes 262176 | tf_op jit(solution)/shard_map/ppermute | solution.py:1119
  451.4 9.1 %qkv_grad.1 = (bf16[4,3,256,128]{3,2,1,0:T(8,128)(2,1)}, bf16[2,3,256,128]{3,2,1,0:T(8,128)(2,1)}, bf16[2,3,256,128]{3,2,1,0:T(8,128)(2,1)}, bf16[2,3,256,128]{3...) custom-call(s32[4]{0:T(128)} %pad_add_fusion.pos, ...), custom_call_target="tpu_custom_call" | custom-call | flops 483183808 | bytes 2400000 | tf_op jit(solution)/shard_map/qkv_grad/pallas_call | solution.py:988
  462.6 9.3 %collective-permute-done.40.refs_1_ = bf16[2,3,256,128]{3,2,1,0:T(8,128)(2,1)S(1)} collective-permute-done((bf16[2,3,256,128]{3,2,1,0:T(8,128)(2,1)}, bf16[2,3,256,128]{3,2,1,0:T(8,128)(2,1)S(1)}, u32[]{:S(2)}, u32[]{:S(2)}) %collective-permute-start.40) | collective-permute-done | bytes 393248 | tf_op jit(solution)/shard_map/ppermute | solution.py:1119
  482.7 14.4 %input_grad.1 = (f32[384,1024]{1,0:T(8,128)}, f32[8,1024]{1,0:T(8,128)}) custom-call(s32[4]{0:T(128)} %pad_add_fusion.pos, bf16[4,2,2,3,128,128]{5,4,3,2,1,0:T(8,128)(2,1)} %bitcast.55, bf16[4,2,1,3,128,128]{5,4,3,2,1,0:T(8,128)(2,1)} %bitcast.58, bf16[384,1024]{1,0:T(8,128)(2,1)} %bitcast.61, f32[4,1024]{1,0:T(4,128)} %get-tuple-element.201.gains.refs_4_.refs_1_.refs_3_, ...), custom_call_target="tpu_custom_call" | custom-call | flops 483183808 | bytes 3200000 | tf_op jit(solution)/shard_map/input_grad/pallas_call | solution.py:1039
  (251 shorter events, 159.6 us)
Async XLA Ops:
  38.7 26.2 %collective-permute-start.12 = (bf16[4,3,256,128]{3,2,1,0:T(8,128)(2,1)S(1)}, bf16[4,3,256,128]{3,2,1,0:T(8,128)(2,1)S(1)}, u32[]{:S(2)}, u32[]{:S(2)}) collective-permute-start(bf16[4,3,256,128]{3,2,1,0:T(8,128)(2,1)S(1)} %pad_maximum_fusion.1.refs_0_.refs_5_), channel_id=1, source_target_pairs={{0,8},{8,0},{1,9},{9,1},{2,10},{10,2},{3,11},{11,3},{4,12},{12,4},... | collective-permute-start | bytes 2359304 | tf_op jit(solution)/shard_map/ppermute | solution.py:1119
  77.1 79.8 %all-to-all-start = ((bf16[8,2,3,128,128]{4,3,2,1,0:T(8,128)(2,1)}), bf16[8,2,3,128,128]{4,3,2,1,0:T(8,128)(2,1)}, u32[]{:S(2)}, u32[]{:S(2)}) async-start(bf16[8,2,3,128,128]{4,3,2,1,0:T(8,128)(2,1)} %bitcast.64), calls=%async_computation | async-start | bytes 3145728 | tf_op jit(solution)/shard_map/all_to_all | solution.py:1178
  81.5 75.3 %all-gather.5.cloned.1.call-start = ((), (), s32[]{:S(2)}) async-start(), calls=%async_computation.14 | async-start | bytes 1310720 | tf_op jit(solution)/shard_map/all_gather | solution.py:1196
  84.6 30.9 %collective-permute-start.20 = (bf16[4,640,256]{2,1,0:T(8,128)(2,1)S(1)}, bf16[4,640,256]{2,1,0:T(8,128)(2,1)}, u32[]{:S(2)}, u32[]{:S(2)}) collective-permute-start(bf16[4,640,256]{2,1,0:T(8,128)(2,1)S(1)} %pad_maximum_fusion.refs_14_.refs_22_.refs_17_.refs_25_), channel_id=1, source_target_pairs={{0,16},{16,0},{1,17},{17,1},{2,18},{18,2},{3,19},{19,3},{4,20},{20... | collective-permute-start | bytes 3932168 | tf_op jit(solution)/shard_map/ppermute | solution.py:1119
  86.2 42.9 %collective-permute-start.18 = (bf16[4,640,256]{2,1,0:T(8,128)(2,1)S(1)}, bf16[4,640,256]{2,1,0:T(8,128)(2,1)S(1)}, u32[]{:S(2)}, u32[]{:S(2)}) collective-permute-start(bf16[4,640,256]{2,1,0:T(8,128)(2,1)S(1)} %pad_maximum_fusion.refs_14_.refs_22_.refs_17_.refs_25_), channel_id=1, source_target_pairs={{0,1},{1,0},{2,3},{3,2},{4,5},{5,4},{6,7},{7,6},{8,9},{9,8},{10,11... | collective-permute-start | bytes 3932168 | tf_op jit(solution)/shard_map/ppermute | solution.py:1119
  87.1 130.0 %all-gather.7.cloned.1.call-start = ((), (), s32[]{:S(2)}) async-start(), calls=%async_computation.15 | async-start | bytes 5242880 | tf_op jit(solution)/shard_map/all_gather | solution.py:1219
  87.1 66.4 %collective-permute-start.17 = (bf16[4,640,256]{2,1,0:T(8,128)(2,1)S(1)}, bf16[4,640,256]{2,1,0:T(8,128)(2,1)S(1)}, u32[]{:S(2)}, u32[]{:S(2)}) collective-permute-start(bf16[4,640,256]{2,1,0:T(8,128)(2,1)S(1)} %pad_maximum_fusion.refs_14_.refs_22_.refs_17_.refs_25_), channel_id=1, source_target_pairs={{0,8},{8,0},{1,9},{9,1},{2,10},{10,2},{3,11},{11,3},{4,12},{12,4},... | collective-permute-start | bytes 3932168 | tf_op jit(solution)/shard_map/ppermute | solution.py:1119
  115.5 39.1 %collective-permute-start.21 = (bf16[4,640,256]{2,1,0:T(8,128)(2,1)}, bf16[4,640,256]{2,1,0:T(8,128)(2,1)S(1)}, u32[]{:S(2)}, u32[]{:S(2)}) collective-permute-start(bf16[4,640,256]{2,1,0:T(8,128)(2,1)} %collective-permute-done.20.refs_16_.refs_24_.refs_19_.refs_27_), channel_id=1, source_target_pairs={{0,8},{8,0},{1,9},{9,1},{2,10},{10,2},{3,11},{11,3},{4,12},{12,4},... | collective-permute-start | bytes 3932168 | tf_op jit(solution)/shard_map/ppermute | solution.py:1119
  129.2 27.7 %collective-permute-start.19 = (bf16[4,640,256]{2,1,0:T(8,128)(2,1)S(1)}, bf16[4,640,256]{2,1,0:T(8,128)(2,1)}, u32[]{:S(2)}, u32[]{:S(2)}) collective-permute-start(bf16[4,640,256]{2,1,0:T(8,128)(2,1)S(1)} %collective-permute-done.18.refs_15_.refs_23_.refs_18_.refs_26_), channel_id=1, source_target_pairs={{0,8},{8,0},{1,9},{9,1},{2,10},{10,2},{3,11},{11,3},{4,12},{12,4},... | collective-permute-start | bytes 3932168 | tf_op jit(solution)/shard_map/ppermute | solution.py:1119
  161.6 30.8 %collective-permute-start.24 = (bf16[4,640,256]{2,1,0:T(8,128)(2,1)S(1)}, bf16[4,640,256]{2,1,0:T(8,128)(2,1)S(1)}, u32[]{:S(2)}, u32[]{:S(2)}) collective-permute-start(bf16[4,640,256]{2,1,0:T(8,128)(2,1)S(1)} %copy-done.3), channel_id=1, source_target_pairs={{0,8},{8,0},{1,9},{9,1},{2,10},{10,2},{3,11},{11,3},{4,12},{12,4},... | collective-permute-start | bytes 3932168 | tf_op jit(solution)/shard_map/ppermute | solution.py:1119
  185.9 260.4 %reduce-scatter.13.cloned.1.call-start = ((), (), s32[]{:S(2)}) async-start(), calls=%async_computation.16 | async-start | bytes 6553600
  258.7 25.5 %collective-permute-start.26 = (bf16[4,2,384,512]{3,2,1,0:T(8,128)(2,1)}, bf16[4,2,384,512]{3,2,1,0:T(8,128)(2,1)S(1)}, u32[]{:S(2)}, u32[]{:S(2)}) collective-permute-start(bf16[4,2,384,512]{3,2,1,0:T(8,128)(2,1)} %get-tuple-element.121.act), channel_id=1, source_target_pairs={{0,8},{8,0},{1,9},{9,1},{2,10},{10,2},{3,11},{11,3},{4,12},{12,4},... | collective-permute-start | bytes 9437192 | tf_op jit(solution)/shard_map/ppermute | solution.py:1119
  283.1 27.4 %collective-permute-start.28 = (bf16[4,2,384,512]{3,2,1,0:T(8,128)(2,1)}, bf16[4,2,384,512]{3,2,1,0:T(8,128)(2,1)}, u32[]{:S(2)}, u32[]{:S(2)}) collective-permute-start(bf16[4,2,384,512]{3,2,1,0:T(8,128)(2,1)} %get-tuple-element.130.g_up), channel_id=1, source_target_pairs={{0,8},{8,0},{1,9},{9,1},{2,10},{10,2},{3,11},{11,3},{4,12},{12,4},... | collective-permute-start | bytes 9437192 | tf_op jit(solution)/shard_map/ppermute | solution.py:1119
  283.7 26.8 %collective-permute-start.30 = (bf16[384,1024]{1,0:T(8,128)(2,1)}, bf16[384,1024]{1,0:T(8,128)(2,1)}, u32[]{:S(2)}, u32[]{:S(2)}) collective-permute-start(bf16[384,1024]{1,0:T(8,128)(2,1)} %get-tuple-element.133.att), channel_id=1, source_target_pairs={{0,8},{8,0},{1,9},{9,1},{2,10},{10,2},{3,11},{11,3},{4,12},{12,4},... | collective-permute-start | bytes 2359304 | tf_op jit(solution)/shard_map/ppermute | solution.py:1119
  284.1 26.3 %collective-permute-start.29 = (bf16[384,512]{1,0:T(8,128)(2,1)}, bf16[384,512]{1,0:T(8,128)(2,1)}, u32[]{:S(2)}, u32[]{:S(2)}) collective-permute-start(bf16[384,512]{1,0:T(8,128)(2,1)} %get-tuple-element.132), channel_id=1, source_target_pairs={{0,8},{8,0},{1,9},{9,1},{2,10},{10,2},{3,11},{11,3},{4,12},{12,4},... | collective-permute-start | bytes 1179656 | tf_op jit(solution)/shard_map/ppermute | solution.py:1119
  353.2 32.8 %all-to-all-start.5 = ((bf16[8,1,3,128,128]{4,3,2,1,0:T(8,128)(2,1)}), bf16[8,1,3,128,128]{4,3,2,1,0:T(8,128)(2,1)S(1)}, u32[]{:S(2)}, u32[]{:S(2)}) async-start(bf16[8,1,3,128,128]{4,3,2,1,0:T(8,128)(2,1)} %attend_back.2), calls=%async_computation.5 | async-start | bytes 1572864 | tf_op jit(solution)/shard_map/all_to_all | solution.py:1178
  384.3 53.4 %collective-permute-start.35 = (bf16[3,512,256]{2,1,0:T(8,128)(2,1)}, bf16[3,512,256]{2,1,0:T(8,128)(2,1)S(1)}, u32[]{:S(2)}, u32[]{:S(2)}) collective-permute-start(bf16[3,512,256]{2,1,0:T(8,128)(2,1)} %get-tuple-element.143), channel_id=1, source_target_pairs={{0,16},{16,0},{1,17},{17,1},{2,18},{18,2},{3,19},{19,3},{4,20},{20... | collective-permute-start | bytes 2359304 | tf_op jit(solution)/shard_map/ppermute | solution.py:1119
  385.8 51.9 %collective-permute-start.33 = (bf16[3,512,256]{2,1,0:T(8,128)(2,1)}, bf16[3,512,256]{2,1,0:T(8,128)(2,1)}, u32[]{:S(2)}, u32[]{:S(2)}) collective-permute-start(bf16[3,512,256]{2,1,0:T(8,128)(2,1)} %add.82), channel_id=1, source_target_pairs={{0,1},{1,0},{2,3},{3,2},{4,5},{5,4},{6,7},{7,6},{8,9},{9,8},{10,11... | collective-permute-start | bytes 2359304 | tf_op jit(solution)/shard_map/ppermute | solution.py:1119
  386.0 60.2 %all-to-all-start.6 = ((bf16[8,2,3,128,128]{4,3,2,1,0:T(8,128)(2,1)}), bf16[8,2,3,128,128]{4,3,2,1,0:T(8,128)(2,1)S(1)}, u32[]{:S(2)}, u32[]{:S(2)}) async-start(bf16[8,2,3,128,128]{4,3,2,1,0:T(8,128)(2,1)} %attend_back.3), calls=%async_computation.6 | async-start | bytes 3145728 | tf_op jit(solution)/shard_map/all_to_all | solution.py:1178
  391.8 127.3 %reduce-scatter.7.cloned.1.call-start = ((), (), s32[]{:S(2)}) async-start(), calls=%async_computation.11 | async-start | bytes 1310720 | tf_op jit(solution)/shard_map/reduce_scatter | solution.py:1284
  391.9 45.9 %collective-permute-start.34 = (bf16[1,512,256]{2,1,0:T(8,128)(2,1)}, bf16[1,512,256]{2,1,0:T(8,128)(2,1)S(1)}, u32[]{:S(2)}, u32[]{:S(2)}) collective-permute-start(bf16[1,512,256]{2,1,0:T(8,128)(2,1)} %get-tuple-element.142), channel_id=1, source_target_pairs={{0,1},{1,0},{2,3},{3,2},{4,5},{5,4},{6,7},{7,6},{8,9},{9,8},{10,11... | collective-permute-start | bytes 786440 | tf_op jit(solution)/shard_map/ppermute | solution.py:1119
  393.8 43.9 %collective-permute-start.36 = (bf16[1,512,256]{2,1,0:T(8,128)(2,1)S(1)}, bf16[1,512,256]{2,1,0:T(8,128)(2,1)S(1)}, u32[]{:S(2)}, u32[]{:S(2)}) collective-permute-start(bf16[1,512,256]{2,1,0:T(8,128)(2,1)S(1)} %copy-done.34), channel_id=1, source_target_pairs={{0,16},{16,0},{1,17},{17,1},{2,18},{18,2},{3,19},{19,3},{4,20},{20... | collective-permute-start | bytes 786440 | tf_op jit(solution)/shard_map/ppermute | solution.py:1119
  443.6 78.4 %reduce-scatter.11.cloned.1.call-start = ((), (), s32[]{:S(2)}) async-start(), calls=%async_computation.13 | async-start | bytes 1638400 | tf_op jit(solution)/shard_map/reduce_scatter | solution.py:1277
  446.3 81.3 %reduce-scatter.9.cloned.1.call-start = ((), (), s32[]{:S(2)}) async-start(), calls=%async_computation.12 | async-start | bytes 983040 | tf_op jit(solution)/shard_map/reduce_scatter | solution.py:1302
  (83 other events, 819.3 us)
Sparse Core Ops, SparseCore 0:
  87.2 47.9 all-gather.4
  157.0 60.0 all-gather.6
  320.7 102.1 reduce-scatter.12
  443.7 27.1 reduce-scatter.6
  473.1 29.8 reduce-scatter.10
  505.3 22.2 reduce-scatter.8

commit v4 on v3

v4 whole, which is shorter than its diff:
```python
import functools
import math
import jax
import jax.numpy as jnp
import numpy as np
from jax import lax
from jax.experimental import pallas as pl
from jax.experimental.pallas import tpu as pltpu
from jax.sharding import Mesh, PartitionSpec as P
HD = 64
EPSILON = 1e-05
F32 = jnp.float32
BF16 = jnp.bfloat16
CHIPS = ('y', 'z', 'x')
SEQ = ('z', 'x')
SWAP = [(0, 1), (1, 0)]

def ln_forward(values, gain, shift):
    average = jnp.mean(values, axis=-1, keepdims=True)
    centred = values - average
    variance = jnp.mean(centred * centred, axis=-1, keepdims=True)
    scale = lax.rsqrt(variance + EPSILON)
    xhat = centred * scale
    return (xhat * gain + shift, xhat, scale)

def ln_backward(grad, xhat, scale, gain):
    e = grad * gain
    dv = scale * (e - jnp.mean(e, axis=-1, keepdims=True) - xhat * jnp.mean(e * xhat, axis=-1, keepdims=True))
    return (dv, jnp.sum(grad * xhat, axis=0), jnp.sum(grad, axis=0))

def rotate(values, cosines, sines):
    half_dim = values.shape[-1] // 2
    lower = values[..., :half_dim]
    upper = values[..., half_dim:]
    return jnp.concatenate([lower * cosines - upper * sines, upper * cosines + lower * sines], axis=-1)

def doc_layout(starts, token_index):
    inside = token_index[:, None] >= starts[None, :]
    segment = jnp.sum(inside.astype(jnp.int32), axis=1)
    begins = jnp.max(jnp.where(inside, starts[None, :], 0), axis=1)
    return (segment, token_index - begins)

def angles_of(position):
    frequency = jnp.exp(jnp.arange(HD // 2, dtype=F32) * (-2.0 * math.log(10000.0) / HD))
    angles = position.astype(F32)[..., None] * frequency
    return (jnp.cos(angles), jnp.sin(angles))

def block_mask(segment, offset, block_len, key_len):
    query_pos = jnp.arange(offset, offset + block_len, dtype=jnp.int32)
    key_pos = jnp.arange(key_len, dtype=jnp.int32)
    causal = key_pos[None, :] <= query_pos[:, None]
    return causal & (segment[offset:offset + block_len, None] == segment[None, :key_len])

def attention_forward(q, k, v, segment):
    seq_len = q.shape[1]
    block_len = min(512, seq_len)
    pieces, lses = ([], [])
    for offset in range(0, seq_len, block_len):
        end = offset + block_len
        allowed = block_mask(segment, offset, block_len, end)[None]
        scores = 0.125 * jnp.einsum('hqe,hke->hqk', q[:, offset:end], k[:, :end], preferred_element_type=F32)
        scores = jnp.where(allowed, scores, -1e+30)
        peak = jnp.max(scores, axis=-1, keepdims=True)
        lse = peak + jnp.log(jnp.sum(jnp.exp(scores - peak), axis=-1, keepdims=True))
        probs = jnp.exp(scores - lse).astype(BF16)
        pieces.append(jnp.einsum('hqk,hke->hqe', probs, v[:, :end], preferred_element_type=F32).astype(BF16))
        lses.append(lse)
    return (jnp.concatenate(pieces, axis=1), lses)

def attention_backward(q, k, v, do, lses, segment):
    seq_len = q.shape[1]
    block_len = min(512, seq_len)
    dq = []
    dk = jnp.zeros(k.shape, F32)
    dv = jnp.zeros(v.shape, F32)
    for index, offset in enumerate(range(0, seq_len, block_len)):
        end = offset + block_len
        allowed = block_mask(segment, offset, block_len, end)[None]
        qb, kb, vb, dob = (q[:, offset:end], k[:, :end], v[:, :end], do[:, offset:end])
        scores = 0.125 * jnp.einsum('hqe,hke->hqk', qb, kb, preferred_element_type=F32)
        scores = jnp.where(allowed, scores, -1e+30)
        soft = jnp.exp(scores - lses[index])
        probs = soft.astype(BF16)
        dp = jnp.einsum('hqe,hke->hqk', dob, vb, preferred_element_type=F32)
        dot = jnp.sum(soft * dp, axis=-1, keepdims=True)
        ds = (soft * (dp - dot)).astype(BF16)
        dq.append(0.125 * jnp.einsum('hqk,hke->hqe', ds, kb, preferred_element_type=F32))
        pad = ((0, 0), (0, seq_len - end), (0, 0))
        dk = dk + jnp.pad(0.125 * jnp.einsum('hqk,hqe->hke', ds, qb, preferred_element_type=F32), pad)
        dv = dv + jnp.pad(jnp.einsum('hqk,hqe->hke', probs, dob, preferred_element_type=F32), pad)
    return (jnp.concatenate(dq, axis=1), dk, dv)

def gather_both(shard):
    mine = lax.all_gather(shard, CHIPS, axis=0, tiled=False)
    return jnp.stack([mine, lax.ppermute(mine, 'c', SWAP)])

def scatter_both(partial, sizes):
    ny, nz, nx = sizes
    shard_shape = partial.shape[2:]
    low = partial.astype(BF16)
    got = lax.ppermute(low[1], 'c', SWAP)
    mine = (low[0].astype(F32) + got.astype(F32)).astype(BF16)
    mine = mine.reshape((ny, nz, nx) + shard_shape)
    mine = mine.transpose((0, 2, 1) + tuple(range(3, mine.ndim)))
    mine = mine.reshape((ny * nx, nz) + shard_shape)
    mine = lax.psum_scatter(mine, ('y', 'x'), scatter_dimension=0, tiled=False)
    return lax.psum_scatter(mine, 'z', scatter_dimension=0, tiled=False).astype(F32)

def shards(inputs, doc_starts, w_qkv, w_out, w_up, w_down, norm_gains, norm_biases, cotangent):
    ny, nz, nx = (lax.axis_size(name) for name in CHIPS)
    core = lax.axis_index('c')
    sizes = (ny, nz, nx)
    parts = nz * nx
    micro, _, shard_len, width = inputs.shape
    tokens = micro * shard_len
    seq_len = shard_len * parts
    dpart = width // (2 * ny)
    hcols = w_out.shape[0]
    heads = hcols // HD
    units = w_up.shape[1]

    def to_own(values):
        pieces = values.reshape(values.shape[:-1] + (ny, 2, dpart))
        pieces = jnp.where(core == 0, pieces, pieces[..., ::-1, :])
        return jnp.swapaxes(pieces, -3, -2).reshape(values.shape)

    def from_own(values):
        pieces = jnp.swapaxes(values.reshape(values.shape[:-1] + (2, ny, dpart)), -3, -2)
        return jnp.where(core == 0, pieces, pieces[..., ::-1, :]).reshape(values.shape)
    qkv_all = gather_both(w_qkv).reshape(2, ny, parts, 3, dpart, hcols)
    norms = jnp.stack([norm_gains, norm_biases])
    norms = gather_dp(norms, ny, dpart)
    norms = to_own(norms.astype(F32))
    gains, shifts = (norms[0], norms[1])
    out_all = gather_both(w_out).reshape(2, ny, parts, hcols, dpart)
    up_all = gather_both(w_up).reshape(2, ny, parts, dpart, units)
    down_all = gather_both(w_down).reshape(2, ny, parts, units, dpart)
    qkv_full = qkv_all.transpose(0, 1, 4, 3, 2, 5).reshape(width, 3 * parts * hcols)
    out_full = out_all.transpose(2, 3, 0, 1, 4).reshape(parts * hcols, width)
    up_full = up_all.transpose(0, 1, 3, 2, 4).reshape(width, parts * units)
    down_full = down_all.transpose(2, 3, 0, 1, 4).reshape(parts * units, width)
    x = to_own(inputs.reshape(tokens, width)).astype(F32)
    cot = to_own(cotangent.reshape(tokens, width)).astype(F32)
    place = lax.axis_index(SEQ) * shard_len + jnp.arange(shard_len, dtype=jnp.int32)
    cos_own, sin_own, cos_row, sin_row, segments = ([], [], [], [], [])
    for index in range(micro):
        starts = doc_starts[index, 0]
        c, s = angles_of(doc_layout(starts, place)[1])
        cos_own.append(c)
        sin_own.append(s)
        segment, position = doc_layout(starts, jnp.arange(seq_len, dtype=jnp.int32))
        c, s = angles_of(position)
        cos_row.append(c)
        sin_row.append(s)
        segments.append(segment)
    cos_own = jnp.concatenate(cos_own)[:, None, None]
    sin_own = jnp.concatenate(sin_own)[:, None, None]
    normed1, xhat0, scale0 = ln_forward(x, gains[0], shifts[0])
    normed1 = normed1.astype(BF16)
    projected = jnp.dot(normed1, qkv_full, preferred_element_type=F32)
    projected = projected.reshape(tokens, 3, parts * heads, HD)
    rotated = rotate(projected[:, :2], cos_own, sin_own)
    projected = jnp.concatenate([rotated, projected[:, 2:]], axis=1).astype(BF16)
    projected = projected.reshape(micro, shard_len, 3, parts, hcols).transpose(0, 3, 2, 1, 4)

    def to_heads(values):
        kinds = values.shape[1]
        got = lax.all_to_all(values, SEQ, 0, 0, tiled=True)
        got = got.reshape(parts, kinds, shard_len, heads, HD).transpose(1, 3, 0, 2, 4)
        return got.reshape(kinds, heads, seq_len, HD)

    def to_tokens(values):
        kinds = values.shape[0]
        sent = values.reshape(kinds, heads, parts, shard_len, HD).transpose(2, 0, 3, 1, 4)
        sent = sent.reshape(parts, kinds, shard_len, hcols)
        return lax.all_to_all(sent, SEQ, 0, 0, tiled=True)
    qkvs, lses, attended = ([], [], [])
    for index in range(micro):
        q, k, v = to_heads(projected[index])
        out, lse = attention_forward(q, k, v, segments[index])
        qkvs.append((q, k, v))
        lses.append(lse)
        attended.append(to_tokens(out[None])[:, 0])
    attended = jnp.stack(attended).transpose(0, 2, 1, 3).reshape(tokens, parts * hcols)
    branch1 = jnp.dot(attended, out_full, preferred_element_type=F32)
    post1, xhat1, scale1 = ln_forward(branch1, gains[1], shifts[1])
    hidden = x + post1
    normed2, xhat2, scale2 = ln_forward(hidden, gains[2], shifts[2])
    normed2 = normed2.astype(BF16)
    up_act = jnp.dot(normed2, up_full, preferred_element_type=F32)
    gated, gate_pull = jax.vjp(lambda u: jax.nn.gelu(u, approximate=True), up_act)
    activated = gated.astype(BF16)
    branch2 = jnp.dot(activated, down_full, preferred_element_type=F32)
    post2, xhat3, scale3 = ln_forward(branch2, gains[3], shifts[3])
    outputs = (hidden + post2).astype(BF16)
    grad_branch2, gain3, shift3 = ln_backward(cot, xhat3, scale3, gains[3])
    grad_branch2 = grad_branch2.astype(BF16)
    down_part = jnp.einsum('tf,td->fd', activated, grad_branch2, preferred_element_type=F32)
    down_part = down_part.astype(BF16).reshape(parts, units, 2, ny, dpart)
    down_grad = scatter_both(down_part.transpose(2, 3, 0, 1, 4).reshape(2, ny * parts, units, dpart), sizes)
    grad_act = jnp.einsum('td,fd->tf', grad_branch2, down_full, preferred_element_type=F32)
    grad_up = gate_pull(grad_act)[0].astype(BF16)
    up_part = jnp.einsum('td,tf->df', normed2, grad_up, preferred_element_type=F32)
    up_part = up_part.astype(BF16).reshape(2, ny, dpart, parts, units)
    up_grad = scatter_both(up_part.transpose(0, 1, 3, 2, 4).reshape(2, ny * parts, dpart, units), sizes)
    grad_normed2 = jnp.einsum('tf,df->td', grad_up, up_full, preferred_element_type=F32)
    extra, gain2, shift2 = ln_backward(grad_normed2, xhat2, scale2, gains[2])
    grad_hidden = cot + extra
    grad_branch1, gain1, shift1 = ln_backward(grad_hidden, xhat1, scale1, gains[1])
    grad_branch1 = grad_branch1.astype(BF16)
    grad_attended = jnp.einsum('td,fd->tf', grad_branch1, out_full, preferred_element_type=F32).astype(BF16)
    grad_attended = grad_attended.reshape(micro, shard_len, parts, 1, hcols)
    grad_attended = grad_attended.transpose(0, 2, 3, 1, 4)
    out_part = jnp.einsum('tf,td->fd', attended, grad_branch1, preferred_element_type=F32)
    out_part = out_part.astype(BF16).reshape(parts, hcols, 2, ny, dpart)
    out_grad = scatter_both(out_part.transpose(2, 3, 0, 1, 4).reshape(2, ny * parts, hcols, dpart), sizes)
    grad_projected = []
    for index in range(micro):
        do = to_heads(grad_attended[index])[0]
        q, k, v = qkvs[index]
        dq, dk, dv = attention_backward(q, k, v, do, lses[index], segments[index])
        cos, sin = (cos_row[index], -sin_row[index])
        back = jnp.stack([rotate(dq, cos, sin), rotate(dk, cos, sin), dv]).astype(BF16)
        grad_projected.append(to_tokens(back))
    grad_projected = jnp.stack(grad_projected).transpose(0, 3, 2, 1, 4)
    grad_projected = grad_projected.reshape(tokens, 3 * parts * hcols)
    qkv_part = jnp.einsum('td,te->de', normed1, grad_projected, preferred_element_type=F32)
    qkv_part = qkv_part.astype(BF16).reshape(2, ny, dpart, 3, parts, hcols)
    qkv_grad = scatter_both(qkv_part.transpose(0, 1, 4, 3, 2, 5).reshape(2, ny * parts, 3, dpart, hcols), sizes)
    grad_normed1 = jnp.einsum('te,de->td', grad_projected, qkv_full, preferred_element_type=F32)
    extra, gain0, shift0 = ln_backward(grad_normed1, xhat0, scale0, gains[0])
    inputs_grad = grad_hidden + extra
    sums = jnp.stack([gain0, gain1, gain2, gain3, shift0, shift1, shift2, shift3])
    sums = lax.psum(from_own(sums), ('y', 'c', 'z', 'x'))
    place = (lax.axis_index('y') * 2 + core) * dpart
    sums = lax.dynamic_slice_in_dim(sums, place, dpart, 1)
    return (from_own(outputs).reshape(inputs.shape), from_own(inputs_grad).reshape(inputs.shape), qkv_grad, out_grad, up_grad, down_grad, sums[:4], sums[4:])

def gather_dp(norms, ny, dpart):
    full = lax.all_gather(norms, ('y', 'c'), axis=2, tiled=True)
    return full
NT = (((1,), (1,)), ((), ()))
GELU_A = 0.7978845608
GELU_B = 0.044715
COST = 0.2

def dot(a, b):
    return jnp.dot(a, b, preferred_element_type=F32)

def dot_nt(a, b):
    return lax.dot_general(a, b, NT, preferred_element_type=F32)

def params(semantics=1):
    return pltpu.CompilerParams(dimension_semantics=('arbitrary',) * semantics, vmem_limit_bytes=60 * 1024 * 1024)

def cost(flops, size, transcendentals=0):
    return pl.CostEstimate(flops=int(flops * COST), bytes_accessed=int(size * COST), transcendentals=int(transcendentals * COST))

def whole(shape):
    return pl.BlockSpec(shape, lambda *_: (0,) * len(shape))

def swap_halves(values):
    lane = lax.broadcasted_iota(jnp.int32, values.shape, 1)
    low = lax.rem(lane, HD) < HD // 2
    return jnp.where(low, pltpu.roll(values, 96, 1), pltpu.roll(values, 32, 1))

def row_stats(values):
    average = jnp.mean(values, axis=-1, keepdims=True)
    centred = values - average
    variance = jnp.mean(centred * centred, axis=-1, keepdims=True)
    scale = lax.rsqrt(variance + EPSILON)
    return (centred * scale, scale)

def row_pull(grad, xhat, scale, gain):
    e = grad * gain
    return scale * (e - jnp.mean(e, axis=-1, keepdims=True) - xhat * jnp.mean(e * xhat, axis=-1, keepdims=True))

def column_sum(values):
    return jnp.sum(values, axis=0, keepdims=True)

def own_place(pos, q, part):
    place = lax.bitwise_xor(pos[0], q % 2) * 2 + lax.bitwise_xor(pos[1], q // 2)
    return pl.multiple_of(place * part, part)

def load_columns(ref, pos, part):
    return jnp.concatenate([ref[:, pl.ds(own_place(pos, q, part), part)] for q in range(4)], 1)

def store_columns(ref, values, pos, part):
    for q in range(4):
        ref[:, pl.ds(own_place(pos, q, part), part)] = values[:, q * part:(q + 1) * part].astype(ref.dtype)

def tables(seq_len):
    lane = np.arange(128)
    frequency = np.exp(lane % (HD // 2) * (-2.0 * math.log(10000.0) / HD))
    angle = np.arange(seq_len)[:, None] * frequency.astype(np.float32).astype(np.float64)
    sign = np.where(lane % HD < HD // 2, -1.0, 1.0)
    return (np.cos(angle).astype(np.float32), (np.sin(angle) * sign).astype(np.float32))

def start_tables(starts):
    lane = jnp.arange(128)
    frequency = jnp.exp((lane % (HD // 2)).astype(F32) * (-2.0 * math.log(10000.0) / HD))
    angle = starts.astype(F32)[..., None] * frequency
    return (jnp.cos(angle), jnp.sin(angle) * jnp.where(lane % HD < HD // 2, -1.0, 1.0))

def angle_rows(rows, starts, base, table, start_cos, start_sin):
    cb, sb = (start_cos[0:1], start_sin[0:1])
    for d in range(1, 4):
        inside = rows >= starts[base + d]
        cb = jnp.where(inside, start_cos[d:d + 1], cb)
        sb = jnp.where(inside, start_sin[d:d + 1], sb)
    tc, ts = table
    return (tc * cb + ts * sb, ts * cb - tc * sb)

def begin_of(rows, starts, base):
    begin = jnp.zeros(rows.shape, jnp.int32)
    for d in range(1, 4):
        begin = jnp.where(rows >= starts[base + d], starts[base + d], begin)
    return begin

def proj_kernel(pos, starts, x, gains, shifts, tcos, tsin, start_cos, start_sin, *refs):
    weights = [refs[2 * q:2 * q + 2] for q in range(4)]
    first, last, keep, send = refs[8:12]
    normed, cos, sin = refs[12:15]
    outs = [first.at[0, :, 0], first.at[0, :, 1], last.at[0, :, 0]]
    part = weights[0][0].shape[2]
    count = first.shape[4]

    @pl.when(pl.program_id(0) == 0)
    def _():
        xhat, _ = row_stats(load_columns(x, pos, part).astype(F32))
        value = (xhat * gains[0:1] + shifts[0:1]).astype(BF16)
        normed[...] = value
        keep[...] = value[:, :2 * part]
        send[...] = value[:, 2 * part:]
        rows = lax.broadcasted_iota(jnp.int32, (count, 128), 0) + (pos[2] * 2 + pos[3]) * count
        for m in range(3):
            at = slice(m * count, (m + 1) * count)
            cos[at], sin[at] = angle_rows(rows, starts, 4 * m, (tcos[...], tsin[...]), start_cos.at[m], start_sin.at[m])
    total = None
    for q in range(4):
        block = jnp.concatenate([weights[q][dx][0, kind] for dx in range(2) for kind in range(3)], 1)
        term = dot(normed[:, q * part:(q + 1) * part], block)
        total = term if total is None else total + term
    for dx in range(2):
        place = lax.bitwise_xor(pos[3], dx)
        for kind in range(3):
            at = (dx * 3 + kind) * 128
            u = total[:, at:at + 128]
            if kind < 2:
                u = u * cos[...] + swap_halves(u) * sin[...]
            u = u.astype(BF16)
            for m in range(3):
                outs[m][place, kind] = u[m * count:(m + 1) * count]

def ring_place(pos, i, nz):
    return lax.rem(pos[2] + i, nz)

def head_index(nz):
    return lambda i, pos, *_: (ring_place(pos, i, nz), 0, 0, 0, 0, 0)

def call_proj(pos, starts, x, gains, shifts, table, start_table, pieces, shard_len):
    tokens, width = x.shape
    nz, _, part, cols = pieces[0][0].shape
    piece = pl.BlockSpec((1, 3, part, cols), lambda i, *_: (i, 0, 0, 0))
    outs = [pl.BlockSpec((1, 2, n, 3, shard_len, cols), head_index(nz)) for n in (2, 1)]
    shapes = [jax.ShapeDtypeStruct((nz, 2, n, 3, shard_len, cols), BF16) for n in (2, 1)]
    half = (tokens, width // 2)
    rows = pl.BlockSpec((shard_len, 128), lambda i, pos, _: (pos[2] * 2 + pos[3], 0))
    return pl.pallas_call(proj_kernel, grid_spec=pltpu.PrefetchScalarGridSpec(num_scalar_prefetch=2, grid=(nz,), in_specs=[whole(a.shape) for a in (x, gains, shifts)] + [rows] * 2 + [whole(a.shape) for a in start_table] + [piece] * 8, out_specs=outs + [whole(half)] * 2, scratch_shapes=[pltpu.VMEM((tokens, width), BF16), pltpu.VMEM((tokens, 128), F32), pltpu.VMEM((tokens, 128), F32)]), out_shape=shapes + [jax.ShapeDtypeStruct(half, BF16)] * 2, compiler_params=params(), cost_estimate=cost(2 * tokens * width * 3 * nz * 2 * cols, 12000000.0), name='project')(pos, starts, x, gains, shifts, *table, *start_table, *[p for pair in pieces for p in pair])

def head_mask(shape, head):
    lane = lax.broadcasted_iota(jnp.int32, shape, 1)
    return lane < HD if head == 0 else lane >= HD

def attend_kernel(first, starts, got, out, lse_out):
    micro = first + pl.program_id(0)
    shards_n, _, count, lanes = got.shape
    seq_len = shards_n * count
    block = min(256, seq_len)
    q_all = (got[:, 0] * 0.125).reshape(seq_len, lanes)
    k_all = got[:, 1].reshape(seq_len, lanes)
    v_all = got[:, 2].reshape(seq_len, lanes)
    per = block // count
    for start in range(0, seq_len, block):
        end = start + block
        qb = q_all[start:end]
        key = lax.broadcasted_iota(jnp.int32, (block, end), 1)
        query = start + lax.broadcasted_iota(jnp.int32, (block, end), 0)
        begin = begin_of(start + lax.broadcasted_iota(jnp.int32, (block, 1), 0), starts, 4 * micro)
        allowed = (key <= query) & (key >= begin)
        results = []
        for head in range(2):
            mask = head_mask(qb.shape, head)
            scores = dot_nt(jnp.where(mask, qb, 0), k_all[:end])
            scores = jnp.where(allowed, scores, -1e+30)
            peak = jnp.max(scores, axis=-1, keepdims=True)
            e = jnp.exp(scores - peak)
            total = jnp.sum(e, axis=-1, keepdims=True)
            results.append(dot(e.astype(BF16), v_all[:end]) / total)
            lse = jnp.broadcast_to(peak + jnp.log(total), (block, 128))
            lse_out[head:head + 1, start:end] = jnp.transpose(lse)[0:1]
        mixed = jnp.where(head_mask(results[0].shape, 0), results[0], results[1]).astype(BF16)
        out[start // count:end // count] = mixed.reshape(per, count, lanes)

def call_attend(first, starts, got):
    parts, number, _, count, lanes = got.shape
    seq_len = parts * count
    return pl.pallas_call(functools.partial(attend_kernel, first), grid_spec=pltpu.PrefetchScalarGridSpec(num_scalar_prefetch=1, grid=(number,), in_specs=[pl.BlockSpec((parts, None, 3, count, lanes), lambda i, _: (0, i, 0, 0, 0))], out_specs=[pl.BlockSpec((parts, None, count, lanes), lambda i, _: (0, i, 0, 0)), pl.BlockSpec((None, 8, seq_len), lambda i, _: (i, 0, 0))]), out_shape=[jax.ShapeDtypeStruct((parts, number, count, lanes), BF16), jax.ShapeDtypeStruct((number, 8, seq_len), F32)], compiler_params=params(), cost_estimate=cost(number * 8 * seq_len * seq_len * lanes, number * 2000000.0, number * 2 * seq_len * seq_len), name='attend')(starts, got)

def attend_back_kernel(first, starts, tcos, tsin, start_cos, start_sin, got, grad, att, lse, out, dq_ref, dk_ref, dv_ref):
    micro = first + pl.program_id(0)
    shards_n, _, count, lanes = got.shape
    seq_len = shards_n * count
    block = min(256, seq_len)
    q_all = (got[:, 0] * 0.125).reshape(seq_len, lanes)
    k_all = got[:, 1].reshape(seq_len, lanes)
    v_all = got[:, 2].reshape(seq_len, lanes)
    do_all = grad[...].reshape(seq_len, lanes)
    prod = do_all.astype(F32) * att[...].reshape(seq_len, lanes).astype(F32)
    prod = jnp.transpose(prod)
    deltas = [jnp.sum(prod[:HD], axis=0, keepdims=True), jnp.sum(prod[HD:], axis=0, keepdims=True)]
    begins = begin_of(lax.broadcasted_iota(jnp.int32, (1, seq_len), 1), starts, 4 * micro)
    for start in range(0, seq_len, block):
        end = start + block
        kb, vb = (k_all[start:end], v_all[start:end])
        qs, dos = (q_all[start:], do_all[start:])
        span = seq_len - start
        key = start + lax.broadcasted_iota(jnp.int32, (block, span), 0)
        query = start + lax.broadcasted_iota(jnp.int32, (block, span), 1)
        allowed = (key <= query) & (key >= begins[:, start:])
        dks, dvs, dqs = ([], [], [])
        for head in range(2):
            mask = head_mask(kb.shape, head)
            scores = dot_nt(jnp.where(mask, kb, 0), qs)
            soft = jnp.exp(jnp.where(allowed, scores, -1e+30) - lse[head:head + 1, start:])
            pull = dot_nt(jnp.where(mask, vb, 0), dos)
            ds = (soft * (pull - deltas[head][:, start:])).astype(BF16)
            dvs.append(dot(soft.astype(BF16), dos))
            dks.append(dot(ds, qs))
            dqs.append(lax.dot_general(ds, kb, (((0,), (0,)), ((), ())), preferred_element_type=F32))
        low = head_mask(kb.shape, 0)
        dk_ref[start:end] = jnp.where(low, dks[0], dks[1])
        dv_ref[start:end] = jnp.where(low, dvs[0], dvs[1])
        dq = jnp.where(head_mask(dqs[0].shape, 0), dqs[0], dqs[1])
        if start == 0:
            dq_ref[...] = dq
        else:
            dq_ref[start:] += dq
    rows = lax.broadcasted_iota(jnp.int32, (seq_len, lanes), 0)
    cos, sin = angle_rows(rows, starts, 4 * micro, (tcos[...], tsin[...]), start_cos.at[micro], start_sin.at[micro])
    for kind, ref in enumerate((dq_ref, dk_ref, dv_ref)):
        u = ref[...]
        if kind == 0:
            u = u * 0.125
        if kind < 2:
            u = u * cos - swap_halves(u) * sin
        out[:, kind] = u.astype(BF16).reshape(shards_n, count, lanes)

def call_attend_back(first, starts, table, start_table, got, grads, att, lse):
    parts, number, _, count, lanes = got.shape
    seq_len = parts * count
    return pl.pallas_call(functools.partial(attend_back_kernel, first), grid_spec=pltpu.PrefetchScalarGridSpec(num_scalar_prefetch=1, grid=(number,), in_specs=[whole(a.shape) for a in (*table, *start_table)] + [pl.BlockSpec((parts, None, 3, count, lanes), lambda i, _: (0, i, 0, 0, 0)), pl.BlockSpec((parts, None, count, lanes), lambda i, _: (0, first + i, 0, 0)), pl.BlockSpec((parts, None, count, lanes), lambda i, _: (0, i, 0, 0)), pl.BlockSpec((None, 8, seq_len), lambda i, _: (i, 0, 0))], out_specs=pl.BlockSpec((parts, None, 3, count, lanes), lambda i, _: (0, i, 0, 0, 0)), scratch_shapes=[pltpu.VMEM((seq_len, lanes), F32)] * 3), out_shape=jax.ShapeDtypeStruct((parts, number, 3, count, lanes), BF16), compiler_params=params(), cost_estimate=cost(number * 20 * seq_len * seq_len * lanes, number * 4000000.0, number * 2 * seq_len * seq_len), name='attend_back')(starts, *table, *start_table, got, grads, att, lse)

def mix_block(mixes, q, k):
    return jnp.concatenate([mixes[q][0][k], mixes[q][1][k]], 0)

def add_into(ref, cols, first, value):

    @pl.when(first)
    def _():
        ref[:, cols] = value

    @pl.when(jnp.logical_not(first))
    def _():
        ref[:, cols] += value

def layer_kernel(pos, *refs):
    att = [refs[0].at[:, 0], refs[0].at[:, 1], refs[1].at[:, 0]]
    x, cot, gains, shifts = refs[2:6]
    ups = [refs[6 + 2 * q:8 + 2 * q] for q in range(4)]
    downs = [refs[14 + 2 * q:16 + 2 * q] for q in range(4)]
    mixes = [refs[22 + 2 * q:24 + 2 * q] for q in range(4)]
    outputs, att_all, act, slope, keep, send, xhat1, scale1, xhat2, scale2, sums = refs[30:41]
    normed, hidden, total = refs[41:44]
    nz = mixes[0][0].shape[0]
    count = refs[0].shape[2]
    part = downs[0][0].shape[2]
    step = pl.program_id(0)

    def hand_out(index, value):
        keep[index] = value[:, :2 * part]
        send[index] = value[:, 2 * part:]

    @pl.when(step == 0)
    def _():
        for k in range(nz):
            for dx in range(2):
                place = ring_place(pos, k, nz) * 2 + lax.bitwise_xor(pos[3], dx)
                for m in range(3):
                    at = (k * 2 + dx) * 128
                    att_all[m * count:(m + 1) * count, at:at + 128] = att[m][place]
        for q in range(4):
            acc = None
            for k in range(nz):
                term = dot(att_all[:, k * 256:(k + 1) * 256], mix_block(mixes, q, k))
                acc = term if acc is None else acc + term
            total[:, q * part:(q + 1) * part] = acc
        xhat, scale = row_stats(total[...])
        xhat1[...] = xhat
        scale1[...] = jnp.broadcast_to(scale, scale1.shape)
        value = load_columns(x, pos, part).astype(F32) + xhat * gains[1:2] + shifts[1:2]
        hidden[...] = value
        xhat, scale = row_stats(value)
        xhat2[...] = xhat
        scale2[...] = jnp.broadcast_to(scale, scale2.shape)
        value = (xhat * gains[2:3] + shifts[2:3]).astype(BF16)
        normed[...] = value
        hand_out(0, value)
    for dx in range(2):
        u = None
        for q in range(4):
            term = dot(normed[:, q * part:(q + 1) * part], ups[q][dx][...])
            u = term if u is None else u + term
        square = u * u
        t = jnp.tanh(GELU_A * (u * (1.0 + GELU_B * square)))
        half = 0.5 * (1.0 + t)
        act[0, dx] = (u * half).astype(BF16)
        bend = half + 0.5 * GELU_A * u * (1.0 - t * t) * (1.0 + 3.0 * GELU_B * square)
        slope[0, dx] = bend.astype(BF16)
    for q in range(4):
        term = dot(act[0, 0], downs[q][0][0]) + dot(act[0, 1], downs[q][1][0])
        add_into(total, slice(q * part, (q + 1) * part), step == 0, term)

    @pl.when(step == nz - 1)
    def _():
        xhat, scale = row_stats(total[...])
        value = hidden[...] + xhat * gains[3:4] + shifts[3:4]
        store_columns(outputs, value, pos, part)
        grad = load_columns(cot, pos, part).astype(F32)
        sums[0:1] = column_sum(grad * xhat)
        sums[1:2] = column_sum(grad)
        hand_out(1, row_pull(grad, xhat, scale, gains[3:4]).astype(BF16))

def layer_specs(units, part, rows, nz, order):

    def up_spec(dy, dx):

        def index(i, pos):
            place = lax.bitwise_xor(pos[0], dy) * 2 + lax.bitwise_xor(pos[3], dx)
            return (place, ring_place(pos, order(i), nz), 0, 0)
        return pl.BlockSpec((None, None, part, units), index)
    ups = [up_spec(dy, dx) for _ in range(2) for dy in range(2) for dx in range(2)]
    down = pl.BlockSpec((1, units, part), lambda i, pos: (order(i), 0, 0))
    mix = pl.BlockSpec((nz, rows, part), lambda i, pos: (0, units // rows, 0))
    return ups + [down] * 8 + [mix] * 8

def layer_weights(ups, mixes):
    mixes_flat = [p for pair in mixes for p in pair]
    return [ups[0]] * 4 + [ups[1]] * 4 + mixes_flat * 2

def call_layer(pos, att, x, cot, gains, shifts, ups, mixes):
    tokens, width = x.shape
    _, nz, part, units = ups[0].shape
    rows = mixes[0][0].shape[1] - units
    act = pl.BlockSpec((1, 2, tokens, units), lambda i, pos: (i, 0, 0, 0))
    flat, column = ((tokens, width), (tokens, 128))
    side = (2, tokens, width // 2)
    ffn = jax.ShapeDtypeStruct((nz, 2, tokens, units), BF16)
    low = jax.ShapeDtypeStruct(flat, BF16)
    return pl.pallas_call(layer_kernel, grid_spec=pltpu.PrefetchScalarGridSpec(num_scalar_prefetch=1, grid=(nz,), in_specs=[whole(a.shape) for a in (*att, x, cot, gains, shifts)] + layer_specs(units, part, rows, nz, lambda i: i), out_specs=[whole(flat)] * 2 + [act] * 2 + [whole(side)] * 2 + [whole(flat), whole(column)] * 2 + [whole((8, width))], scratch_shapes=[pltpu.VMEM(flat, BF16), pltpu.VMEM(flat, F32), pltpu.VMEM(flat, F32)]), out_shape=[low, low, ffn, ffn] + [jax.ShapeDtypeStruct(side, BF16)] * 2 + [jax.ShapeDtypeStruct(flat, F32), jax.ShapeDtypeStruct(column, F32)] * 2 + [jax.ShapeDtypeStruct((8, width), F32)], compiler_params=params(), cost_estimate=cost(2 * tokens * width * (2 * nz * 2 * units + width), 40000000.0, tokens * nz * 2 * units), name='layer')(pos, *att, x, cot, gains, shifts, *layer_weights(ups, mixes))

def layer_back_kernel(pos, *refs):
    cot, gains, xhat1, scale1, xhat2, scale2, slope, keep, send = refs[0:9]
    ups = [refs[9 + 2 * q:11 + 2 * q] for q in range(4)]
    downs = [refs[17 + 2 * q:19 + 2 * q] for q in range(4)]
    mixes = [refs[25 + 2 * q:27 + 2 * q] for q in range(4)]
    g_up, keep_out, send_out, g_hidden, g_att, sums, total = refs[33:40]
    nz = mixes[0][0].shape[0]
    count = g_att.shape[2]
    part = downs[0][0].shape[2]
    step = pl.program_id(0)
    g_b2 = [keep[1, :, :part], keep[1, :, part:], send[1, :, :part], send[1, :, part:]]
    for dx in range(2):
        g = None
        for q in range(4):
            term = dot_nt(g_b2[q], downs[q][dx][0])
            g = term if g is None else g + term
        g_up[0, dx] = (g * slope[0, dx].astype(F32)).astype(BF16)
    for q in range(4):
        term = dot_nt(g_up[0, 0], ups[q][0][...]) + dot_nt(g_up[0, 1], ups[q][1][...])
        add_into(total, slice(q * part, (q + 1) * part), step == 0, term)

    @pl.when(step == nz - 1)
    def _():
        grad = total[...]
        xhat = xhat2[...]
        sums[1:2] = column_sum(grad * xhat)
        sums[3:4] = column_sum(grad)
        grad = load_columns(cot, pos, part).astype(F32) + row_pull(grad, xhat, scale2[:, 0:1], gains[2:3])
        g_hidden[...] = grad
        xhat = xhat1[...]
        sums[0:1] = column_sum(grad * xhat)
        sums[2:3] = column_sum(grad)
        g_b1 = row_pull(grad, xhat, scale1[:, 0:1], gains[1:2]).astype(BF16)
        keep_out[...] = g_b1[:, :2 * part]
        send_out[...] = g_b1[:, 2 * part:]
        for k in range(nz):
            acc = None
            for q in range(4):
                term = dot_nt(g_b1[:, q * part:(q + 1) * part], mix_block(mixes, q, k))
                acc = term if acc is None else acc + term
            acc = acc.astype(BF16)
            for dx in range(2):
                place = ring_place(pos, k, nz) * 2 + lax.bitwise_xor(pos[3], dx)
                for m in range(3):
                    g_att[place, m] = acc[m * count:(m + 1) * count, dx * 128:(dx + 1) * 128]

def call_layer_back(pos, cot, gains, kept, slope, keep, send, ups, mixes, count):
    tokens, width = cot.shape
    _, nz, part, units = ups[0].shape
    rows = mixes[0][0].shape[1] - units
    turn = nz - 1
    act = pl.BlockSpec((1, 2, tokens, units), lambda i, pos: (turn - i, 0, 0, 0))
    flat, half = ((tokens, width), (tokens, width // 2))
    heads = (2 * nz, tokens // count, count, rows)
    return pl.pallas_call(layer_back_kernel, grid_spec=pltpu.PrefetchScalarGridSpec(num_scalar_prefetch=1, grid=(nz,), in_specs=[whole(a.shape) for a in (cot, gains, *kept)] + [act, whole(keep.shape), whole(send.shape)] + layer_specs(units, part, rows, nz, lambda i: turn - i), out_specs=[act] + [whole(v) for v in (half, half, flat, heads, (8, width))], scratch_shapes=[pltpu.VMEM(flat, F32)]), out_shape=[jax.ShapeDtypeStruct(slope.shape, BF16), jax.ShapeDtypeStruct(half, BF16), jax.ShapeDtypeStruct(half, BF16), jax.ShapeDtypeStruct(flat, F32), jax.ShapeDtypeStruct(heads, BF16), jax.ShapeDtypeStruct((8, width), F32)], compiler_params=params(), cost_estimate=cost(2 * tokens * width * (2 * nz * 2 * units + width), 40000000.0), name='layer_back')(pos, cot, gains, *kept, slope, keep, send, *layer_weights(ups, mixes))

def place_piece(outs, dy, dx, cut, index, value):
    if dy == 0 and dx == 0:
        outs[0][index] = value
        return
    if cut is None:
        outs[2 * dy + dx][index] = value
        return
    low, high = outs[1 + 2 * (2 * dy + dx - 1):][:2]
    step = pl.program_id(0)

    @pl.when(step < cut)
    def _():
        low[index] = value

    @pl.when(step >= cut)
    def _():
        high[index] = value

def piece_specs(block, nz, cut):
    zeros = (0,) * (len(block) - 1)
    if cut is None:
        spec = pl.BlockSpec(block, lambda i, *_: (i,) + zeros)
        return ([spec] * 4, [jax.ShapeDtypeStruct((nz,) + block[1:], BF16)] * 4)
    low = pl.BlockSpec(block, lambda i, *_: (jnp.minimum(i, cut - 1),) + zeros)
    high = pl.BlockSpec(block, lambda i, *_: (jnp.maximum(i - cut, 0),) + zeros)
    specs = [pl.BlockSpec(block, lambda i, *_: (i,) + zeros)] + [low, high] * 3
    shapes = [nz] + [cut, nz - cut] * 3
    return (specs, [jax.ShapeDtypeStruct((n,) + block[1:], BF16) for n in shapes])

def down_grad_kernel(pos, act, act2, keep, recv, out):
    part = out.shape[3]
    for dx in range(2):
        side = jnp.concatenate([jnp.transpose(act[0, dx]), jnp.transpose(act2[0, dx])], 1)
        for dy in range(2):
            cols = slice(dy * part, (dy + 1) * part)
            grad = jnp.concatenate([keep[0, :, cols], recv[0, :, cols]], 0)
            place = lax.bitwise_xor(pos[0], dy) * 2 + lax.bitwise_xor(pos[3], dx)
            out[place, 0] = dot(side, grad).astype(BF16)

def call_down_grad(pos, act, act2, keep, recv):
    nz, _, tokens, units = act.shape
    half = keep.shape[2]
    part = half // 2
    ffn = pl.BlockSpec((1, 2, tokens, units), lambda i, pos: (i, 0, 0, 0))
    side = pl.BlockSpec((1, tokens, half), lambda i, pos: (1, 0, 0))
    return pl.pallas_call(down_grad_kernel, grid_spec=pltpu.PrefetchScalarGridSpec(num_scalar_prefetch=1, grid=(nz,), in_specs=[ffn, ffn, side, side], out_specs=pl.BlockSpec((4, 1, units, part), lambda i, pos: (0, ring_place(pos, i, nz), 0, 0))), out_shape=jax.ShapeDtypeStruct((4, nz, units, part), BF16), compiler_params=params(), cost_estimate=cost(2 * tokens * 2 * half * nz * 2 * units, 16000000.0), name='down_grad')(pos, act, act2, keep, recv)

def up_grad_kernel(cut, g_up, g_up2, keep, recv, keep1, recv1, att, att2, *refs):
    outs, flipped = (refs[:-1], refs[-1])
    part, units = (g_up.shape[3] // 2, g_up.shape[3])
    tokens = g_up.shape[2]

    @pl.when(pl.program_id(0) == 0)
    def _():
        flipped[:, :tokens] = jnp.transpose(keep[0])
        flipped[:, tokens:] = jnp.transpose(recv[0])
    side = jnp.concatenate([jnp.transpose(att[...]), jnp.transpose(att2[...])], 1)
    for dy in range(2):
        cols = slice(dy * part, (dy + 1) * part)
        both = dot(side, jnp.concatenate([keep1[:, cols], recv1[:, cols]], 0)).astype(BF16)
        for dx in range(2):
            grad = jnp.concatenate([g_up[0, dx], g_up2[0, dx]], 0)
            value = dot(flipped[cols], grad).astype(BF16)
            rows = both[dx * 128:(dx + 1) * 128]
            rows = jnp.concatenate([rows[:64], rows[64:]], 1)
            place_piece(outs, dy, dx, cut, 0, jnp.concatenate([value, rows], 0))

def call_up_grad(cut, g_up, g_up2, keep, recv, keep1, recv1, att, att2):
    nz, _, tokens, units = g_up.shape
    half = keep.shape[2]
    part = half // 2
    heads = att.shape[1] // nz
    ffn = pl.BlockSpec((1, 2, tokens, units), lambda i: (i, 0, 0, 0))
    side = pl.BlockSpec((1, tokens, half), lambda i: (0, 0, 0))
    head = pl.BlockSpec((tokens, heads), lambda i: (0, i))
    specs, shapes = piece_specs((1, part + heads // 4, units), nz, cut)
    return pl.pallas_call(functools.partial(up_grad_kernel, cut), grid=(nz,), in_specs=[ffn, ffn, side, side, whole(keep1.shape), whole(keep1.shape), head, head], out_specs=specs, out_shape=shapes, scratch_shapes=[pltpu.VMEM((half, 2 * tokens), BF16)], compiler_params=params(), cost_estimate=cost(2 * tokens * 2 * half * nz * 2 * units, 16000000.0), name='up_grad')(g_up, g_up2, keep, recv, keep1, recv1, att, att2)

def load_grads(pos, grads):
    columns = []
    for dx in range(2):
        place = lax.bitwise_xor(pos[3], dx)
        for kind in range(3):
            rows = [g[0, place, m, kind] for g in grads for m in range(g.shape[2])]
            columns.append(jnp.concatenate(rows, 0))
    return jnp.concatenate(columns, 1)

def qkv_grad_kernel(cut, pos, *refs):
    grads, keep, recv = (refs[0:4], refs[4], refs[5])
    outs, flipped = (refs[6:-1], refs[-1])
    part = outs[0].shape[2]
    tokens = keep.shape[0]

    @pl.when(pl.program_id(0) == 0)
    def _():
        flipped[:, :tokens] = jnp.transpose(keep[...])
        flipped[:, tokens:] = jnp.transpose(recv[...])
    block = load_grads(pos, grads)
    for dy in range(2):
        res = dot(flipped[dy * part:(dy + 1) * part], block).astype(BF16)
        for dx in range(2):
            for kind in range(3):
                at = (dx * 3 + kind) * 128
                place_piece(outs, dy, dx, cut, (0, kind), res[:, at:at + 128])

def call_qkv_grad(cut, pos, grads, grads2, keep, recv):
    nz, _, _, _, count, cols = grads[0].shape
    tokens, half = keep.shape
    part = half // 2
    grad_specs = [pl.BlockSpec((1,) + g.shape[1:], head_index(nz)) for g in grads]
    specs, shapes = piece_specs((1, 3, part, cols), nz, cut)
    return pl.pallas_call(functools.partial(qkv_grad_kernel, cut), grid_spec=pltpu.PrefetchScalarGridSpec(num_scalar_prefetch=1, grid=(nz,), in_specs=grad_specs * 2 + [whole(keep.shape)] * 2, out_specs=specs, scratch_shapes=[pltpu.VMEM((half, 2 * tokens), BF16)]), out_shape=shapes, compiler_params=params(), cost_estimate=cost(2 * tokens * 2 * half * 3 * nz * 2 * cols, 12000000.0), name='qkv_grad')(pos, *grads, *grads2, keep, recv)

def input_grad_kernel(pos, *refs):
    grads, x, gains, g_hidden = (refs[0:2], refs[2], refs[3], refs[4])
    weights = [refs[5 + 2 * q:7 + 2 * q] for q in range(4)]
    out, sums, total = refs[13:16]
    part = weights[0][0].shape[2]
    step = pl.program_id(0)
    block = load_grads(pos, grads)
    for q in range(4):
        side = jnp.concatenate([weights[q][dx][0, kind] for dx in range(2) for kind in range(3)], 1)
        term = dot_nt(block, side)

        @pl.when(step == 0)
        def _():
            total[:, q * part:(q + 1) * part] = term

        @pl.when(step > 0)
        def _():
            total[:, q * part:(q + 1) * part] += term

    @pl.when(step == pl.num_programs(0) - 1)
    def _():
        grad = total[...]
        xhat, scale = row_stats(load_columns(x, pos, part).astype(F32))
        sums[0:1] = column_sum(grad * xhat)
        sums[1:2] = column_sum(grad)
        value = g_hidden[...] + row_pull(grad, xhat, scale, gains[0:1])
        store_columns(out, value, pos, part)

def call_input_grad(pos, grads, x, gains, g_hidden, pieces):
    nz, _, _, _, count, cols = grads[0].shape
    tokens, width = x.shape
    part = width // 4
    grad_specs = [pl.BlockSpec((1,) + g.shape[1:], head_index(nz)) for g in grads]
    piece = pl.BlockSpec((1, 3, part, cols), lambda i, pos: (i, 0, 0, 0))
    return pl.pallas_call(input_grad_kernel, grid_spec=pltpu.PrefetchScalarGridSpec(num_scalar_prefetch=1, grid=(nz,), in_specs=grad_specs + [whole(a.shape) for a in (x, gains, g_hidden)] + [piece] * 8, out_specs=[whole((tokens, width)), whole((8, width))], scratch_shapes=[pltpu.VMEM((tokens, width), F32)]), out_shape=[jax.ShapeDtypeStruct((tokens, width), F32), jax.ShapeDtypeStruct((8, width), F32)], compiler_params=params(), cost_estimate=cost(2 * tokens * width * 3 * nz * 2 * cols, 16000000.0), name='input_grad')(pos, *grads, x, gains, g_hidden, *[p for pair in pieces for p in pair])

def sum_kernel(*refs):
    total = refs[0][...].astype(F32)
    for ref in refs[1:-1]:
        total = total + ref[...].astype(F32)
    refs[-1][...] = total.astype(BF16)

def add(*values):
    shape = values[0].shape
    block = pl.BlockSpec((1,) + shape[1:], lambda i: (i,) + (0,) * (len(shape) - 1))
    return pl.pallas_call(sum_kernel, grid=(shape[0],), in_specs=[block] * len(values), out_specs=block, out_shape=jax.ShapeDtypeStruct(shape, BF16), compiler_params=params(), cost_estimate=cost(values[0].size * len(values), 2 * values[0].size * (len(values) + 1)), name='add')(*values)

def sum_cut_kernel(cut, pos, mine, low_x, high_x, low_y, high_y, out):
    step = pl.program_id(0)

    @pl.when(step < cut)
    def _():
        total = mine[...].astype(F32) + low_x[...].astype(F32) + low_y[...].astype(F32)
        out[...] = total.astype(BF16)

    @pl.when(step >= cut)
    def _():
        total = mine[...].astype(F32) + high_x[...].astype(F32) + high_y[...].astype(F32)
        out[...] = total.astype(BF16)

def sum_ring_kernel(pos, *refs):
    sum_kernel(*refs)

def send_direct(parts):
    corner = lax.ppermute(parts[3], ('y', 'x'), [(i, 3 - i) for i in range(4)])
    return (corner, swap(parts[1], 'x'), swap(parts[2], 'y'))

def add_direct(pos, values):
    shape = values[0].shape
    nz = shape[0]
    block = (1,) + shape[1:]
    zeros = (0,) * (len(block) - 1)
    return pl.pallas_call(sum_ring_kernel, grid_spec=pltpu.PrefetchScalarGridSpec(num_scalar_prefetch=1, grid=(nz,), in_specs=[pl.BlockSpec(block, lambda i, pos: (i,) + zeros)] * len(values), out_specs=pl.BlockSpec(block, lambda i, pos: (ring_place(pos, i, nz),) + zeros)), out_shape=jax.ShapeDtypeStruct(shape, BF16), compiler_params=params(), cost_estimate=cost(values[0].size * 4, 10 * values[0].size), name='add_direct')(pos, *values)

def add_sides(cut, pos, mine, sides, ordered=True):
    nz = mine.shape[0]
    block = (1,) + mine.shape[1:]
    specs, _ = piece_specs(block, nz, cut)
    zeros = (0,) * (len(block) - 1)
    return pl.pallas_call(functools.partial(sum_cut_kernel, cut), grid_spec=pltpu.PrefetchScalarGridSpec(num_scalar_prefetch=1, grid=(nz,), in_specs=specs[:5], out_specs=pl.BlockSpec(block, lambda i, pos: (ring_place(pos, i, nz) if ordered else i,) + zeros)), out_shape=jax.ShapeDtypeStruct(mine.shape, BF16), compiler_params=params(), cost_estimate=cost(mine.size * 2, 8 * mine.size), name='add_sides')(pos, mine, *sides)

def after(values, *others):
    return lax.optimization_barrier((values, others))[0]

def swap(values, axis):
    return lax.ppermute(values, axis, SWAP)

def ring(values, step, size):
    return lax.ppermute(values, 'z', [(i, (i + step) % size) for i in range(size)])

def gather_sides(mine):
    return (swap(mine, 'x'), swap(mine, 'y'))

def gather_corner(over_x, over_y, cut):
    return jnp.concatenate([swap(over_x[:cut], 'y'), swap(over_y[cut:], 'x')])

def pair_up(mine, over_x, over_y, corner):
    return [[mine, over_x], [over_y, corner]]

def send_corner(parts):
    return (swap(parts[5], 'y'), swap(parts[6], 'x'))

def add_pair_kernel(a, b, c, d, first, second):
    first[...] = (a[...].astype(F32) + b[...].astype(F32)).astype(BF16)
    second[...] = (c[...].astype(F32) + d[...].astype(F32)).astype(BF16)

def corner_sums(parts, corner):
    if parts[1].shape != parts[4].shape:
        return (add(parts[1], corner[0]), add(parts[4], corner[1]))
    shape = parts[1].shape
    block = pl.BlockSpec((1,) + shape[1:], lambda i: (i,) + (0,) * (len(shape) - 1))
    return pl.pallas_call(add_pair_kernel, grid=(shape[0],), in_specs=[block] * 4, out_specs=[block] * 2, out_shape=[jax.ShapeDtypeStruct(shape, BF16)] * 2, compiler_params=params(), cost_estimate=cost(parts[1].size * 4, parts[1].size * 12), name='add_pair')(parts[1], corner[0], parts[4], corner[1])

def send_sides(parts, sums):
    high_x, low_y = after((parts[2], parts[3]), sums)
    return (swap(sums[0], 'x'), swap(high_x, 'x'), swap(low_y, 'y'), swap(sums[1], 'y'))

def plane_norms(sums, part):
    pieces = [sums[:, q * part:(q + 1) * part] for q in range(4)]
    low, high = (pieces[dy] + swap(pieces[2 + dy], 'c') for dy in range(2))
    mine = low + swap(high, 'y')
    return mine + swap(mine, 'x')

def line_norms(mine):
    mine = mine + lax.ppermute(mine, 'z', [(i, i ^ 1) for i in range(4)])
    return mine + lax.ppermute(mine, 'z', [(i, i ^ 2) for i in range(4)])

def fast_shards(inputs, doc_starts, w_qkv, w_out, w_up, w_down, norm_gains, norm_biases, cotangent):
    pos = jnp.stack([lax.axis_index(name) for name in ('y', 'c', 'z', 'x')]).astype(jnp.int32)
    nz = lax.axis_size('z')
    parts = nz * 2
    micro, _, shard_len, width = inputs.shape
    tokens = micro * shard_len
    seq_len = shard_len * parts
    part = width // 4
    cols = w_qkv.shape[2]
    half = nz // 2
    starts = doc_starts.reshape(-1)
    x = inputs.reshape(tokens, width)
    cot = cotangent.reshape(tokens, width)

    def exchange(values):
        return lax.all_to_all(values, SEQ, 0, 0, tiled=True)
    rings = [ring(w_qkv, nz - k, nz) for k in range(1, nz)]
    norms = jnp.concatenate([norm_gains, norm_biases])
    norms_y, norms_c = (swap(norms, 'y'), swap(norms, 'c'))
    norms = jnp.concatenate([norms, norms_y, norms_c, swap(norms_y, 'c')], 1).astype(F32)
    gains, shifts = (norms[:4], norms[4:])
    start_table = start_tables(doc_starts[:, 0])
    table = tables(seq_len)
    mix = jnp.concatenate([w_down, w_out])
    qkv_mine, mix = after((jnp.stack([w_qkv] + rings), mix), norms, start_table)
    mix1, mix3 = (ring(after(mix, qkv_mine), k, nz) for k in (nz - 1, 1))
    qkv_sides = after(gather_sides(qkv_mine), mix1, mix3)
    mix2 = ring(after(mix, qkv_sides), nz - 2, nz)
    qkv_corner = gather_corner(*qkv_sides, half)
    qkv_other = [swap(p, 'c') for p in (qkv_mine, *qkv_sides)]
    qkv_corner = after(qkv_corner, qkv_other)
    up_mine = lax.all_gather(after(w_up, qkv_corner), 'z', axis=0, tiled=False)
    mix_mine = jnp.stack([mix, mix1, mix2, mix3])
    qkv_other.append(swap(qkv_corner, 'c'))
    qkv = pair_up(qkv_mine, *qkv_sides, qkv_corner) + pair_up(*qkv_other)
    first, last, keep0, send1 = call_proj(pos, starts, x, gains, shifts, table, start_table, qkv, shard_len)
    mix_mine = after(mix_mine, first)
    mix_sides = gather_sides(mix_mine)
    got = [None, None]
    got[0] = exchange(first.reshape(parts, 2, 3, shard_len, cols))
    got[1] = exchange(after(last.reshape(parts, 1, 3, shard_len, cols), got[0]))
    mix_corner = gather_corner(*mix_sides, 3)
    mix_other = [swap(p, 'c') for p in (mix_mine, *mix_sides)]
    att_local, lses, att = ([None, None], [None, None], [None, None])
    got[0] = after(got[0], mix_other, mix_corner)
    up_own = lax.all_gather(after(up_mine, got[0]), ('y', 'x'), axis=0, tiled=False)
    mix_other.append(swap(mix_corner, 'c'))
    att_local[0], lses[0] = call_attend(0, starts, got[0])
    got[1] = after(got[1], att_local[0], mix_corner)
    att[0] = exchange(att_local[0])
    att_local[1], lses[1] = call_attend(2, starts, got[1])
    att[0] = after(att[0], att_local[1], mix_other)
    att[1] = exchange(after(att_local[1], att[0]))
    mixes = pair_up(mix_mine, *mix_sides, mix_corner) + pair_up(*mix_other)
    up_own = after(up_own, att[1])
    ups = [up_own, swap(up_own, 'c')]
    res = call_layer(pos, att, x, cot, gains, shifts, ups, mixes)
    outputs, att_all, act, slope, keep, send = res[:6]
    kept, sums3 = (res[6:10], res[10])
    recv, act2, att_all2, recv0 = (swap(v, 'c') for v in (send, act, att_all, send1))
    res = call_layer_back(pos, cot, gains, kept, slope, keep, send, ups, mixes, shard_len)
    g_up, keep1, send1, g_hidden, g_att, sums = res
    back, back2 = ([None, None], [None, None])
    recv1, g_up2 = (swap(send1, 'c'), swap(g_up, 'c'))
    act2 = after(act2, g_up)
    down_parts = call_down_grad(pos, act, act2, keep, recv)
    down_sum = lax.psum_scatter(down_parts, ('y', 'x'), scatter_dimension=0, tiled=True)
    down_sum = down_sum.reshape(down_parts.shape[1:])
    g_up = after(g_up, down_parts)
    grad = exchange(g_att)
    grad = after(grad, down_parts)
    res2 = call_attend_back(2, starts, table, start_table, got[1], grad, att_local[1], lses[1])
    back[1] = exchange(res2)
    grad = after(grad, res2)
    res = call_attend_back(0, starts, table, start_table, got[0], grad, att_local[0], lses[0])
    up_parts = call_up_grad(None, after(g_up, res), g_up2, keep, recv, keep1, recv1, att_all, att_all2)
    up_sent = send_direct(up_parts)
    back[1] = after(back[1], res)
    back[0] = exchange(after(res, back[1]))
    back2[1] = swap(back[1].reshape((nz, 2) + back[1].shape[1:]), 'c')
    back[0] = after(back[0], down_sum)
    down_sum = lax.psum_scatter(down_sum, 'z', scatter_dimension=0, tiled=False)
    back[0] = after(back[0], back2[1], up_parts)
    back[0] = after(back[0], up_sent[1], up_sent[2])
    back = [b.reshape((nz, 2) + b.shape[1:]) for b in back]
    back2[0] = swap(back[0], 'c')
    qkv_cut = half
    qkv_parts = call_qkv_grad(qkv_cut, pos, back, back2, keep0, recv0)
    back = after(back, qkv_parts)
    up_sent = after(up_sent, qkv_parts)
    qkv_corner = send_corner(qkv_parts)
    qkv_sums = corner_sums(qkv_parts, qkv_corner)
    qkv_sent = send_sides(qkv_parts, qkv_sums)
    inputs_grad, sums0 = call_input_grad(pos, after(back, qkv_sums), x, gains, g_hidden, qkv)
    up_sum = add_direct(pos, (up_parts[0], *up_sent))
    qkv_sent = after(qkv_sent, up_sum)
    up_sum = lax.psum_scatter(up_sum, 'z', scatter_dimension=0, tiled=False)
    norm_sums = [sums0[:1], sums[:2], sums3[:1], sums0[1:2], sums[2:4], sums3[1:2]]
    norm_sums = jnp.concatenate(norm_sums)
    qkv_sent, norm_sums = after((qkv_sent, norm_sums), norm_sums, down_sum)
    qkv_sum = add_sides(half, pos, qkv_parts[0], qkv_sent, True)
    norm_sums = line_norms(plane_norms(after(norm_sums, qkv_sum), part))
    qkv_sum = lax.psum_scatter(qkv_sum, 'z', scatter_dimension=0, tiled=False)
    down_sum = down_sum.astype(F32)
    up_sum, out_sum = (up_sum[:part].astype(F32), up_sum[part:].astype(F32))
    out_sum = jnp.concatenate([out_sum[:, :part], out_sum[:, part:]], 0)
    qkv_sum = after(qkv_sum, norm_sums, down_sum, out_sum, up_sum)
    return (outputs.reshape(inputs.shape), inputs_grad.reshape(inputs.shape), qkv_sum.astype(F32), out_sum, up_sum, down_sum, norm_sums[:4], norm_sums[4:])

def fits_fast(mesh, inputs, w_qkv, w_up):
    dp, tensor = (mesh.shape['dp'], mesh.shape['tensor'])
    return dp == 4 and tensor == 8 and (inputs.shape[0] == 3) and (inputs.shape[1] == dp) and (inputs.shape[2] == 1024) and (w_qkv.shape[1:] == (1024, 1024)) and (w_up.shape[1] == 4096)

def solution(mesh):
    dp, tensor = (mesh.shape['dp'], mesh.shape['tensor'])
    names = ('y', 'c', 'z', 'x')
    fine = Mesh(mesh.devices.reshape(dp // 2, 2, 4, tensor // 4), names)
    rows, seq = (('y', 'c'), ('z', 'x'))
    tokens = P(None, rows, seq, None)
    weights = (P(None, rows, seq), P(seq, rows), P(rows, seq), P(seq, rows))
    norm = P(None, rows)

    def run(*arrays):
        fast = fits_fast(mesh, arrays[0], arrays[2], arrays[4])
        return jax.shard_map(fast_shards if fast else shards, mesh=fine, in_specs=(tokens, P(None, rows, None)) + weights + (norm, norm, tokens), out_specs=(tokens, tokens) + weights + (norm, norm), check_vma=False)(*arrays)
    return run
```

time: 541 us -> 527 us (0.974)
  blocking collectives: 37.9 us -> 12.7 us
  waiting for transfers between devices: 220 us -> 243 us
  Pallas kernels: 168 us -> 150 us
    all_to_all x5 -> x6, waiting for transfers between devices: 17.8 us -> 83.7 us  [exchange(): return lax.all_to_all(values, SEQ, 0, 0, tiled=True)]
    ppermute x44 -> x40, waiting for transfers between devices: 153 us -> 101 us  [swap(): return lax.ppermute(values, axis, SWAP)]
    all_to_all x2 -> x1, blocking collectives: 37.9 us -> 12.7 us  [exchange(): return lax.all_to_all(values, SEQ, 0, 0, tiled=True)]
    ppermute x0 -> x1, waiting for transfers between devices: none -> 18.2 us  [send_direct(): corner = lax.ppermute(parts[3], ('y', 'x'), [(i, 3 - i) for i in range(4)])]
    pallas_call x6 -> x4, Pallas kernels: 37.7 us -> 24.7 us  [the longest x1 8.86 us: call_up_grad(): pl.pallas_call(functools.partial(up_grad_kernel, cut), grid=(nz,), in_spe...]
    all_gather x1, waiting for transfers between devices: 17 us -> 7.12 us  [fast_shards(): lax.all_gather(after(up_mine, got[0]), ('y', 'x'), axis=0, tiled=False)]
    ppermute x44 -> x40, starting transfers between devices: 30.4 us -> 27.8 us  [swap(): return lax.ppermute(values, axis, SWAP)]
    unnamed x90 -> x88, local copies, waits for them, and re-layouts: 10.8 us -> 13.4 us
  transfers between devices with their start and end apart: 63 -> 61, of which waited for: 30 -> 32; matrix products, arithmetic and copies ran while one was open for 3% -> 3% of each run, Pallas kernels for 24% -> 22%
where the time goes in v4:
time: 527 us; the launch traced here: 519 us
  waiting for transfers between devices  243 us (46%)
  Pallas kernels  150 us (28%)
  starting transfers between devices  65.7 us (12%)
  local copies, waits for them, and re-layouts  18.3 us (3%)
  between operations  15.1 us (3%)
  other arithmetic  13.6 us (3%)
  blocking collectives  12.7 us (2%)
    ppermute x40, waiting for transfers between devices, swap(): return lax.ppermute(values, axis, SWAP)  101 us
    all_to_all x6, waiting for transfers between devices, exchange(): return lax.all_to_all(values, SEQ, 0, 0, tiled=True)  83.7 us
    ppermute x40, starting transfers between devices, swap(): return lax.ppermute(values, axis, SWAP)  27.8 us
    pallas_call x1, Pallas kernels, call_layer(): pl.pallas_call(layer_kernel, grid_spec=pltpu.PrefetchScalarGridSpec(num_s...  27.6 us
    ppermute x6, waiting for transfers between devices, ring(): lax.ppermute(values, 'z', [(i, (i + step) % size) for i in range(size)])  26.3 us
    all_to_all x6, starting transfers between devices, exchange(): return lax.all_to_all(values, SEQ, 0, 0, tiled=True)  25.1 us
    pallas_call x1, Pallas kernels, call_layer_back(): pl.pallas_call(layer_back_kernel, grid_spec=pltpu.PrefetchScalarGridSpec(...  24.3 us
    pallas_call x2, Pallas kernels, call_attend_back(): pl.pallas_call(functools.partial(attend_back_kernel, first), grid_spec=pl...  19.8 us
  transfers between devices with their start and end apart: 61, of which 32 were waited for; matrix products, arithmetic and copies ran while one was open for 3% of the time, Pallas kernels for 22%

profile of v4, /device:TPU:0, one launch (start us, length us, event | category | flops | bytes accessed | tf_op | source)
XLA Modules:
  0.0 518.5 jit_solution(8861619238417698566)
XLA Ops:
  38.7 8.6 %collective-permute-done.9 = bf16[640,256]{1,0:T(8,128)(2,1)S(1)} collective-permute-done((bf16[640,256]{1,0:T(8,128)(2,1)S(1)}, bf16[640,256]{1,0:T(8,128)(2,1)S(1)}, u32[]{:S(2)}, u32[]{:S(2)}) %collective-permute-start.9) | collective-permute-done | bytes 327712 | tf_op jit(solution)/shard_map/ppermute | solution.py:829
  55.5 8.0 %collective-permute-done.11 = bf16[2,3,256,128]{3,2,1,0:T(8,128)(2,1)S(1)} collective-permute-done((bf16[2,3,256,128]{3,2,1,0:T(8,128)(2,1)S(1)}, bf16[2,3,256,128]{3,2,1,0:T(8,128)(2,1)S(1)}, u32[]{:S(2)}, u32[]{:S(2)}) %collective-permute-start.11) | collective-permute-done | bytes 393248 | tf_op jit(solution)/shard_map/ppermute | solution.py:826
  67.8 9.3 %project.1 = (bf16[4,2,2,3,128,128]{5,4,3,2,1,0:T(8,128)(2,1)}, bf16[4,2,1,3,128,128]{5,4,3,2,1,0:T(8,128)(2,1)}, bf16[384,512]{1,0:T(8,128)(2,1)}, bf16[384,512]{1,0:T(8,128)(2,1)}) custom-call(s32[4]{0:T(128)} %pad_add_fusion.pos, s32[12]{0:T(128)} %reshape.82.starts, bf16[384,1024]{1,0:T(8,128)(2,1)} %bitcast.59, ...), custom_call_target="tpu_custom_call" | custom-call | flops 483183808 | bytes 2400000 | tf_op jit(solution)/shard_map/project/pallas_call | solution.py:369
  87.2 28.3 %collective-permute-done.20.refs_16_.refs_24_.refs_19_.refs_27_ = bf16[4,640,256]{2,1,0:T(8,128)(2,1)} collective-permute-done((bf16[4,640,256]{2,1,0:T(8,128)(2,1)S(1)}, bf16[4,640,256]{2,1,0:T(8,128)(2,1)}, u32[]{:S(2)}, u32[]{:S(2)}) %collective-permute-start.20) | collective-permute-done | bytes 1310752 | tf_op jit(solution)/shard_map/ppermute | solution.py:826
  115.5 13.7 %collective-permute-done.18.refs_15_.refs_23_.refs_18_.refs_26_ = bf16[4,640,256]{2,1,0:T(8,128)(2,1)S(1)} collective-permute-done((bf16[4,640,256]{2,1,0:T(8,128)(2,1)S(1)}, bf16[4,640,256]{2,1,0:T(8,128)(2,1)S(1)}, u32[]{:S(2)}, u32[]{:S(2)}) %collective-permute-start.18) | collective-permute-done | bytes 1310752 | tf_op jit(solution)/shard_map/ppermute | solution.py:826
  131.9 21.6 %collective-permute-done.22 = bf16[3,640,256]{2,1,0:T(8,128)(2,1)S(1)} collective-permute-done((bf16[3,640,256]{2,1,0:T(8,128)(2,1)S(1)}, bf16[3,640,256]{2,1,0:T(8,128)(2,1)S(1)}, u32[]{:S(2)}, u32[]{:S(2)}) %collective-permute-start.22) | collective-permute-done | bytes 983072 | tf_op jit(solution)/shard_map/ppermute | solution.py:826
  161.7 10.0 %attend.2 = (bf16[8,2,128,128]{3,2,1,0:T(8,128)(2,1)}, f32[2,8,1024]{2,1,0:T(8,128)}) custom-call(s32[12]{0:T(128)} %reshape.82.starts, bf16[8,2,3,128,128]{4,3,2,1,0:T(8,128)(2,1)} %all-to-all-done.got), custom_call_target="tpu_custom_call" | custom-call | flops 429496736 | bytes 800000 | tf_op jit(solution)/shard_map/attend/pallas_call | solution.py:408
  171.7 10.1 %all-to-all-done.2.got = bf16[8,1,3,128,128]{4,3,2,1,0:T(8,128)(2,1)S(1)} async-done(((bf16[8,1,3,128,128]{4,3,2,1,0:T(8,128)(2,1)}), bf16[8,1,3,128,128]{4,3,2,1,0:T(8,128)(2,1)S(1)}, u32[]{:S(2)}, u32[]{:S(2)}) %all-to-all-start.2) | async-done | bytes 786464 | tf_op jit(solution)/shard_map/all_to_all | solution.py:883
  192.3 7.8 %all-to-all-done.1.refs_0_ = bf16[8,2,128,128]{3,2,1,0:T(8,128)(2,1)} async-done(((bf16[8,2,128,128]{3,2,1,0:T(8,128)(2,1)}), bf16[8,2,128,128]{3,2,1,0:T(8,128)(2,1)}, u32[]{:S(2)}, u32[]{:S(2)}) %all-to-all-start.1) | async-done | bytes 524320 | tf_op jit(solution)/shard_map/all_to_all | solution.py:883
  200.1 12.7 %all_to_all.35.refs_1_ = bf16[8,1,128,128]{3,2,1,0:T(8,128)(2,1)} all-to-all(bf16[8,1,128,128]{3,2,1,0:T(8,128)(2,1)} %get-tuple-element.110.att), channel_id=1, replica_groups=mesh['y'=2,'c'=2,'z'=4,'x'=2] {'z','x'}, dimensions={0} | all-to-all | bytes 524288 | tf_op jit(solution)/shard_map/all_to_all | solution.py:883
  220.0 7.4 %collective-permute-done.25.refs_10_.refs_11_.refs_12_.refs_13_.refs_14_.refs_15_.refs_16_ = bf16[4,4,256,512]{3,2,1,0:T(8,128)(2,1)} collective-permute-done((bf16[4,4,256,512]{3,2,1,0:T(8,128)(2,1)}, bf16[4,4,256,512]{3,2,1,0:T(8,128)(2,1)}, u32[]{:S(2)}, u32[]{:S(2)}) %collective-permute-start.25) | collective-permute-done | bytes 4194336 | tf_op jit(solution)/shard_map/ppermute | solution.py:826
  227.4 27.6 %layer.1 = (bf16[384,1024]{1,0:T(8,128)(2,1)}, bf16[384,1024]{1,0:T(8,128)(2,1)}, bf16[4,2,384,512]{3,2,1,0:T(8,128)(2,1)}, bf16[4,2,384,512]{3,2,1,0:T(8,128)(2...) custom-call(s32[4]{0:T(128)} %pad_add_fusion.pos, ...), custom_call_target="tpu_custom_call" | custom-call | flops 1449551488 | bytes 8000000 | tf_op jit(solution)/shard_map/layer/pallas_call | solution.py:570
  255.6 24.3 %layer_back.1 = (bf16[4,2,384,512]{3,2,1,0:T(8,128)(2,1)}, bf16[384,512]{1,0:T(8,128)(2,1)}, bf16[384,512]{1,0:T(8,128)(2,1)}, f32[384,1024]{1,0:T(8,128)}, bf16...) custom-call(s32[4]{0:T(128)} %pad_add_fusion.pos, bf16[384,1024]{1,0:T(8,128)(2,1)} %bitcast.63, ...), custom_call_target="tpu_custom_call" | custom-call | flops 1449551488 | bytes 8000000 | tf_op jit(solution)/shard_map/layer_back/pallas_call | solution.py:626
  282.5 8.4 %down_grad.1 = bf16[4,4,512,256]{3,2,1,0:T(8,128)(2,1)} custom-call(s32[4]{0:T(128)} %pad_add_fusion.pos, bf16[4,2,384,512]{3,2,1,0:T(8,128)(2,1)} %get-tuple-element.123.act, bf16[4,2,384,512]{3,2,1,0:T(8,128)(2,1)} %copy-done.16, bf16[2,384,512]{2,1,0:T(8,128)(2,1)} %get-tuple-element.120.refs_7_.keep, bf16[2,384,512]{2,1,0:T(8,128)(2,1)} %copy-done.14), custom_call_target="tpu_custom_call" | custom-call | flops 644245120 | bytes 3200000 | tf_op jit(solution)/shard_map/down_grad/pallas_call | solution.py:673
  295.6 20.3 %all-to-all-done.4.grad = bf16[8,3,128,128]{3,2,1,0:T(8,128)(2,1)S(1)} async-done(((bf16[8,3,128,128]{3,2,1,0:T(8,128)(2,1)}), bf16[8,3,128,128]{3,2,1,0:T(8,128)(2,1)S(1)}, u32[]{:S(2)}, u32[]{:S(2)}) %all-to-all-start.4) | async-done | bytes 786464 | tf_op jit(solution)/shard_map/all_to_all | solution.py:883
  316.8 7.6 %attend_back.2 = bf16[8,1,3,128,128]{4,3,2,1,0:T(8,128)(2,1)} custom-call(s32[12]{0:T(128)} %reshape.82.starts, f32[1024,128]{1,0:T(8,128)} %constant.54.clone.tcos, f32[1024,128]{1,0:T(8,128)} %constant.55.clone.tsin, f32[3,4,128]{2,1,0:T(4,128)} %get-tuple-element.211.start_cos, f32[3,4,128]{2,1,0:T(4,128)} %get-tuple-element.210.start_sin, ...), custom_call_target="tpu_custom_call" | custom-call | flops 536870912 | bytes 800000 | tf_op jit(solution)/shard_map/attend_back/pallas_call | solution.py:462
  328.1 12.2 %attend_back.3 = bf16[8,2,3,128,128]{4,3,2,1,0:T(8,128)(2,1)} custom-call(s32[12]{0:T(128)} %reshape.82.starts, f32[1024,128]{1,0:T(8,128)} %constant.54.clone.tcos, f32[1024,128]{1,0:T(8,128)} %constant.55.clone.tsin, f32[3,4,128]{2,1,0:T(4,128)} %get-tuple-element.211.start_cos, f32[3,4,128]{2,1,0:T(4,128)} %get-tuple-element.210.start_sin, ...), custom_call_target="tpu_custom_call" | custom-call | flops 1073741824 | bytes 1600000 | tf_op jit(solution)/shard_map/attend_back/pallas_call | solution.py:462
  340.3 8.2 %all-to-all-done.5 = bf16[8,1,3,128,128]{4,3,2,1,0:T(8,128)(2,1)S(1)} async-done(((bf16[8,1,3,128,128]{4,3,2,1,0:T(8,128)(2,1)}), bf16[8,1,3,128,128]{4,3,2,1,0:T(8,128)(2,1)S(1)}, u32[]{:S(2)}, u32[]{:S(2)}) %all-to-all-start.5) | async-done | bytes 786464 | tf_op jit(solution)/shard_map/all_to_all | solution.py:883
  356.0 8.9 %up_grad.1 = (bf16[4,320,512]{2,1,0:T(8,128)(2,1)}, bf16[4,320,512]{2,1,0:T(8,128)(2,1)}, bf16[4,320,512]{2,1,0:T(8,128)(2,1)}, bf16[4,320,512]{2,1,0:T(8,128)(2,1)}) custom-call(bf16[4,2,384,512]{3,2,1,0:T(8,128)(2,1)} %get-tuple-element.134.g_up, bf16[4,2,384,512]{3,2,1,0:T(8,128)(2,1)} %collective-permute-done.29.g_up2, ...), custom_call_target="tpu_custom_call" | custom-call | flops 644245120 | bytes 3200000 | tf_op jit(solution)/shard_map/up_grad/pallas_call | solution.py:704
  368.7 37.3 %all-to-all-done.6 = bf16[8,2,3,128,128]{4,3,2,1,0:T(8,128)(2,1)S(1)} async-done(((bf16[8,2,3,128,128]{4,3,2,1,0:T(8,128)(2,1)}), bf16[8,2,3,128,128]{4,3,2,1,0:T(8,128)(2,1)S(1)}, u32[]{:S(2)}, u32[]{:S(2)}) %all-to-all-start.6) | async-done | bytes 1572896 | tf_op jit(solution)/shard_map/all_to_all | solution.py:883
  412.2 9.0 %qkv_grad.1 = (bf16[4,3,256,128]{3,2,1,0:T(8,128)(2,1)}, bf16[2,3,256,128]{3,2,1,0:T(8,128)(2,1)}, bf16[2,3,256,128]{3,2,1,0:T(8,128)(2,1)}, bf16[2,3,256,128]{3...) custom-call(s32[4]{0:T(128)} %pad_add_fusion.pos, ...), custom_call_target="tpu_custom_call" | custom-call | flops 483183808 | bytes 2400000 | tf_op jit(solution)/shard_map/qkv_grad/pallas_call | solution.py:739
  421.2 18.2 %collective-permute-done.42.refs_1_ = bf16[4,320,512]{2,1,0:T(8,128)(2,1)} collective-permute-done((bf16[4,320,512]{2,1,0:T(8,128)(2,1)}, bf16[4,320,512]{2,1,0:T(8,128)(2,1)}, u32[]{:S(2)}, u32[]{:S(2)}) %collective-permute-start.42) | collective-permute-done | bytes 1310752 | tf_op jit(solution)/shard_map/ppermute | solution.py:805
  448.3 7.9 %collective-permute-done.36.b = bf16[2,3,256,128]{3,2,1,0:T(8,128)(2,1)S(1)} collective-permute-done((bf16[2,3,256,128]{3,2,1,0:T(8,128)(2,1)S(1)}, bf16[2,3,256,128]{3,2,1,0:T(8,128)(2,1)S(1)}, u32[]{:S(2)}, u32[]{:S(2)}) %collective-permute-start.36) | collective-permute-done | bytes 393248 | tf_op jit(solution)/shard_map/ppermute | solution.py:826
  465.4 14.4 %input_grad.1 = (f32[384,1024]{1,0:T(8,128)}, f32[8,1024]{1,0:T(8,128)}) custom-call(s32[4]{0:T(128)} %pad_add_fusion.pos, bf16[4,2,2,3,128,128]{5,4,3,2,1,0:T(8,128)(2,1)} %bitcast.55, bf16[4,2,1,3,128,128]{5,4,3,2,1,0:T(8,128)(2,1)} %bitcast.58, bf16[384,1024]{1,0:T(8,128)(2,1)} %bitcast.61, f32[4,1024]{1,0:T(4,128)} %get-tuple-element.207.gains.refs_4_.refs_1_.refs_3_, ...), custom_call_target="tpu_custom_call" | custom-call | flops 483183808 | bytes 3200000 | tf_op jit(solution)/shard_map/input_grad/pallas_call | solution.py:775
  (241 shorter events, 161.7 us)
Async XLA Ops:
  38.7 26.2 %collective-permute-start.12 = (bf16[4,3,256,128]{3,2,1,0:T(8,128)(2,1)S(1)}, bf16[4,3,256,128]{3,2,1,0:T(8,128)(2,1)S(1)}, u32[]{:S(2)}, u32[]{:S(2)}) collective-permute-start(bf16[4,3,256,128]{3,2,1,0:T(8,128)(2,1)S(1)} %pad_maximum_fusion.1.refs_0_.refs_5_), channel_id=1, source_target_pairs={{0,8},{8,0},{1,9},{9,1},{2,10},{10,2},{3,11},{11,3},{4,12},{12,4},... | collective-permute-start | bytes 2359304 | tf_op jit(solution)/shard_map/ppermute | solution.py:826
  77.1 79.8 %all-to-all-start = ((bf16[8,2,3,128,128]{4,3,2,1,0:T(8,128)(2,1)}), bf16[8,2,3,128,128]{4,3,2,1,0:T(8,128)(2,1)}, u32[]{:S(2)}, u32[]{:S(2)}) async-start(bf16[8,2,3,128,128]{4,3,2,1,0:T(8,128)(2,1)} %bitcast.64), calls=%async_computation | async-start | bytes 3145728 | tf_op jit(solution)/shard_map/all_to_all | solution.py:883
  81.5 75.3 %all-gather.5.cloned.1.call-start = ((), (), s32[]{:S(2)}) async-start(), calls=%async_computation.14 | async-start | bytes 1310720 | tf_op jit(solution)/shard_map/all_gather | solution.py:899
  84.6 30.9 %collective-permute-start.20 = (bf16[4,640,256]{2,1,0:T(8,128)(2,1)S(1)}, bf16[4,640,256]{2,1,0:T(8,128)(2,1)}, u32[]{:S(2)}, u32[]{:S(2)}) collective-permute-start(bf16[4,640,256]{2,1,0:T(8,128)(2,1)S(1)} %pad_maximum_fusion.refs_14_.refs_22_.refs_17_.refs_25_), channel_id=1, source_target_pairs={{0,16},{16,0},{1,17},{17,1},{2,18},{18,2},{3,19},{19,3},{4,20},{20... | collective-permute-start | bytes 3932168 | tf_op jit(solution)/shard_map/ppermute | solution.py:826
  86.2 43.0 %collective-permute-start.18 = (bf16[4,640,256]{2,1,0:T(8,128)(2,1)S(1)}, bf16[4,640,256]{2,1,0:T(8,128)(2,1)S(1)}, u32[]{:S(2)}, u32[]{:S(2)}) collective-permute-start(bf16[4,640,256]{2,1,0:T(8,128)(2,1)S(1)} %pad_maximum_fusion.refs_14_.refs_22_.refs_17_.refs_25_), channel_id=1, source_target_pairs={{0,1},{1,0},{2,3},{3,2},{4,5},{5,4},{6,7},{7,6},{8,9},{9,8},{10,11... | collective-permute-start | bytes 3932168 | tf_op jit(solution)/shard_map/ppermute | solution.py:826
  87.0 132.9 %all-gather.7.cloned.1.call-start = ((), (), s32[]{:S(2)}) async-start(), calls=%async_computation.15 | async-start | bytes 5242880 | tf_op jit(solution)/shard_map/all_gather | solution.py:913
  87.1 66.5 %collective-permute-start.17 = (bf16[4,640,256]{2,1,0:T(8,128)(2,1)S(1)}, bf16[4,640,256]{2,1,0:T(8,128)(2,1)S(1)}, u32[]{:S(2)}, u32[]{:S(2)}) collective-permute-start(bf16[4,640,256]{2,1,0:T(8,128)(2,1)S(1)} %pad_maximum_fusion.refs_14_.refs_22_.refs_17_.refs_25_), channel_id=1, source_target_pairs={{0,8},{8,0},{1,9},{9,1},{2,10},{10,2},{3,11},{11,3},{4,12},{12,4},... | collective-permute-start | bytes 3932168 | tf_op jit(solution)/shard_map/ppermute | solution.py:826
  115.5 39.2 %collective-permute-start.21 = (bf16[4,640,256]{2,1,0:T(8,128)(2,1)}, bf16[4,640,256]{2,1,0:T(8,128)(2,1)S(1)}, u32[]{:S(2)}, u32[]{:S(2)}) collective-permute-start(bf16[4,640,256]{2,1,0:T(8,128)(2,1)} %collective-permute-done.20.refs_16_.refs_24_.refs_19_.refs_27_), channel_id=1, source_target_pairs={{0,8},{8,0},{1,9},{9,1},{2,10},{10,2},{3,11},{11,3},{4,12},{12,4},... | collective-permute-start | bytes 3932168 | tf_op jit(solution)/shard_map/ppermute | solution.py:826
  129.2 27.7 %collective-permute-start.19 = (bf16[4,640,256]{2,1,0:T(8,128)(2,1)S(1)}, bf16[4,640,256]{2,1,0:T(8,128)(2,1)}, u32[]{:S(2)}, u32[]{:S(2)}) collective-permute-start(bf16[4,640,256]{2,1,0:T(8,128)(2,1)S(1)} %collective-permute-done.18.refs_15_.refs_23_.refs_18_.refs_26_), channel_id=1, source_target_pairs={{0,8},{8,0},{1,9},{9,1},{2,10},{10,2},{3,11},{11,3},{4,12},{12,4},... | collective-permute-start | bytes 3932168 | tf_op jit(solution)/shard_map/ppermute | solution.py:826
  156.9 24.9 %all-to-all-start.2 = ((bf16[8,1,3,128,128]{4,3,2,1,0:T(8,128)(2,1)}), bf16[8,1,3,128,128]{4,3,2,1,0:T(8,128)(2,1)S(1)}, u32[]{:S(2)}, u32[]{:S(2)}) async-start(bf16[8,1,3,128,128]{4,3,2,1,0:T(8,128)(2,1)} %bitcast.68), calls=%async_computation.2 | async-start | bytes 1572864 | tf_op jit(solution)/shard_map/all_to_all | solution.py:883
  161.6 30.7 %collective-permute-start.24 = (bf16[4,640,256]{2,1,0:T(8,128)(2,1)S(1)}, bf16[4,640,256]{2,1,0:T(8,128)(2,1)S(1)}, u32[]{:S(2)}, u32[]{:S(2)}) collective-permute-start(bf16[4,640,256]{2,1,0:T(8,128)(2,1)S(1)} %copy-done.3), channel_id=1, source_target_pairs={{0,8},{8,0},{1,9},{9,1},{2,10},{10,2},{3,11},{11,3},{4,12},{12,4},... | collective-permute-start | bytes 3932168 | tf_op jit(solution)/shard_map/ppermute | solution.py:826
  185.9 182.5 %reduce-scatter.13.cloned.1.call-start = ((), (), s32[]{:S(2)}) async-start(), calls=%async_computation.16 | async-start | bytes 5242880
  255.0 24.9 %collective-permute-start.26 = (bf16[4,2,384,512]{3,2,1,0:T(8,128)(2,1)}, bf16[4,2,384,512]{3,2,1,0:T(8,128)(2,1)S(1)}, u32[]{:S(2)}, u32[]{:S(2)}) collective-permute-start(bf16[4,2,384,512]{3,2,1,0:T(8,128)(2,1)} %get-tuple-element.123.act), channel_id=1, source_target_pairs={{0,8},{8,0},{1,9},{9,1},{2,10},{10,2},{3,11},{11,3},{4,12},{12,4},... | collective-permute-start | bytes 9437192 | tf_op jit(solution)/shard_map/ppermute | solution.py:826
  255.2 24.7 %collective-permute-start.27 = (bf16[2,384,512]{2,1,0:T(8,128)(2,1)}, bf16[2,384,512]{2,1,0:T(8,128)(2,1)S(1)}, u32[]{:S(2)}, u32[]{:S(2)}) collective-permute-start(bf16[2,384,512]{2,1,0:T(8,128)(2,1)} %get-tuple-element.121.refs_8_), channel_id=1, source_target_pairs={{0,8},{8,0},{1,9},{9,1},{2,10},{10,2},{3,11},{11,3},{4,12},{12,4},... | collective-permute-start | bytes 2359304 | tf_op jit(solution)/shard_map/ppermute | solution.py:826
  291.0 24.9 %all-to-all-start.4 = ((bf16[8,3,128,128]{3,2,1,0:T(8,128)(2,1)}), bf16[8,3,128,128]{3,2,1,0:T(8,128)(2,1)S(1)}, u32[]{:S(2)}, u32[]{:S(2)}) async-start(bf16[8,3,128,128]{3,2,1,0:T(8,128)(2,1)} %get-tuple-element.122), calls=%async_computation.4 | async-start | bytes 1572864 | tf_op jit(solution)/shard_map/all_to_all | solution.py:883
  295.5 60.5 %collective-permute-start.29 = (bf16[4,2,384,512]{3,2,1,0:T(8,128)(2,1)}, bf16[4,2,384,512]{3,2,1,0:T(8,128)(2,1)}, u32[]{:S(2)}, u32[]{:S(2)}) collective-permute-start(bf16[4,2,384,512]{3,2,1,0:T(8,128)(2,1)} %get-tuple-element.134.g_up), channel_id=1, source_target_pairs={{0,8},{8,0},{1,9},{9,1},{2,10},{10,2},{3,11},{11,3},{4,12},{12,4},... | collective-permute-start | bytes 9437192 | tf_op jit(solution)/shard_map/ppermute | solution.py:826
  348.4 57.6 %all-to-all-start.6 = ((bf16[8,2,3,128,128]{4,3,2,1,0:T(8,128)(2,1)}), bf16[8,2,3,128,128]{4,3,2,1,0:T(8,128)(2,1)S(1)}, u32[]{:S(2)}, u32[]{:S(2)}) async-start(bf16[8,2,3,128,128]{4,3,2,1,0:T(8,128)(2,1)} %attend_back.3), calls=%async_computation.6 | async-start | bytes 3145728 | tf_op jit(solution)/shard_map/all_to_all | solution.py:883
  352.0 148.2 %reduce-scatter.7.cloned.1.call-start = ((), (), s32[]{:S(2)}) async-start(), calls=%async_computation.11 | async-start | bytes 1310720 | tf_op jit(solution)/shard_map/reduce_scatter | solution.py:949
  364.9 41.2 %collective-permute-start.32 = (bf16[4,320,512]{2,1,0:T(8,128)(2,1)}, bf16[4,320,512]{2,1,0:T(8,128)(2,1)}, u32[]{:S(2)}, u32[]{:S(2)}) collective-permute-start(bf16[4,320,512]{2,1,0:T(8,128)(2,1)} %get-tuple-element.139), channel_id=1, source_target_pairs={{0,1},{1,0},{2,3},{3,2},{4,5},{5,4},{6,7},{7,6},{8,9},{9,8},{10,11... | collective-permute-start | bytes 3932168 | tf_op jit(solution)/shard_map/ppermute | solution.py:826
  366.9 39.2 %collective-permute-start.33 = (bf16[4,320,512]{2,1,0:T(8,128)(2,1)}, bf16[4,320,512]{2,1,0:T(8,128)(2,1)}, u32[]{:S(2)}, u32[]{:S(2)}) collective-permute-start(bf16[4,320,512]{2,1,0:T(8,128)(2,1)} %get-tuple-element.140), channel_id=1, source_target_pairs={{0,16},{16,0},{1,17},{17,1},{2,18},{18,2},{3,19},{19,3},{4,20},{20... | collective-permute-start | bytes 3932168 | tf_op jit(solution)/shard_map/ppermute | solution.py:826
  368.4 37.7 %collective-permute-start.28 = (bf16[4,2,1,3,128,128]{5,4,3,2,1,0:T(8,128)(2,1)S(1)}, bf16[4,2,1,3,128,128]{5,4,3,2,1,0:T(8,128)(2,1)S(1)}, u32[]{:S(2)}, u32[]{:S(2)}) collective-permute-start(bf16[4,2,1,3,128,128]{5,4,3,2,1,0:T(8,128)(2,1)S(1)} %bitcast.56), channel_id=1, source_target_pairs={{0,8},{8,0},{1,9},{9,1},{2,10},{10,2},{3,11},{11,3},{4,12},{12,4},... | collective-permute-start | bytes 2359304 | tf_op jit(solution)/shard_map/ppermute | solution.py:826
  368.4 136.9 %reduce-scatter.11.cloned.1.call-start = ((), (), s32[]{:S(2)}) async-start(), calls=%async_computation.13 | async-start | bytes 1638400 | tf_op jit(solution)/shard_map/reduce_scatter | solution.py:964
  407.0 32.4 %collective-permute-start.42 = (bf16[4,320,512]{2,1,0:T(8,128)(2,1)}, bf16[4,320,512]{2,1,0:T(8,128)(2,1)}, u32[]{:S(2)}, u32[]{:S(2)}) collective-permute-start(bf16[4,320,512]{2,1,0:T(8,128)(2,1)} %get-tuple-element.141), channel_id=1, source_target_pairs={{0,17},{1,16},{16,1},{17,0},{2,19},{3,18},{18,3},{19,2},{4,21},{5,... | collective-permute-start | bytes 3932168 | tf_op jit(solution)/shard_map/ppermute | solution.py:805
  444.6 65.0 %reduce-scatter.9.cloned.1.call-start = ((), (), s32[]{:S(2)}) async-start(), calls=%async_computation.12 | async-start | bytes 983040 | tf_op jit(solution)/shard_map/reduce_scatter | solution.py:970
  (80 other events, 759.1 us)
Sparse Core Ops, SparseCore 0:
  87.2 47.9 all-gather.4
  157.0 62.8 all-gather.6
  291.1 62.2 reduce-scatter.12
  368.6 36.8 reduce-scatter.6
  444.7 30.1 reduce-scatter.10
  487.3 22.1 reduce-scatter.8

commit v5 on v4

--- a/solution.py
+++ b/solution.py
@@ -906,7 +906,7 @@
     got = [None, None]
     got[0] = exchange(first.reshape(parts, 2, 3, shard_len, cols))
     got[1] = exchange(after(last.reshape(parts, 1, 3, shard_len, cols), got[0]))
-    mix_corner = gather_corner(*mix_sides, 3)
+    mix_corner = gather_corner(*mix_sides, 2)
     mix_other = [swap(p, 'c') for p in (mix_mine, *mix_sides)]
     att_local, lses, att = ([None, None], [None, None], [None, None])
     got[0] = after(got[0], mix_other, mix_corner)

time: 527 us -> 521 us (0.989)
  transfers between devices with their start and end apart: 61 -> 61, of which waited for: 32 -> 33; matrix products, arithmetic and copies ran while one was open for 3% -> 3% of each run, Pallas kernels for 22% -> 22%
where the time goes in v5:
time: 521 us; the launch traced here: 513 us
  waiting for transfers between devices  240 us (46%)
  Pallas kernels  150 us (29%)
  starting transfers between devices  62.6 us (12%)
  local copies, waits for them, and re-layouts  18.2 us (3%)
  between operations  15.1 us (3%)
  other arithmetic  13.6 us (3%)
  blocking collectives  12.7 us (2%)
    ppermute x40, waiting for transfers between devices, swap(): return lax.ppermute(values, axis, SWAP)  96.9 us
    all_to_all x6, waiting for transfers between devices, exchange(): return lax.all_to_all(values, SEQ, 0, 0, tiled=True)  84.3 us
    pallas_call x1, Pallas kernels, call_layer(): pl.pallas_call(layer_kernel, grid_spec=pltpu.PrefetchScalarGridSpec(num_s...  27.6 us
    ppermute x6, waiting for transfers between devices, ring(): lax.ppermute(values, 'z', [(i, (i + step) % size) for i in range(size)])  26.3 us
    ppermute x40, starting transfers between devices, swap(): return lax.ppermute(values, axis, SWAP)  25.7 us
    all_to_all x6, starting transfers between devices, exchange(): return lax.all_to_all(values, SEQ, 0, 0, tiled=True)  25.1 us
    pallas_call x1, Pallas kernels, call_layer_back(): pl.pallas_call(layer_back_kernel, grid_spec=pltpu.PrefetchScalarGridSpec(...  24.3 us
    pallas_call x2, Pallas kernels, call_attend_back(): pl.pallas_call(functools.partial(attend_back_kernel, first), grid_spec=pl...  19.8 us
  transfers between devices with their start and end apart: 61, of which 33 were waited for; matrix products, arithmetic and copies ran while one was open for 3% of the time, Pallas kernels for 22%

profile of v5, /device:TPU:0, one launch (start us, length us, event | category | flops | bytes accessed | tf_op | source)
XLA Modules:
  0.0 512.6 jit_solution(13141650126678788599)
XLA Ops:
  38.7 8.6 %collective-permute-done.9 = bf16[640,256]{1,0:T(8,128)(2,1)S(1)} collective-permute-done((bf16[640,256]{1,0:T(8,128)(2,1)S(1)}, bf16[640,256]{1,0:T(8,128)(2,1)S(1)}, u32[]{:S(2)}, u32[]{:S(2)}) %collective-permute-start.9) | collective-permute-done | bytes 327712 | tf_op jit(solution)/shard_map/ppermute | solution.py:829
  55.5 8.0 %collective-permute-done.11 = bf16[2,3,256,128]{3,2,1,0:T(8,128)(2,1)S(1)} collective-permute-done((bf16[2,3,256,128]{3,2,1,0:T(8,128)(2,1)S(1)}, bf16[2,3,256,128]{3,2,1,0:T(8,128)(2,1)S(1)}, u32[]{:S(2)}, u32[]{:S(2)}) %collective-permute-start.11) | collective-permute-done | bytes 393248 | tf_op jit(solution)/shard_map/ppermute | solution.py:826
  67.8 9.3 %project.1 = (bf16[4,2,2,3,128,128]{5,4,3,2,1,0:T(8,128)(2,1)}, bf16[4,2,1,3,128,128]{5,4,3,2,1,0:T(8,128)(2,1)}, bf16[384,512]{1,0:T(8,128)(2,1)}, bf16[384,512]{1,0:T(8,128)(2,1)}) custom-call(s32[4]{0:T(128)} %pad_add_fusion.pos, s32[12]{0:T(128)} %reshape.82.starts, bf16[384,1024]{1,0:T(8,128)(2,1)} %bitcast.59, ...), custom_call_target="tpu_custom_call" | custom-call | flops 483183808 | bytes 2400000 | tf_op jit(solution)/shard_map/project/pallas_call | solution.py:369
  87.2 28.2 %collective-permute-done.20.refs_16_.refs_24_.refs_19_.refs_27_ = bf16[4,640,256]{2,1,0:T(8,128)(2,1)S(1)} collective-permute-done((bf16[4,640,256]{2,1,0:T(8,128)(2,1)S(1)}, bf16[4,640,256]{2,1,0:T(8,128)(2,1)S(1)}, u32[]{:S(2)}, u32[]{:S(2)}) %collective-permute-start.20) | collective-permute-done | bytes 1310752 | tf_op jit(solution)/shard_map/ppermute | solution.py:826
  115.4 13.9 %collective-permute-done.18.refs_15_.refs_23_.refs_18_.refs_26_ = bf16[4,640,256]{2,1,0:T(8,128)(2,1)} collective-permute-done((bf16[4,640,256]{2,1,0:T(8,128)(2,1)S(1)}, bf16[4,640,256]{2,1,0:T(8,128)(2,1)}, u32[]{:S(2)}, u32[]{:S(2)}) %collective-permute-start.18) | collective-permute-done | bytes 1310752 | tf_op jit(solution)/shard_map/ppermute | solution.py:826
  132.1 15.5 %collective-permute-done.22 = bf16[2,640,256]{2,1,0:T(8,128)(2,1)S(1)} collective-permute-done((bf16[2,640,256]{2,1,0:T(8,128)(2,1)S(1)}, bf16[2,640,256]{2,1,0:T(8,128)(2,1)S(1)}, u32[]{:S(2)}, u32[]{:S(2)}) %collective-permute-start.22) | collective-permute-done | bytes 655392 | tf_op jit(solution)/shard_map/ppermute | solution.py:826
  156.5 10.0 %attend.2 = (bf16[8,2,128,128]{3,2,1,0:T(8,128)(2,1)}, f32[2,8,1024]{2,1,0:T(8,128)}) custom-call(s32[12]{0:T(128)} %reshape.82.starts, bf16[8,2,3,128,128]{4,3,2,1,0:T(8,128)(2,1)} %all-to-all-done.got), custom_call_target="tpu_custom_call" | custom-call | flops 429496736 | bytes 800000 | tf_op jit(solution)/shard_map/attend/pallas_call | solution.py:408
  166.5 9.7 %all-to-all-done.2.got = bf16[8,1,3,128,128]{4,3,2,1,0:T(8,128)(2,1)S(1)} async-done(((bf16[8,1,3,128,128]{4,3,2,1,0:T(8,128)(2,1)}), bf16[8,1,3,128,128]{4,3,2,1,0:T(8,128)(2,1)S(1)}, u32[]{:S(2)}, u32[]{:S(2)}) %all-to-all-start.2) | async-done | bytes 786464 | tf_op jit(solution)/shard_map/all_to_all | solution.py:883
  186.9 7.8 %all-to-all-done.1.refs_0_ = bf16[8,2,128,128]{3,2,1,0:T(8,128)(2,1)} async-done(((bf16[8,2,128,128]{3,2,1,0:T(8,128)(2,1)}), bf16[8,2,128,128]{3,2,1,0:T(8,128)(2,1)}, u32[]{:S(2)}, u32[]{:S(2)}) %all-to-all-start.1) | async-done | bytes 524320 | tf_op jit(solution)/shard_map/all_to_all | solution.py:883
  194.6 12.7 %all_to_all.35.refs_1_ = bf16[8,1,128,128]{3,2,1,0:T(8,128)(2,1)} all-to-all(bf16[8,1,128,128]{3,2,1,0:T(8,128)(2,1)} %get-tuple-element.110.att), channel_id=1, replica_groups=mesh['y'=2,'c'=2,'z'=4,'x'=2] {'z','x'}, dimensions={0} | all-to-all | bytes 524288 | tf_op jit(solution)/shard_map/all_to_all | solution.py:883
  214.5 7.4 %collective-permute-done.25.refs_10_.refs_11_.refs_12_.refs_13_.refs_14_.refs_15_.refs_16_ = bf16[4,4,256,512]{3,2,1,0:T(8,128)(2,1)} collective-permute-done((bf16[4,4,256,512]{3,2,1,0:T(8,128)(2,1)}, bf16[4,4,256,512]{3,2,1,0:T(8,128)(2,1)}, u32[]{:S(2)}, u32[]{:S(2)}) %collective-permute-start.25) | collective-permute-done | bytes 4194336 | tf_op jit(solution)/shard_map/ppermute | solution.py:826
  222.0 27.6 %layer.1 = (bf16[384,1024]{1,0:T(8,128)(2,1)}, bf16[384,1024]{1,0:T(8,128)(2,1)}, bf16[4,2,384,512]{3,2,1,0:T(8,128)(2,1)}, bf16[4,2,384,512]{3,2,1,0:T(8,128)(2...) custom-call(s32[4]{0:T(128)} %pad_add_fusion.pos, ...), custom_call_target="tpu_custom_call" | custom-call | flops 1449551488 | bytes 8000000 | tf_op jit(solution)/shard_map/layer/pallas_call | solution.py:570
  250.1 24.3 %layer_back.1 = (bf16[4,2,384,512]{3,2,1,0:T(8,128)(2,1)}, bf16[384,512]{1,0:T(8,128)(2,1)}, bf16[384,512]{1,0:T(8,128)(2,1)}, f32[384,1024]{1,0:T(8,128)}, bf16...) custom-call(s32[4]{0:T(128)} %pad_add_fusion.pos, bf16[384,1024]{1,0:T(8,128)(2,1)} %bitcast.63, ...), custom_call_target="tpu_custom_call" | custom-call | flops 1449551488 | bytes 8000000 | tf_op jit(solution)/shard_map/layer_back/pallas_call | solution.py:626
  277.1 8.4 %down_grad.1 = bf16[4,4,512,256]{3,2,1,0:T(8,128)(2,1)} custom-call(s32[4]{0:T(128)} %pad_add_fusion.pos, bf16[4,2,384,512]{3,2,1,0:T(8,128)(2,1)} %get-tuple-element.123.act, bf16[4,2,384,512]{3,2,1,0:T(8,128)(2,1)} %copy-done.16, bf16[2,384,512]{2,1,0:T(8,128)(2,1)} %get-tuple-element.120.refs_7_.keep, bf16[2,384,512]{2,1,0:T(8,128)(2,1)} %copy-done.14), custom_call_target="tpu_custom_call" | custom-call | flops 644245120 | bytes 3200000 | tf_op jit(solution)/shard_map/down_grad/pallas_call | solution.py:673
  290.1 20.3 %all-to-all-done.4.grad = bf16[8,3,128,128]{3,2,1,0:T(8,128)(2,1)S(1)} async-done(((bf16[8,3,128,128]{3,2,1,0:T(8,128)(2,1)}), bf16[8,3,128,128]{3,2,1,0:T(8,128)(2,1)S(1)}, u32[]{:S(2)}, u32[]{:S(2)}) %all-to-all-start.4) | async-done | bytes 786464 | tf_op jit(solution)/shard_map/all_to_all | solution.py:883
  311.3 7.6 %attend_back.2 = bf16[8,1,3,128,128]{4,3,2,1,0:T(8,128)(2,1)} custom-call(s32[12]{0:T(128)} %reshape.82.starts, f32[1024,128]{1,0:T(8,128)} %constant.54.clone.tcos, f32[1024,128]{1,0:T(8,128)} %constant.55.clone.tsin, f32[3,4,128]{2,1,0:T(4,128)} %get-tuple-element.211.start_cos, f32[3,4,128]{2,1,0:T(4,128)} %get-tuple-element.210.start_sin, ...), custom_call_target="tpu_custom_call" | custom-call | flops 536870912 | bytes 800000 | tf_op jit(solution)/shard_map/attend_back/pallas_call | solution.py:462
  322.6 12.2 %attend_back.3 = bf16[8,2,3,128,128]{4,3,2,1,0:T(8,128)(2,1)} custom-call(s32[12]{0:T(128)} %reshape.82.starts, f32[1024,128]{1,0:T(8,128)} %constant.54.clone.tcos, f32[1024,128]{1,0:T(8,128)} %constant.55.clone.tsin, f32[3,4,128]{2,1,0:T(4,128)} %get-tuple-element.211.start_cos, f32[3,4,128]{2,1,0:T(4,128)} %get-tuple-element.210.start_sin, ...), custom_call_target="tpu_custom_call" | custom-call | flops 1073741824 | bytes 1600000 | tf_op jit(solution)/shard_map/attend_back/pallas_call | solution.py:462
  334.8 8.2 %all-to-all-done.5 = bf16[8,1,3,128,128]{4,3,2,1,0:T(8,128)(2,1)S(1)} async-done(((bf16[8,1,3,128,128]{4,3,2,1,0:T(8,128)(2,1)}), bf16[8,1,3,128,128]{4,3,2,1,0:T(8,128)(2,1)S(1)}, u32[]{:S(2)}, u32[]{:S(2)}) %all-to-all-start.5) | async-done | bytes 786464 | tf_op jit(solution)/shard_map/all_to_all | solution.py:883
  350.6 8.9 %up_grad.1 = (bf16[4,320,512]{2,1,0:T(8,128)(2,1)}, bf16[4,320,512]{2,1,0:T(8,128)(2,1)}, bf16[4,320,512]{2,1,0:T(8,128)(2,1)}, bf16[4,320,512]{2,1,0:T(8,128)(2,1)}) custom-call(bf16[4,2,384,512]{3,2,1,0:T(8,128)(2,1)} %get-tuple-element.134.g_up, bf16[4,2,384,512]{3,2,1,0:T(8,128)(2,1)} %collective-permute-done.29.g_up2, ...), custom_call_target="tpu_custom_call" | custom-call | flops 644245120 | bytes 3200000 | tf_op jit(solution)/shard_map/up_grad/pallas_call | solution.py:704
  362.3 38.3 %all-to-all-done.6 = bf16[8,2,3,128,128]{4,3,2,1,0:T(8,128)(2,1)S(1)} async-done(((bf16[8,2,3,128,128]{4,3,2,1,0:T(8,128)(2,1)}), bf16[8,2,3,128,128]{4,3,2,1,0:T(8,128)(2,1)S(1)}, u32[]{:S(2)}, u32[]{:S(2)}) %all-to-all-start.6) | async-done | bytes 1572896 | tf_op jit(solution)/shard_map/all_to_all | solution.py:883
  406.8 9.0 %qkv_grad.1 = (bf16[4,3,256,128]{3,2,1,0:T(8,128)(2,1)}, bf16[2,3,256,128]{3,2,1,0:T(8,128)(2,1)}, bf16[2,3,256,128]{3,2,1,0:T(8,128)(2,1)}, bf16[2,3,256,128]{3...) custom-call(s32[4]{0:T(128)} %pad_add_fusion.pos, ...), custom_call_target="tpu_custom_call" | custom-call | flops 483183808 | bytes 2400000 | tf_op jit(solution)/shard_map/qkv_grad/pallas_call | solution.py:739
  415.7 18.2 %collective-permute-done.42.refs_1_ = bf16[4,320,512]{2,1,0:T(8,128)(2,1)} collective-permute-done((bf16[4,320,512]{2,1,0:T(8,128)(2,1)}, bf16[4,320,512]{2,1,0:T(8,128)(2,1)}, u32[]{:S(2)}, u32[]{:S(2)}) %collective-permute-start.42) | collective-permute-done | bytes 1310752 | tf_op jit(solution)/shard_map/ppermute | solution.py:805
  441.8 8.9 %collective-permute-done.36.b = bf16[2,3,256,128]{3,2,1,0:T(8,128)(2,1)S(1)} collective-permute-done((bf16[2,3,256,128]{3,2,1,0:T(8,128)(2,1)S(1)}, bf16[2,3,256,128]{3,2,1,0:T(8,128)(2,1)S(1)}, u32[]{:S(2)}, u32[]{:S(2)}) %collective-permute-start.36) | collective-permute-done | bytes 393248 | tf_op jit(solution)/shard_map/ppermute | solution.py:826
  459.5 14.4 %input_grad.1 = (f32[384,1024]{1,0:T(8,128)}, f32[8,1024]{1,0:T(8,128)}) custom-call(s32[4]{0:T(128)} %pad_add_fusion.pos, bf16[4,2,2,3,128,128]{5,4,3,2,1,0:T(8,128)(2,1)} %bitcast.55, bf16[4,2,1,3,128,128]{5,4,3,2,1,0:T(8,128)(2,1)} %bitcast.58, bf16[384,1024]{1,0:T(8,128)(2,1)} %bitcast.61, f32[4,1024]{1,0:T(4,128)} %get-tuple-element.207.gains.refs_4_.refs_1_.refs_3_, ...), custom_call_target="tpu_custom_call" | custom-call | flops 483183808 | bytes 3200000 | tf_op jit(solution)/shard_map/input_grad/pallas_call | solution.py:775
  (241 shorter events, 159.9 us)
Async XLA Ops:
  38.7 26.2 %collective-permute-start.12 = (bf16[4,3,256,128]{3,2,1,0:T(8,128)(2,1)S(1)}, bf16[4,3,256,128]{3,2,1,0:T(8,128)(2,1)S(1)}, u32[]{:S(2)}, u32[]{:S(2)}) collective-permute-start(bf16[4,3,256,128]{3,2,1,0:T(8,128)(2,1)S(1)} %pad_maximum_fusion.1.refs_0_.refs_5_), channel_id=1, source_target_pairs={{0,8},{8,0},{1,9},{9,1},{2,10},{10,2},{3,11},{11,3},{4,12},{12,4},... | collective-permute-start | bytes 2359304 | tf_op jit(solution)/shard_map/ppermute | solution.py:826
  77.1 74.6 %all-to-all-start = ((bf16[8,2,3,128,128]{4,3,2,1,0:T(8,128)(2,1)}), bf16[8,2,3,128,128]{4,3,2,1,0:T(8,128)(2,1)}, u32[]{:S(2)}, u32[]{:S(2)}) async-start(bf16[8,2,3,128,128]{4,3,2,1,0:T(8,128)(2,1)} %bitcast.64), calls=%async_computation | async-start | bytes 3145728 | tf_op jit(solution)/shard_map/all_to_all | solution.py:883
  81.5 70.2 %all-gather.5.cloned.1.call-start = ((), (), s32[]{:S(2)}) async-start(), calls=%async_computation.14 | async-start | bytes 1310720 | tf_op jit(solution)/shard_map/all_gather | solution.py:899
  84.6 30.8 %collective-permute-start.20 = (bf16[4,640,256]{2,1,0:T(8,128)(2,1)S(1)}, bf16[4,640,256]{2,1,0:T(8,128)(2,1)S(1)}, u32[]{:S(2)}, u32[]{:S(2)}) collective-permute-start(bf16[4,640,256]{2,1,0:T(8,128)(2,1)S(1)} %pad_maximum_fusion.refs_14_.refs_22_.refs_17_.refs_25_), channel_id=1, source_target_pairs={{0,16},{16,0},{1,17},{17,1},{2,18},{18,2},{3,19},{19,3},{4,20},{20... | collective-permute-start | bytes 3932168 | tf_op jit(solution)/shard_map/ppermute | solution.py:826
  86.2 43.1 %collective-permute-start.18 = (bf16[4,640,256]{2,1,0:T(8,128)(2,1)S(1)}, bf16[4,640,256]{2,1,0:T(8,128)(2,1)}, u32[]{:S(2)}, u32[]{:S(2)}) collective-permute-start(bf16[4,640,256]{2,1,0:T(8,128)(2,1)S(1)} %pad_maximum_fusion.refs_14_.refs_22_.refs_17_.refs_25_), channel_id=1, source_target_pairs={{0,1},{1,0},{2,3},{3,2},{4,5},{5,4},{6,7},{7,6},{8,9},{9,8},{10,11... | collective-permute-start | bytes 3932168 | tf_op jit(solution)/shard_map/ppermute | solution.py:826
  87.0 127.4 %all-gather.7.cloned.1.call-start = ((), (), s32[]{:S(2)}) async-start(), calls=%async_computation.15 | async-start | bytes 5242880 | tf_op jit(solution)/shard_map/all_gather | solution.py:913
  87.1 61.9 %collective-permute-start.17 = (bf16[4,640,256]{2,1,0:T(8,128)(2,1)S(1)}, bf16[4,640,256]{2,1,0:T(8,128)(2,1)S(1)}, u32[]{:S(2)}, u32[]{:S(2)}) collective-permute-start(bf16[4,640,256]{2,1,0:T(8,128)(2,1)S(1)} %pad_maximum_fusion.refs_14_.refs_22_.refs_17_.refs_25_), channel_id=1, source_target_pairs={{0,8},{8,0},{1,9},{9,1},{2,10},{10,2},{3,11},{11,3},{4,12},{12,4},... | collective-permute-start | bytes 3932168 | tf_op jit(solution)/shard_map/ppermute | solution.py:826
  115.4 33.7 %collective-permute-start.21 = (bf16[4,640,256]{2,1,0:T(8,128)(2,1)S(1)}, bf16[4,640,256]{2,1,0:T(8,128)(2,1)S(1)}, u32[]{:S(2)}, u32[]{:S(2)}) collective-permute-start(bf16[4,640,256]{2,1,0:T(8,128)(2,1)S(1)} %collective-permute-done.20.refs_16_.refs_24_.refs_19_.refs_27_), channel_id=1, source_target_pairs={{0,8},{8,0},{1,9},{9,1},{2,10},{10,2},{3,11},{11,3},{4,12},{12,4},... | collective-permute-start | bytes 3932168 | tf_op jit(solution)/shard_map/ppermute | solution.py:826
  151.7 24.6 %all-to-all-start.2 = ((bf16[8,1,3,128,128]{4,3,2,1,0:T(8,128)(2,1)}), bf16[8,1,3,128,128]{4,3,2,1,0:T(8,128)(2,1)S(1)}, u32[]{:S(2)}, u32[]{:S(2)}) async-start(bf16[8,1,3,128,128]{4,3,2,1,0:T(8,128)(2,1)} %bitcast.68), calls=%async_computation.2 | async-start | bytes 1572864 | tf_op jit(solution)/shard_map/all_to_all | solution.py:883
  156.4 30.5 %collective-permute-start.24 = (bf16[4,640,256]{2,1,0:T(8,128)(2,1)S(1)}, bf16[4,640,256]{2,1,0:T(8,128)(2,1)S(1)}, u32[]{:S(2)}, u32[]{:S(2)}) collective-permute-start(bf16[4,640,256]{2,1,0:T(8,128)(2,1)S(1)} %copy-done.3), channel_id=1, source_target_pairs={{0,8},{8,0},{1,9},{9,1},{2,10},{10,2},{3,11},{11,3},{4,12},{12,4},... | collective-permute-start | bytes 3932168 | tf_op jit(solution)/shard_map/ppermute | solution.py:826
  180.4 181.5 %reduce-scatter.13.cloned.1.call-start = ((), (), s32[]{:S(2)}) async-start(), calls=%async_computation.16 | async-start | bytes 5242880
  249.5 24.9 %collective-permute-start.26 = (bf16[4,2,384,512]{3,2,1,0:T(8,128)(2,1)}, bf16[4,2,384,512]{3,2,1,0:T(8,128)(2,1)S(1)}, u32[]{:S(2)}, u32[]{:S(2)}) collective-permute-start(bf16[4,2,384,512]{3,2,1,0:T(8,128)(2,1)} %get-tuple-element.123.act), channel_id=1, source_target_pairs={{0,8},{8,0},{1,9},{9,1},{2,10},{10,2},{3,11},{11,3},{4,12},{12,4},... | collective-permute-start | bytes 9437192 | tf_op jit(solution)/shard_map/ppermute | solution.py:826
  249.7 24.7 %collective-permute-start.27 = (bf16[2,384,512]{2,1,0:T(8,128)(2,1)}, bf16[2,384,512]{2,1,0:T(8,128)(2,1)S(1)}, u32[]{:S(2)}, u32[]{:S(2)}) collective-permute-start(bf16[2,384,512]{2,1,0:T(8,128)(2,1)} %get-tuple-element.121.refs_8_), channel_id=1, source_target_pairs={{0,8},{8,0},{1,9},{9,1},{2,10},{10,2},{3,11},{11,3},{4,12},{12,4},... | collective-permute-start | bytes 2359304 | tf_op jit(solution)/shard_map/ppermute | solution.py:826
  285.5 24.9 %all-to-all-start.4 = ((bf16[8,3,128,128]{3,2,1,0:T(8,128)(2,1)}), bf16[8,3,128,128]{3,2,1,0:T(8,128)(2,1)S(1)}, u32[]{:S(2)}, u32[]{:S(2)}) async-start(bf16[8,3,128,128]{3,2,1,0:T(8,128)(2,1)} %get-tuple-element.122), calls=%async_computation.4 | async-start | bytes 1572864 | tf_op jit(solution)/shard_map/all_to_all | solution.py:883
  290.0 60.4 %collective-permute-start.29 = (bf16[4,2,384,512]{3,2,1,0:T(8,128)(2,1)}, bf16[4,2,384,512]{3,2,1,0:T(8,128)(2,1)}, u32[]{:S(2)}, u32[]{:S(2)}) collective-permute-start(bf16[4,2,384,512]{3,2,1,0:T(8,128)(2,1)} %get-tuple-element.134.g_up), channel_id=1, source_target_pairs={{0,8},{8,0},{1,9},{9,1},{2,10},{10,2},{3,11},{11,3},{4,12},{12,4},... | collective-permute-start | bytes 9437192 | tf_op jit(solution)/shard_map/ppermute | solution.py:826
  319.0 24.0 %all-to-all-start.5 = ((bf16[8,1,3,128,128]{4,3,2,1,0:T(8,128)(2,1)}), bf16[8,1,3,128,128]{4,3,2,1,0:T(8,128)(2,1)S(1)}, u32[]{:S(2)}, u32[]{:S(2)}) async-start(bf16[8,1,3,128,128]{4,3,2,1,0:T(8,128)(2,1)} %attend_back.2), calls=%async_computation.5 | async-start | bytes 1572864 | tf_op jit(solution)/shard_map/all_to_all | solution.py:883
  343.0 57.6 %all-to-all-start.6 = ((bf16[8,2,3,128,128]{4,3,2,1,0:T(8,128)(2,1)}), bf16[8,2,3,128,128]{4,3,2,1,0:T(8,128)(2,1)S(1)}, u32[]{:S(2)}, u32[]{:S(2)}) async-start(bf16[8,2,3,128,128]{4,3,2,1,0:T(8,128)(2,1)} %attend_back.3), calls=%async_computation.6 | async-start | bytes 3145728 | tf_op jit(solution)/shard_map/all_to_all | solution.py:883
  346.6 147.7 %reduce-scatter.7.cloned.1.call-start = ((), (), s32[]{:S(2)}) async-start(), calls=%async_computation.11 | async-start | bytes 1310720 | tf_op jit(solution)/shard_map/reduce_scatter | solution.py:949
  359.4 41.2 %collective-permute-start.32 = (bf16[4,320,512]{2,1,0:T(8,128)(2,1)}, bf16[4,320,512]{2,1,0:T(8,128)(2,1)}, u32[]{:S(2)}, u32[]{:S(2)}) collective-permute-start(bf16[4,320,512]{2,1,0:T(8,128)(2,1)} %get-tuple-element.139), channel_id=1, source_target_pairs={{0,1},{1,0},{2,3},{3,2},{4,5},{5,4},{6,7},{7,6},{8,9},{9,8},{10,11... | collective-permute-start | bytes 3932168 | tf_op jit(solution)/shard_map/ppermute | solution.py:826
  361.4 39.2 %collective-permute-start.33 = (bf16[4,320,512]{2,1,0:T(8,128)(2,1)}, bf16[4,320,512]{2,1,0:T(8,128)(2,1)}, u32[]{:S(2)}, u32[]{:S(2)}) collective-permute-start(bf16[4,320,512]{2,1,0:T(8,128)(2,1)} %get-tuple-element.140), channel_id=1, source_target_pairs={{0,16},{16,0},{1,17},{17,1},{2,18},{18,2},{3,19},{19,3},{4,20},{20... | collective-permute-start | bytes 3932168 | tf_op jit(solution)/shard_map/ppermute | solution.py:826
  361.9 38.7 %collective-permute-start.28 = (bf16[4,2,1,3,128,128]{5,4,3,2,1,0:T(8,128)(2,1)S(1)}, bf16[4,2,1,3,128,128]{5,4,3,2,1,0:T(8,128)(2,1)S(1)}, u32[]{:S(2)}, u32[]{:S(2)}) collective-permute-start(bf16[4,2,1,3,128,128]{5,4,3,2,1,0:T(8,128)(2,1)S(1)} %bitcast.56), channel_id=1, source_target_pairs={{0,8},{8,0},{1,9},{9,1},{2,10},{10,2},{3,11},{11,3},{4,12},{12,4},... | collective-permute-start | bytes 2359304 | tf_op jit(solution)/shard_map/ppermute | solution.py:826
  362.0 137.4 %reduce-scatter.11.cloned.1.call-start = ((), (), s32[]{:S(2)}) async-start(), calls=%async_computation.13 | async-start | bytes 1638400 | tf_op jit(solution)/shard_map/reduce_scatter | solution.py:964
  401.5 32.4 %collective-permute-start.42 = (bf16[4,320,512]{2,1,0:T(8,128)(2,1)}, bf16[4,320,512]{2,1,0:T(8,128)(2,1)}, u32[]{:S(2)}, u32[]{:S(2)}) collective-permute-start(bf16[4,320,512]{2,1,0:T(8,128)(2,1)} %get-tuple-element.141), channel_id=1, source_target_pairs={{0,17},{1,16},{16,1},{17,0},{2,19},{3,18},{18,3},{19,2},{4,21},{5,... | collective-permute-start | bytes 3932168 | tf_op jit(solution)/shard_map/ppermute | solution.py:805
  439.1 64.5 %reduce-scatter.9.cloned.1.call-start = ((), (), s32[]{:S(2)}) async-start(), calls=%async_computation.12 | async-start | bytes 983040 | tf_op jit(solution)/shard_map/reduce_scatter | solution.py:970
  (80 other events, 755.7 us)
Sparse Core Ops, SparseCore 0:
  87.2 47.9 all-gather.4
  151.8 62.5 all-gather.6
  285.6 61.7 reduce-scatter.12
  362.1 37.8 reduce-scatter.6
  439.2 29.2 reduce-scatter.10
  481.4 22.1 reduce-scatter.8

commit v6 on v5

--- a/solution.py
+++ b/solution.py
@@ -506,12 +506,12 @@
                 acc = term if acc is None else acc + term
             total[:, q * part:(q + 1) * part] = acc
         xhat, scale = row_stats(total[...])
-        xhat1[...] = xhat
+        xhat1[...] = xhat.astype(xhat1.dtype)
         scale1[...] = jnp.broadcast_to(scale, scale1.shape)
         value = load_columns(x, pos, part).astype(F32) + xhat * gains[1:2] + shifts[1:2]
         hidden[...] = value
         xhat, scale = row_stats(value)
-        xhat2[...] = xhat
+        xhat2[...] = xhat.astype(xhat2.dtype)
         scale2[...] = jnp.broadcast_to(scale, scale2.shape)
         value = (xhat * gains[2:3] + shifts[2:3]).astype(BF16)
         normed[...] = value
@@ -567,7 +567,7 @@
     side = (2, tokens, width // 2)
     ffn = jax.ShapeDtypeStruct((nz, 2, tokens, units), BF16)
     low = jax.ShapeDtypeStruct(flat, BF16)
-    return pl.pallas_call(layer_kernel, grid_spec=pltpu.PrefetchScalarGridSpec(num_scalar_prefetch=1, grid=(nz,), in_specs=[whole(a.shape) for a in (*att, x, cot, gains, shifts)] + layer_specs(units, part, rows, nz, lambda i: i), out_specs=[whole(flat)] * 2 + [act] * 2 + [whole(side)] * 2 + [whole(flat), whole(column)] * 2 + [whole((8, width))], scratch_shapes=[pltpu.VMEM(flat, BF16), pltpu.VMEM(flat, F32), pltpu.VMEM(flat, F32)]), out_shape=[low, low, ffn, ffn] + [jax.ShapeDtypeStruct(side, BF16)] * 2 + [jax.ShapeDtypeStruct(flat, F32), jax.ShapeDtypeStruct(column, F32)] * 2 + [jax.ShapeDtypeStruct((8, width), F32)], compiler_params=params(), cost_estimate=cost(2 * tokens * width * (2 * nz * 2 * units + width), 40000000.0, tokens * nz * 2 * units), name='layer')(pos, *att, x, cot, gains, shifts, *layer_weights(ups, mixes))
+    return pl.pallas_call(layer_kernel, grid_spec=pltpu.PrefetchScalarGridSpec(num_scalar_prefetch=1, grid=(nz,), in_specs=[whole(a.shape) for a in (*att, x, cot, gains, shifts)] + layer_specs(units, part, rows, nz, lambda i: i), out_specs=[whole(flat)] * 2 + [act] * 2 + [whole(side)] * 2 + [whole(flat), whole(column)] * 2 + [whole((8, width))], scratch_shapes=[pltpu.VMEM(flat, BF16), pltpu.VMEM(flat, F32), pltpu.VMEM(flat, F32)]), out_shape=[low, low, ffn, ffn] + [jax.ShapeDtypeStruct(side, BF16)] * 2 + [jax.ShapeDtypeStruct(flat, BF16), jax.ShapeDtypeStruct(column, F32)] * 2 + [jax.ShapeDtypeStruct((8, width), F32)], compiler_params=params(), cost_estimate=cost(2 * tokens * width * (2 * nz * 2 * units + width), 40000000.0, tokens * nz * 2 * units), name='layer')(pos, *att, x, cot, gains, shifts, *layer_weights(ups, mixes))
 
 def layer_back_kernel(pos, *refs):
     cot, gains, xhat1, scale1, xhat2, scale2, slope, keep, send = refs[0:9]
@@ -593,12 +593,12 @@
     @pl.when(step == nz - 1)
     def _():
         grad = total[...]
-        xhat = xhat2[...]
+        xhat = xhat2[...].astype(F32)
         sums[1:2] = column_sum(grad * xhat)
         sums[3:4] = column_sum(grad)
         grad = load_columns(cot, pos, part).astype(F32) + row_pull(grad, xhat, scale2[:, 0:1], gains[2:3])
         g_hidden[...] = grad
-        xhat = xhat1[...]
+        xhat = xhat1[...].astype(F32)
         sums[0:1] = column_sum(grad * xhat)
         sums[2:3] = column_sum(grad)
         g_b1 = row_pull(grad, xhat, scale1[:, 0:1], gains[1:2]).astype(BF16)

time: 521 us -> 520 us (level)
  no operation moved by 1% of the time
where the time goes in v6:
time: 520 us; the launch traced here: 512 us
  waiting for transfers between devices  240 us (46%)
  Pallas kernels  149 us (29%)
  starting transfers between devices  62.7 us (12%)
  local copies, waits for them, and re-layouts  18.1 us (3%)
  between operations  15.1 us (3%)
  other arithmetic  13.6 us (3%)
  blocking collectives  12.7 us (2%)
    ppermute x40, waiting for transfers between devices, swap(): return lax.ppermute(values, axis, SWAP)  96.9 us
    all_to_all x6, waiting for transfers between devices, exchange(): return lax.all_to_all(values, SEQ, 0, 0, tiled=True)  84.3 us
    pallas_call x1, Pallas kernels, call_layer(): pl.pallas_call(layer_kernel, grid_spec=pltpu.PrefetchScalarGridSpec(num_s...  27.1 us
    ppermute x6, waiting for transfers between devices, ring(): lax.ppermute(values, 'z', [(i, (i + step) % size) for i in range(size)])  26.3 us
    ppermute x40, starting transfers between devices, swap(): return lax.ppermute(values, axis, SWAP)  25.7 us
    all_to_all x6, starting transfers between devices, exchange(): return lax.all_to_all(values, SEQ, 0, 0, tiled=True)  25.1 us
    pallas_call x1, Pallas kernels, call_layer_back(): pl.pallas_call(layer_back_kernel, grid_spec=pltpu.PrefetchScalarGridSpec(...  23.9 us
    pallas_call x2, Pallas kernels, call_attend_back(): pl.pallas_call(functools.partial(attend_back_kernel, first), grid_spec=pl...  19.8 us
  transfers between devices with their start and end apart: 61, of which 33 were waited for; matrix products, arithmetic and copies ran while one was open for 3% of the time, Pallas kernels for 22%

profile of v6, /device:TPU:0, one launch (start us, length us, event | category | flops | bytes accessed | tf_op | source)
XLA Modules:
  0.0 511.6 jit_solution(14185718458216311189)
XLA Ops:
  38.7 8.6 %collective-permute-done.9 = bf16[640,256]{1,0:T(8,128)(2,1)S(1)} collective-permute-done((bf16[640,256]{1,0:T(8,128)(2,1)S(1)}, bf16[640,256]{1,0:T(8,128)(2,1)S(1)}, u32[]{:S(2)}, u32[]{:S(2)}) %collective-permute-start.9) | collective-permute-done | bytes 327712 | tf_op jit(solution)/shard_map/ppermute | solution.py:829
  55.5 8.0 %collective-permute-done.11 = bf16[2,3,256,128]{3,2,1,0:T(8,128)(2,1)S(1)} collective-permute-done((bf16[2,3,256,128]{3,2,1,0:T(8,128)(2,1)S(1)}, bf16[2,3,256,128]{3,2,1,0:T(8,128)(2,1)S(1)}, u32[]{:S(2)}, u32[]{:S(2)}) %collective-permute-start.11) | collective-permute-done | bytes 393248 | tf_op jit(solution)/shard_map/ppermute | solution.py:826
  67.7 9.3 %project.1 = (bf16[4,2,2,3,128,128]{5,4,3,2,1,0:T(8,128)(2,1)}, bf16[4,2,1,3,128,128]{5,4,3,2,1,0:T(8,128)(2,1)}, bf16[384,512]{1,0:T(8,128)(2,1)}, bf16[384,512]{1,0:T(8,128)(2,1)}) custom-call(s32[4]{0:T(128)} %pad_add_fusion.pos, s32[12]{0:T(128)} %reshape.82.starts, bf16[384,1024]{1,0:T(8,128)(2,1)} %bitcast.59, ...), custom_call_target="tpu_custom_call" | custom-call | flops 483183808 | bytes 2400000 | tf_op jit(solution)/shard_map/project/pallas_call | solution.py:369
  87.1 28.2 %collective-permute-done.20.refs_16_.refs_24_.refs_19_.refs_27_ = bf16[4,640,256]{2,1,0:T(8,128)(2,1)S(1)} collective-permute-done((bf16[4,640,256]{2,1,0:T(8,128)(2,1)S(1)}, bf16[4,640,256]{2,1,0:T(8,128)(2,1)S(1)}, u32[]{:S(2)}, u32[]{:S(2)}) %collective-permute-start.20) | collective-permute-done | bytes 1310752 | tf_op jit(solution)/shard_map/ppermute | solution.py:826
  115.4 13.9 %collective-permute-done.18.refs_15_.refs_23_.refs_18_.refs_26_ = bf16[4,640,256]{2,1,0:T(8,128)(2,1)} collective-permute-done((bf16[4,640,256]{2,1,0:T(8,128)(2,1)S(1)}, bf16[4,640,256]{2,1,0:T(8,128)(2,1)}, u32[]{:S(2)}, u32[]{:S(2)}) %collective-permute-start.18) | collective-permute-done | bytes 1310752 | tf_op jit(solution)/shard_map/ppermute | solution.py:826
  132.1 15.5 %collective-permute-done.22 = bf16[2,640,256]{2,1,0:T(8,128)(2,1)S(1)} collective-permute-done((bf16[2,640,256]{2,1,0:T(8,128)(2,1)S(1)}, bf16[2,640,256]{2,1,0:T(8,128)(2,1)S(1)}, u32[]{:S(2)}, u32[]{:S(2)}) %collective-permute-start.22) | collective-permute-done | bytes 655392 | tf_op jit(solution)/shard_map/ppermute | solution.py:826
  156.4 10.0 %attend.2 = (bf16[8,2,128,128]{3,2,1,0:T(8,128)(2,1)}, f32[2,8,1024]{2,1,0:T(8,128)}) custom-call(s32[12]{0:T(128)} %reshape.82.starts, bf16[8,2,3,128,128]{4,3,2,1,0:T(8,128)(2,1)} %all-to-all-done.got), custom_call_target="tpu_custom_call" | custom-call | flops 429496736 | bytes 800000 | tf_op jit(solution)/shard_map/attend/pallas_call | solution.py:408
  166.4 9.7 %all-to-all-done.2.got = bf16[8,1,3,128,128]{4,3,2,1,0:T(8,128)(2,1)S(1)} async-done(((bf16[8,1,3,128,128]{4,3,2,1,0:T(8,128)(2,1)}), bf16[8,1,3,128,128]{4,3,2,1,0:T(8,128)(2,1)S(1)}, u32[]{:S(2)}, u32[]{:S(2)}) %all-to-all-start.2) | async-done | bytes 786464 | tf_op jit(solution)/shard_map/all_to_all | solution.py:883
  186.8 7.8 %all-to-all-done.1.refs_0_ = bf16[8,2,128,128]{3,2,1,0:T(8,128)(2,1)} async-done(((bf16[8,2,128,128]{3,2,1,0:T(8,128)(2,1)}), bf16[8,2,128,128]{3,2,1,0:T(8,128)(2,1)}, u32[]{:S(2)}, u32[]{:S(2)}) %all-to-all-start.1) | async-done | bytes 524320 | tf_op jit(solution)/shard_map/all_to_all | solution.py:883
  194.5 12.7 %all_to_all.35.refs_1_ = bf16[8,1,128,128]{3,2,1,0:T(8,128)(2,1)} all-to-all(bf16[8,1,128,128]{3,2,1,0:T(8,128)(2,1)} %get-tuple-element.110.att), channel_id=1, replica_groups=mesh['y'=2,'c'=2,'z'=4,'x'=2] {'z','x'}, dimensions={0} | all-to-all | bytes 524288 | tf_op jit(solution)/shard_map/all_to_all | solution.py:883
  214.4 7.4 %collective-permute-done.25.refs_10_.refs_11_.refs_12_.refs_13_.refs_14_.refs_15_.refs_16_ = bf16[4,4,256,512]{3,2,1,0:T(8,128)(2,1)} collective-permute-done((bf16[4,4,256,512]{3,2,1,0:T(8,128)(2,1)}, bf16[4,4,256,512]{3,2,1,0:T(8,128)(2,1)}, u32[]{:S(2)}, u32[]{:S(2)}) %collective-permute-start.25) | collective-permute-done | bytes 4194336 | tf_op jit(solution)/shard_map/ppermute | solution.py:826
  221.9 27.1 %layer.1 = (bf16[384,1024]{1,0:T(8,128)(2,1)}, bf16[384,1024]{1,0:T(8,128)(2,1)}, bf16[4,2,384,512]{3,2,1,0:T(8,128)(2,1)}, bf16[4,2,384,512]{3,2,1,0:T(8,128)(2...) custom-call(s32[4]{0:T(128)} %pad_add_fusion.pos, ...), custom_call_target="tpu_custom_call" | custom-call | flops 1449551488 | bytes 8000000 | tf_op jit(solution)/shard_map/layer/pallas_call | solution.py:570
  249.6 23.9 %layer_back.1 = (bf16[4,2,384,512]{3,2,1,0:T(8,128)(2,1)}, bf16[384,512]{1,0:T(8,128)(2,1)}, bf16[384,512]{1,0:T(8,128)(2,1)}, f32[384,1024]{1,0:T(8,128)}, bf16...) custom-call(s32[4]{0:T(128)} %pad_add_fusion.pos, bf16[384,1024]{1,0:T(8,128)(2,1)} %bitcast.63, ...), custom_call_target="tpu_custom_call" | custom-call | flops 1449551488 | bytes 8000000 | tf_op jit(solution)/shard_map/layer_back/pallas_call | solution.py:626
  276.1 8.4 %down_grad.1 = bf16[4,4,512,256]{3,2,1,0:T(8,128)(2,1)} custom-call(s32[4]{0:T(128)} %pad_add_fusion.pos, bf16[4,2,384,512]{3,2,1,0:T(8,128)(2,1)} %get-tuple-element.123.act, bf16[4,2,384,512]{3,2,1,0:T(8,128)(2,1)} %copy-done.16, bf16[2,384,512]{2,1,0:T(8,128)(2,1)} %get-tuple-element.120.refs_7_.keep, bf16[2,384,512]{2,1,0:T(8,128)(2,1)} %copy-done.14), custom_call_target="tpu_custom_call" | custom-call | flops 644245120 | bytes 3200000 | tf_op jit(solution)/shard_map/down_grad/pallas_call | solution.py:673
  289.2 20.3 %all-to-all-done.4.grad = bf16[8,3,128,128]{3,2,1,0:T(8,128)(2,1)S(1)} async-done(((bf16[8,3,128,128]{3,2,1,0:T(8,128)(2,1)}), bf16[8,3,128,128]{3,2,1,0:T(8,128)(2,1)S(1)}, u32[]{:S(2)}, u32[]{:S(2)}) %all-to-all-start.4) | async-done | bytes 786464 | tf_op jit(solution)/shard_map/all_to_all | solution.py:883
  310.4 7.6 %attend_back.2 = bf16[8,1,3,128,128]{4,3,2,1,0:T(8,128)(2,1)} custom-call(s32[12]{0:T(128)} %reshape.82.starts, f32[1024,128]{1,0:T(8,128)} %constant.54.clone.tcos, f32[1024,128]{1,0:T(8,128)} %constant.55.clone.tsin, f32[3,4,128]{2,1,0:T(4,128)} %get-tuple-element.211.start_cos, f32[3,4,128]{2,1,0:T(4,128)} %get-tuple-element.210.start_sin, ...), custom_call_target="tpu_custom_call" | custom-call | flops 536870912 | bytes 800000 | tf_op jit(solution)/shard_map/attend_back/pallas_call | solution.py:462
  321.7 12.2 %attend_back.3 = bf16[8,2,3,128,128]{4,3,2,1,0:T(8,128)(2,1)} custom-call(s32[12]{0:T(128)} %reshape.82.starts, f32[1024,128]{1,0:T(8,128)} %constant.54.clone.tcos, f32[1024,128]{1,0:T(8,128)} %constant.55.clone.tsin, f32[3,4,128]{2,1,0:T(4,128)} %get-tuple-element.211.start_cos, f32[3,4,128]{2,1,0:T(4,128)} %get-tuple-element.210.start_sin, ...), custom_call_target="tpu_custom_call" | custom-call | flops 1073741824 | bytes 1600000 | tf_op jit(solution)/shard_map/attend_back/pallas_call | solution.py:462
  333.9 8.2 %all-to-all-done.5 = bf16[8,1,3,128,128]{4,3,2,1,0:T(8,128)(2,1)S(1)} async-done(((bf16[8,1,3,128,128]{4,3,2,1,0:T(8,128)(2,1)}), bf16[8,1,3,128,128]{4,3,2,1,0:T(8,128)(2,1)S(1)}, u32[]{:S(2)}, u32[]{:S(2)}) %all-to-all-start.5) | async-done | bytes 786464 | tf_op jit(solution)/shard_map/all_to_all | solution.py:883
  349.6 8.9 %up_grad.1 = (bf16[4,320,512]{2,1,0:T(8,128)(2,1)}, bf16[4,320,512]{2,1,0:T(8,128)(2,1)}, bf16[4,320,512]{2,1,0:T(8,128)(2,1)}, bf16[4,320,512]{2,1,0:T(8,128)(2,1)}) custom-call(bf16[4,2,384,512]{3,2,1,0:T(8,128)(2,1)} %get-tuple-element.134.g_up, bf16[4,2,384,512]{3,2,1,0:T(8,128)(2,1)} %collective-permute-done.29.g_up2, ...), custom_call_target="tpu_custom_call" | custom-call | flops 644245120 | bytes 3200000 | tf_op jit(solution)/shard_map/up_grad/pallas_call | solution.py:704
  361.3 38.3 %all-to-all-done.6 = bf16[8,2,3,128,128]{4,3,2,1,0:T(8,128)(2,1)S(1)} async-done(((bf16[8,2,3,128,128]{4,3,2,1,0:T(8,128)(2,1)}), bf16[8,2,3,128,128]{4,3,2,1,0:T(8,128)(2,1)S(1)}, u32[]{:S(2)}, u32[]{:S(2)}) %all-to-all-start.6) | async-done | bytes 1572896 | tf_op jit(solution)/shard_map/all_to_all | solution.py:883
  405.8 9.0 %qkv_grad.1 = (bf16[4,3,256,128]{3,2,1,0:T(8,128)(2,1)}, bf16[2,3,256,128]{3,2,1,0:T(8,128)(2,1)}, bf16[2,3,256,128]{3,2,1,0:T(8,128)(2,1)}, bf16[2,3,256,128]{3...) custom-call(s32[4]{0:T(128)} %pad_add_fusion.pos, ...), custom_call_target="tpu_custom_call" | custom-call | flops 483183808 | bytes 2400000 | tf_op jit(solution)/shard_map/qkv_grad/pallas_call | solution.py:739
  414.8 18.2 %collective-permute-done.42.refs_1_ = bf16[4,320,512]{2,1,0:T(8,128)(2,1)} collective-permute-done((bf16[4,320,512]{2,1,0:T(8,128)(2,1)}, bf16[4,320,512]{2,1,0:T(8,128)(2,1)}, u32[]{:S(2)}, u32[]{:S(2)}) %collective-permute-start.42) | collective-permute-done | bytes 1310752 | tf_op jit(solution)/shard_map/ppermute | solution.py:805
  440.9 8.9 %collective-permute-done.36.b = bf16[2,3,256,128]{3,2,1,0:T(8,128)(2,1)S(1)} collective-permute-done((bf16[2,3,256,128]{3,2,1,0:T(8,128)(2,1)S(1)}, bf16[2,3,256,128]{3,2,1,0:T(8,128)(2,1)S(1)}, u32[]{:S(2)}, u32[]{:S(2)}) %collective-permute-start.36) | collective-permute-done | bytes 393248 | tf_op jit(solution)/shard_map/ppermute | solution.py:826
  458.6 14.4 %input_grad.1 = (f32[384,1024]{1,0:T(8,128)}, f32[8,1024]{1,0:T(8,128)}) custom-call(s32[4]{0:T(128)} %pad_add_fusion.pos, bf16[4,2,2,3,128,128]{5,4,3,2,1,0:T(8,128)(2,1)} %bitcast.55, bf16[4,2,1,3,128,128]{5,4,3,2,1,0:T(8,128)(2,1)} %bitcast.58, bf16[384,1024]{1,0:T(8,128)(2,1)} %bitcast.61, f32[4,1024]{1,0:T(4,128)} %get-tuple-element.207.gains.refs_4_.refs_1_.refs_3_, ...), custom_call_target="tpu_custom_call" | custom-call | flops 483183808 | bytes 3200000 | tf_op jit(solution)/shard_map/input_grad/pallas_call | solution.py:775
  (241 shorter events, 159.9 us)
Async XLA Ops:
  38.7 26.2 %collective-permute-start.12 = (bf16[4,3,256,128]{3,2,1,0:T(8,128)(2,1)S(1)}, bf16[4,3,256,128]{3,2,1,0:T(8,128)(2,1)S(1)}, u32[]{:S(2)}, u32[]{:S(2)}) collective-permute-start(bf16[4,3,256,128]{3,2,1,0:T(8,128)(2,1)S(1)} %pad_maximum_fusion.1.refs_0_.refs_5_), channel_id=1, source_target_pairs={{0,8},{8,0},{1,9},{9,1},{2,10},{10,2},{3,11},{11,3},{4,12},{12,4},... | collective-permute-start | bytes 2359304 | tf_op jit(solution)/shard_map/ppermute | solution.py:826
  77.0 74.5 %all-to-all-start = ((bf16[8,2,3,128,128]{4,3,2,1,0:T(8,128)(2,1)}), bf16[8,2,3,128,128]{4,3,2,1,0:T(8,128)(2,1)}, u32[]{:S(2)}, u32[]{:S(2)}) async-start(bf16[8,2,3,128,128]{4,3,2,1,0:T(8,128)(2,1)} %bitcast.64), calls=%async_computation | async-start | bytes 3145728 | tf_op jit(solution)/shard_map/all_to_all | solution.py:883
  81.5 70.1 %all-gather.5.cloned.1.call-start = ((), (), s32[]{:S(2)}) async-start(), calls=%async_computation.14 | async-start | bytes 1310720 | tf_op jit(solution)/shard_map/all_gather | solution.py:899
  84.6 30.8 %collective-permute-start.20 = (bf16[4,640,256]{2,1,0:T(8,128)(2,1)S(1)}, bf16[4,640,256]{2,1,0:T(8,128)(2,1)S(1)}, u32[]{:S(2)}, u32[]{:S(2)}) collective-permute-start(bf16[4,640,256]{2,1,0:T(8,128)(2,1)S(1)} %pad_maximum_fusion.refs_14_.refs_22_.refs_17_.refs_25_), channel_id=1, source_target_pairs={{0,16},{16,0},{1,17},{17,1},{2,18},{18,2},{3,19},{19,3},{4,20},{20... | collective-permute-start | bytes 3932168 | tf_op jit(solution)/shard_map/ppermute | solution.py:826
  86.1 43.1 %collective-permute-start.18 = (bf16[4,640,256]{2,1,0:T(8,128)(2,1)S(1)}, bf16[4,640,256]{2,1,0:T(8,128)(2,1)}, u32[]{:S(2)}, u32[]{:S(2)}) collective-permute-start(bf16[4,640,256]{2,1,0:T(8,128)(2,1)S(1)} %pad_maximum_fusion.refs_14_.refs_22_.refs_17_.refs_25_), channel_id=1, source_target_pairs={{0,1},{1,0},{2,3},{3,2},{4,5},{5,4},{6,7},{7,6},{8,9},{9,8},{10,11... | collective-permute-start | bytes 3932168 | tf_op jit(solution)/shard_map/ppermute | solution.py:826
  87.0 127.3 %all-gather.7.cloned.1.call-start = ((), (), s32[]{:S(2)}) async-start(), calls=%async_computation.15 | async-start | bytes 5242880 | tf_op jit(solution)/shard_map/all_gather | solution.py:913
  87.1 62.0 %collective-permute-start.17 = (bf16[4,640,256]{2,1,0:T(8,128)(2,1)S(1)}, bf16[4,640,256]{2,1,0:T(8,128)(2,1)S(1)}, u32[]{:S(2)}, u32[]{:S(2)}) collective-permute-start(bf16[4,640,256]{2,1,0:T(8,128)(2,1)S(1)} %pad_maximum_fusion.refs_14_.refs_22_.refs_17_.refs_25_), channel_id=1, source_target_pairs={{0,8},{8,0},{1,9},{9,1},{2,10},{10,2},{3,11},{11,3},{4,12},{12,4},... | collective-permute-start | bytes 3932168 | tf_op jit(solution)/shard_map/ppermute | solution.py:826
  115.4 33.7 %collective-permute-start.21 = (bf16[4,640,256]{2,1,0:T(8,128)(2,1)S(1)}, bf16[4,640,256]{2,1,0:T(8,128)(2,1)S(1)}, u32[]{:S(2)}, u32[]{:S(2)}) collective-permute-start(bf16[4,640,256]{2,1,0:T(8,128)(2,1)S(1)} %collective-permute-done.20.refs_16_.refs_24_.refs_19_.refs_27_), channel_id=1, source_target_pairs={{0,8},{8,0},{1,9},{9,1},{2,10},{10,2},{3,11},{11,3},{4,12},{12,4},... | collective-permute-start | bytes 3932168 | tf_op jit(solution)/shard_map/ppermute | solution.py:826
  151.6 24.6 %all-to-all-start.2 = ((bf16[8,1,3,128,128]{4,3,2,1,0:T(8,128)(2,1)}), bf16[8,1,3,128,128]{4,3,2,1,0:T(8,128)(2,1)S(1)}, u32[]{:S(2)}, u32[]{:S(2)}) async-start(bf16[8,1,3,128,128]{4,3,2,1,0:T(8,128)(2,1)} %bitcast.68), calls=%async_computation.2 | async-start | bytes 1572864 | tf_op jit(solution)/shard_map/all_to_all | solution.py:883
  156.3 30.5 %collective-permute-start.24 = (bf16[4,640,256]{2,1,0:T(8,128)(2,1)S(1)}, bf16[4,640,256]{2,1,0:T(8,128)(2,1)S(1)}, u32[]{:S(2)}, u32[]{:S(2)}) collective-permute-start(bf16[4,640,256]{2,1,0:T(8,128)(2,1)S(1)} %copy-done.3), channel_id=1, source_target_pairs={{0,8},{8,0},{1,9},{9,1},{2,10},{10,2},{3,11},{11,3},{4,12},{12,4},... | collective-permute-start | bytes 3932168 | tf_op jit(solution)/shard_map/ppermute | solution.py:826
  180.3 180.7 %reduce-scatter.13.cloned.1.call-start = ((), (), s32[]{:S(2)}) async-start(), calls=%async_computation.16 | async-start | bytes 5242880
  249.0 24.5 %collective-permute-start.26 = (bf16[4,2,384,512]{3,2,1,0:T(8,128)(2,1)}, bf16[4,2,384,512]{3,2,1,0:T(8,128)(2,1)S(1)}, u32[]{:S(2)}, u32[]{:S(2)}) collective-permute-start(bf16[4,2,384,512]{3,2,1,0:T(8,128)(2,1)} %get-tuple-element.123.act), channel_id=1, source_target_pairs={{0,8},{8,0},{1,9},{9,1},{2,10},{10,2},{3,11},{11,3},{4,12},{12,4},... | collective-permute-start | bytes 9437192 | tf_op jit(solution)/shard_map/ppermute | solution.py:826
  249.2 24.3 %collective-permute-start.27 = (bf16[2,384,512]{2,1,0:T(8,128)(2,1)}, bf16[2,384,512]{2,1,0:T(8,128)(2,1)S(1)}, u32[]{:S(2)}, u32[]{:S(2)}) collective-permute-start(bf16[2,384,512]{2,1,0:T(8,128)(2,1)} %get-tuple-element.121.refs_8_), channel_id=1, source_target_pairs={{0,8},{8,0},{1,9},{9,1},{2,10},{10,2},{3,11},{11,3},{4,12},{12,4},... | collective-permute-start | bytes 2359304 | tf_op jit(solution)/shard_map/ppermute | solution.py:826
  284.5 24.9 %all-to-all-start.4 = ((bf16[8,3,128,128]{3,2,1,0:T(8,128)(2,1)}), bf16[8,3,128,128]{3,2,1,0:T(8,128)(2,1)S(1)}, u32[]{:S(2)}, u32[]{:S(2)}) async-start(bf16[8,3,128,128]{3,2,1,0:T(8,128)(2,1)} %get-tuple-element.122), calls=%async_computation.4 | async-start | bytes 1572864 | tf_op jit(solution)/shard_map/all_to_all | solution.py:883
  289.1 60.4 %collective-permute-start.29 = (bf16[4,2,384,512]{3,2,1,0:T(8,128)(2,1)}, bf16[4,2,384,512]{3,2,1,0:T(8,128)(2,1)}, u32[]{:S(2)}, u32[]{:S(2)}) collective-permute-start(bf16[4,2,384,512]{3,2,1,0:T(8,128)(2,1)} %get-tuple-element.134.g_up), channel_id=1, source_target_pairs={{0,8},{8,0},{1,9},{9,1},{2,10},{10,2},{3,11},{11,3},{4,12},{12,4},... | collective-permute-start | bytes 9437192 | tf_op jit(solution)/shard_map/ppermute | solution.py:826
  318.0 24.0 %all-to-all-start.5 = ((bf16[8,1,3,128,128]{4,3,2,1,0:T(8,128)(2,1)}), bf16[8,1,3,128,128]{4,3,2,1,0:T(8,128)(2,1)S(1)}, u32[]{:S(2)}, u32[]{:S(2)}) async-start(bf16[8,1,3,128,128]{4,3,2,1,0:T(8,128)(2,1)} %attend_back.2), calls=%async_computation.5 | async-start | bytes 1572864 | tf_op jit(solution)/shard_map/all_to_all | solution.py:883
  342.1 57.6 %all-to-all-start.6 = ((bf16[8,2,3,128,128]{4,3,2,1,0:T(8,128)(2,1)}), bf16[8,2,3,128,128]{4,3,2,1,0:T(8,128)(2,1)S(1)}, u32[]{:S(2)}, u32[]{:S(2)}) async-start(bf16[8,2,3,128,128]{4,3,2,1,0:T(8,128)(2,1)} %attend_back.3), calls=%async_computation.6 | async-start | bytes 3145728 | tf_op jit(solution)/shard_map/all_to_all | solution.py:883
  345.6 147.7 %reduce-scatter.7.cloned.1.call-start = ((), (), s32[]{:S(2)}) async-start(), calls=%async_computation.11 | async-start | bytes 1310720 | tf_op jit(solution)/shard_map/reduce_scatter | solution.py:949
  358.5 41.2 %collective-permute-start.32 = (bf16[4,320,512]{2,1,0:T(8,128)(2,1)}, bf16[4,320,512]{2,1,0:T(8,128)(2,1)}, u32[]{:S(2)}, u32[]{:S(2)}) collective-permute-start(bf16[4,320,512]{2,1,0:T(8,128)(2,1)} %get-tuple-element.139), channel_id=1, source_target_pairs={{0,1},{1,0},{2,3},{3,2},{4,5},{5,4},{6,7},{7,6},{8,9},{9,8},{10,11... | collective-permute-start | bytes 3932168 | tf_op jit(solution)/shard_map/ppermute | solution.py:826
  360.5 39.2 %collective-permute-start.33 = (bf16[4,320,512]{2,1,0:T(8,128)(2,1)}, bf16[4,320,512]{2,1,0:T(8,128)(2,1)}, u32[]{:S(2)}, u32[]{:S(2)}) collective-permute-start(bf16[4,320,512]{2,1,0:T(8,128)(2,1)} %get-tuple-element.140), channel_id=1, source_target_pairs={{0,16},{16,0},{1,17},{17,1},{2,18},{18,2},{3,19},{19,3},{4,20},{20... | collective-permute-start | bytes 3932168 | tf_op jit(solution)/shard_map/ppermute | solution.py:826
  361.0 38.6 %collective-permute-start.28 = (bf16[4,2,1,3,128,128]{5,4,3,2,1,0:T(8,128)(2,1)S(1)}, bf16[4,2,1,3,128,128]{5,4,3,2,1,0:T(8,128)(2,1)S(1)}, u32[]{:S(2)}, u32[]{:S(2)}) collective-permute-start(bf16[4,2,1,3,128,128]{5,4,3,2,1,0:T(8,128)(2,1)S(1)} %bitcast.56), channel_id=1, source_target_pairs={{0,8},{8,0},{1,9},{9,1},{2,10},{10,2},{3,11},{11,3},{4,12},{12,4},... | collective-permute-start | bytes 2359304 | tf_op jit(solution)/shard_map/ppermute | solution.py:826
  361.0 137.1 %reduce-scatter.11.cloned.1.call-start = ((), (), s32[]{:S(2)}) async-start(), calls=%async_computation.13 | async-start | bytes 1638400 | tf_op jit(solution)/shard_map/reduce_scatter | solution.py:964
  400.6 32.4 %collective-permute-start.42 = (bf16[4,320,512]{2,1,0:T(8,128)(2,1)}, bf16[4,320,512]{2,1,0:T(8,128)(2,1)}, u32[]{:S(2)}, u32[]{:S(2)}) collective-permute-start(bf16[4,320,512]{2,1,0:T(8,128)(2,1)} %get-tuple-element.141), channel_id=1, source_target_pairs={{0,17},{1,16},{16,1},{17,0},{2,19},{3,18},{18,3},{19,2},{4,21},{5,... | collective-permute-start | bytes 3932168 | tf_op jit(solution)/shard_map/ppermute | solution.py:805
  438.2 64.5 %reduce-scatter.9.cloned.1.call-start = ((), (), s32[]{:S(2)}) async-start(), calls=%async_computation.12 | async-start | bytes 983040 | tf_op jit(solution)/shard_map/reduce_scatter | solution.py:970
  (80 other events, 755.2 us)
Sparse Core Ops, SparseCore 0:
  87.1 47.9 all-gather.4
  151.7 62.6 all-gather.6
  284.7 61.7 reduce-scatter.12
  361.2 37.7 reduce-scatter.6
  438.3 29.2 reduce-scatter.10
  480.4 22.1 reduce-scatter.8
